TPU v7x, 512 devices: a whole 4x8x8 slice. The times are simulated.
512 devices in a mesh: dp: 32 (over y, x_hi, core), seq: 16 (over x_lo, z).
Axes of the slice: x: 4 (x_hi: 2, x_lo: 2; x = x_hi * 2 + x_lo), y: 8, z: 8, core: 2. Of those that a mesh axis runs over, the one named last changes fastest.
Arguments:
- queries: bfloat16 [32, 2048, 1152], P('dp', 'seq'), may hold values from -7 to 7
- keys: bfloat16 [32, 2048, 1152], P('dp', 'seq'), may hold values from -7 to 7
- values_in: bfloat16 [32, 2048, 1152], P('dp', 'seq'), may hold values from -6 to 6
- inputs_x: bfloat16 [32, 2048, 1152], P('dp', 'seq'), may hold values from -6 to 6
- out_grad: bfloat16 [32, 2048, 1152], P('dp', 'seq'), may hold values from -6 to 6
- shift: float32 [32, 1152], P('dp'), may hold values from -3 to 3
- scale: float32 [32, 1152], P('dp'), may hold values from -2.5 to 2.5
- slot_tokens: int32 [32, 16, 16, 1], P('dp', 'seq'), may hold values from 0 to 127, as said below
- slot_counts: int32 [32, 16, 16], P('dp', 'seq'), may hold values from 0 to 1, as said below
- gate_values: bfloat16 [32, 16, 16, 1], P('dp', 'seq'), may hold values from 0.099609375 to 1
- w_gate: bfloat16 [16, 4608, 1152], P('seq', 'dp'), may hold values from -0.1875 to 0.1875
- w_up: bfloat16 [16, 4608, 1152], P('seq', 'dp'), may hold values from -0.1875 to 0.1875
- w_down: bfloat16 [16, 4608, 1152], P('seq', 'dp'), may hold values from -0.09375 to 0.09375
Outputs:
- query_grad: bfloat16 [32, 2048, 1152], P('dp', 'seq')
- key_grad: bfloat16 [32, 2048, 1152], P('dp', 'seq')
- value_grad: bfloat16 [32, 2048, 1152], P('dp', 'seq')
- input_grad: bfloat16 [32, 2048, 1152], P('dp', 'seq')
- shift_grad: float32 [32, 1152], P('dp')
- scale_grad: float32 [32, 1152], P('dp')
- gate_w_grad: bfloat16 [16, 4608, 1152], P('seq', 'dp')
- up_w_grad: bfloat16 [16, 4608, 1152], P('seq', 'dp')
- down_w_grad: bfloat16 [16, 4608, 1152], P('seq', 'dp')
- gate_grad: float32 [32, 16, 16, 1], P('dp', 'seq')
Inputs may be any that keep to these rules, and one draw needn't show every extreme that they name: `slot_tokens`: the first slot_counts entries of each list are distinct; later entries are padding. `slot_counts`: in each video one expert has 1 live slots in every frame block.
All inputs are finite; a program needn't handle non-finite values.
Results may differ from a plain program's by a relative error of at most 0.03.
Values may be sent and summed in bfloat16 or wider, within the bound.
No kernel may reach another device: no remote copies, remote signals or barrier semaphores. Data moves between devices by JAX's collectives and lax.ppermute only.
A program may use at most 64 MiB of HBM per device.

v0:
```python
import math

import jax
import jax.numpy as jnp
from jax import lax
from jax.sharding import PartitionSpec as P

HEAD = 72


EPS = 1e-06


def softmax_rows(query_block, key_heads):
    head_size = query_block.shape[-1]
    scores = jnp.einsum(
        "qhd,khd->hqk", query_block, key_heads, preferred_element_type=jnp.float32
    ) * head_size ** (-0.5)
    highest = jnp.max(scores, axis=-1, keepdims=True)
    expo_vals = jnp.exp(scores - highest)
    return expo_vals / jnp.sum(expo_vals, axis=-1, keepdims=True)


def attend_forward(query_heads, key_heads, value_heads):
    length, heads_local, head_size = query_heads.shape
    block_size = math.gcd(length, 512)
    query_blocks = query_heads.reshape(length // block_size, block_size, heads_local, head_size)

    def one_block(query_block):
        weights_b = softmax_rows(query_block, key_heads).astype(jnp.bfloat16)
        return jnp.einsum(
            "hqk,khd->qhd", weights_b, value_heads, preferred_element_type=jnp.float32
        ).astype(jnp.bfloat16)

    return lax.map(one_block, query_blocks).reshape(length, heads_local, head_size)


def attend_backward(query_heads, key_heads, value_heads, output_heads, grad_heads):
    length, heads_local, head_size = query_heads.shape
    block_size = math.gcd(length, 512)
    factor = head_size ** (-0.5)
    shaped = (length // block_size, block_size, heads_local, head_size)

    def one_step(carry, blocks):
        key_acc, value_acc = carry
        query_block, output_block, grad_block = blocks
        probabilities = softmax_rows(query_block, key_heads)
        weights_b = probabilities.astype(jnp.bfloat16)
        prob_grad = jnp.einsum(
            "qhd,khd->hqk", grad_block, value_heads, preferred_element_type=jnp.float32
        )
        row_terms = jnp.sum(
            grad_block.astype(jnp.float32) * output_block.astype(jnp.float32), axis=-1
        )
        score_grad = (probabilities * (prob_grad - jnp.transpose(row_terms)[:, :, None])).astype(
            jnp.bfloat16
        )
        query_out = (
            jnp.einsum("hqk,khd->qhd", score_grad, key_heads, preferred_element_type=jnp.float32)
            * factor
        ).astype(jnp.bfloat16)
        key_acc = (
            key_acc
            + jnp.einsum(
                "hqk,qhd->khd", score_grad, query_block, preferred_element_type=jnp.float32
            )
            * factor
        )
        value_acc = value_acc + jnp.einsum(
            "hqk,qhd->khd", weights_b, grad_block, preferred_element_type=jnp.float32
        )
        return ((key_acc, value_acc), query_out)

    empty = jnp.zeros((length, heads_local, head_size), jnp.float32)
    (key_acc, value_acc), query_out = lax.scan(
        one_step,
        (empty, empty),
        (query_heads.reshape(shaped), output_heads.reshape(shaped), grad_heads.reshape(shaped)),
    )
    return (
        query_out.reshape(length, heads_local, head_size),
        key_acc.astype(jnp.bfloat16),
        value_acc.astype(jnp.bfloat16),
    )


def shards(
    queries,
    keys,
    values_in,
    inputs_x,
    out_grad,
    shift,
    scale,
    slot_tokens,
    slot_counts,
    gate_values,
    w_gate,
    w_up,
    w_down,
):
    tok_rows = queries.shape[1]
    model_width = queries.shape[2]
    seq_count = lax.axis_size("seq")
    video_count = lax.axis_size("dp")
    capacity = slot_tokens.shape[3]
    experts_all = slot_tokens.shape[2]
    positions = lax.broadcasted_iota(jnp.int32, (experts_all, capacity, tok_rows), 2)
    slot_ids = lax.broadcasted_iota(jnp.int32, (experts_all, capacity, tok_rows), 1)
    live_mask = slot_ids < slot_counts[0, 0][:, None, None]
    selector = jnp.where((slot_tokens[0, 0][:, :, None] == positions) & live_mask, 1.0, 0.0).astype(
        jnp.bfloat16
    )

    def pick_rows(source):
        return jnp.einsum(
            "ect,td->ecd", selector, source, preferred_element_type=jnp.float32
        ).astype(jnp.bfloat16)

    query_heads, key_heads, value_heads = (
        lax.all_to_all(queries, "seq", split_axis=2, concat_axis=1, tiled=True),
        lax.all_to_all(keys, "seq", split_axis=2, concat_axis=1, tiled=True),
        lax.all_to_all(values_in, "seq", split_axis=2, concat_axis=1, tiled=True),
    )
    length = query_heads.shape[1]
    shaped = (length, -1, HEAD)
    query_three = query_heads[0].reshape(shaped)
    key_three = key_heads[0].reshape(shaped)
    value_three = value_heads[0].reshape(shaped)
    output_three = attend_forward(query_three, key_three, value_three)
    attended = lax.all_to_all(
        output_three.reshape(1, length, -1), "seq", split_axis=1, concat_axis=2, tiled=True
    )
    residual = inputs_x[0].astype(jnp.float32) + attended[0].astype(jnp.float32)
    centered = residual - jnp.mean(residual, axis=-1, keepdims=True)
    inv_scale = lax.rsqrt(jnp.mean(centered * centered, axis=-1, keepdims=True) + EPS)
    normed = centered * inv_scale
    modulated = (normed * (1.0 + scale[0]) + shift[0]).astype(jnp.bfloat16)
    feature_rows = pick_rows(modulated)
    sent_rows, sent_grad, sent_gate = (
        lax.all_to_all(feature_rows, "seq", split_axis=0, concat_axis=0, tiled=True),
        lax.all_to_all(pick_rows(out_grad[0]), "seq", split_axis=0, concat_axis=0, tiled=True),
        lax.all_to_all(gate_values[0, 0], "seq", split_axis=0, concat_axis=0, tiled=True),
    )
    all_rows, all_grad, all_gate = (
        lax.all_gather(sent_rows[None], "dp", axis=0, tiled=True),
        lax.all_gather(sent_grad[None], "dp", axis=0, tiled=True),
        lax.all_gather(sent_gate[None], "dp", axis=0, tiled=True),
    )
    row_total = video_count * seq_count * capacity
    slot_rows = all_rows.reshape(row_total, model_width)
    grads_rows = all_grad.reshape(row_total, model_width)
    gate_column = all_gate.reshape(row_total, 1).astype(jnp.float32)
    gate_matrix = w_gate[0]
    up_matrix = w_up[0]
    down_matrix = w_down[0]
    contract_last = (((1,), (1,)), ((), ()))
    contract_first = (((0,), (0,)), ((), ()))
    gate_pre = lax.dot_general(
        slot_rows, gate_matrix, contract_last, preferred_element_type=jnp.float32
    )
    up_pre = lax.dot_general(
        slot_rows, up_matrix, contract_last, preferred_element_type=jnp.float32
    )
    sigmoid_gate = jax.nn.sigmoid(gate_pre)
    silu_gate = gate_pre * sigmoid_gate
    hidden = (silu_gate * up_pre).astype(jnp.bfloat16)
    back_hidden = lax.dot_general(
        grads_rows, down_matrix, contract_last, preferred_element_type=jnp.float32
    )
    gate_part = jnp.sum(hidden.astype(jnp.float32) * back_hidden, axis=1)
    scaled_grad = (gate_column * grads_rows.astype(jnp.float32)).astype(jnp.bfloat16)
    hidden_grad = gate_column * back_hidden
    gate_delta = (
        hidden_grad * up_pre * sigmoid_gate * (1.0 + gate_pre * (1.0 - sigmoid_gate))
    ).astype(jnp.bfloat16)
    up_delta = (hidden_grad * silu_gate).astype(jnp.bfloat16)
    gate_w_grad = lax.dot_general(
        gate_delta, slot_rows, contract_first, preferred_element_type=jnp.float32
    ).astype(jnp.bfloat16)[None]
    up_w_grad = lax.dot_general(
        up_delta, slot_rows, contract_first, preferred_element_type=jnp.float32
    ).astype(jnp.bfloat16)[None]
    down_w_grad = lax.dot_general(
        hidden, scaled_grad, contract_first, preferred_element_type=jnp.float32
    ).astype(jnp.bfloat16)[None]
    summed_gate = lax.psum_scatter(
        gate_part.reshape(video_count, -1), "dp", scatter_dimension=0, tiled=True
    )
    partial_back = jnp.dot(gate_delta, gate_matrix, preferred_element_type=jnp.float32) + jnp.dot(
        up_delta, up_matrix, preferred_element_type=jnp.float32
    )
    summed_back = lax.psum_scatter(
        partial_back.reshape(video_count, -1, model_width).astype(jnp.bfloat16),
        "dp",
        scatter_dimension=0,
        tiled=True,
    ).astype(jnp.float32)
    gate_grad = summed_gate.reshape(1, 1, seq_count, capacity)
    back_send = summed_back.reshape(seq_count, capacity, model_width).astype(jnp.bfloat16)
    returned = lax.all_to_all(back_send, "seq", split_axis=0, concat_axis=0, tiled=True)
    feature_grad = jnp.einsum("ect,ecd->td", selector, returned, preferred_element_type=jnp.float32)
    shift_part = jnp.sum(feature_grad, axis=0)
    scale_part = jnp.sum(feature_grad * normed, axis=0)
    shift_grad, scale_grad = lax.psum((shift_part, scale_part), "seq")
    normed_grad = feature_grad * (1.0 + scale[0])
    residual_grad = out_grad[0].astype(jnp.float32) + inv_scale * (
        normed_grad
        - jnp.mean(normed_grad, axis=-1, keepdims=True)
        - normed * jnp.mean(normed_grad * normed, axis=-1, keepdims=True)
    )
    input_grad = residual_grad.astype(jnp.bfloat16)[None]
    grad_heads = lax.all_to_all(input_grad, "seq", split_axis=2, concat_axis=1, tiled=True)
    query_out, key_out, value_out = attend_backward(
        query_three, key_three, value_three, output_three, grad_heads[0].reshape(shaped)
    )
    query_grad, key_grad, value_grad = (
        lax.all_to_all(
            query_out.reshape(1, length, -1), "seq", split_axis=1, concat_axis=2, tiled=True
        ),
        lax.all_to_all(
            key_out.reshape(1, length, -1), "seq", split_axis=1, concat_axis=2, tiled=True
        ),
        lax.all_to_all(
            value_out.reshape(1, length, -1), "seq", split_axis=1, concat_axis=2, tiled=True
        ),
    )
    return (
        query_grad,
        key_grad,
        value_grad,
        input_grad,
        shift_grad[None],
        scale_grad[None],
        gate_w_grad,
        up_w_grad,
        down_w_grad,
        gate_grad,
    )


def solution(mesh):
    in_specs = (
        P("dp", "seq", None),
        P("dp", "seq", None),
        P("dp", "seq", None),
        P("dp", "seq", None),
        P("dp", "seq", None),
        P("dp", None),
        P("dp", None),
        P("dp", "seq", None, None),
        P("dp", "seq", None),
        P("dp", "seq", None, None),
        P("seq", "dp", None),
        P("seq", "dp", None),
        P("seq", "dp", None),
    )
    out_specs = (
        P("dp", "seq", None),
        P("dp", "seq", None),
        P("dp", "seq", None),
        P("dp", "seq", None),
        P("dp", None),
        P("dp", None),
        P("seq", "dp", None),
        P("seq", "dp", None),
        P("seq", "dp", None),
        P("dp", "seq", None, None),
    )
    return jax.shard_map(shards, mesh=mesh, in_specs=in_specs, out_specs=out_specs, check_vma=False)
```

profile of v0, /device:TPU:2, one launch (start us, length us, event | category | flops | bytes accessed | tf_op | source)
XLA Modules:
  0.0 741.4 jit_solution(10259987763726677330)
XLA Ops:
  7.2 1.6 copy.145
  9.3 6.8 reduce.14
  16.9 11.8 %all-to-all-start = ((bf16[16,2,4608]{2,1,0:T(2,128)(2,1)}), bf16[16,2,4608]{2,1,0:T(2,128)(2,1)S(1)}, u32[]{:S(2)}, u32[]{:S(2)}) async-start(bf16[16,2,4608]{2,1,0:T(2,128)(2,1)} %reshape.419), calls=%async_computation | async-start | bytes 589824 | tf_op jit(solution)/shard_map/all_to_all | solution.py:121
  28.7 1.5 copy.147
  30.2 6.8 reduce.15
  38.6 7.3 all-to-all-start.1
  46.6 6.8 reduce.16
  54.2 1.1 all-to-all-done.1
  55.3 7.3 all-to-all-start.2
  63.7 7.7 %all-to-all-done.2 = bf16[16,2,4608]{2,1,0:T(2,128)(2,1)S(1)} async-done(((bf16[16,2,4608]{2,1,0:T(2,128)(2,1)}), bf16[16,2,4608]{2,1,0:T(2,128)(2,1)S(1)}, u32[]{:S(2)}, u32[]{:S(2)}) %all-to-all-start.2) | async-done | bytes 294944 | tf_op jit(solution)/shard_map/all_to_all | solution.py:123
  71.9 11.2 %while.25 = (s32[]{:T(128)}, bf16[4,512,1,72]{1,3,2,0:T(8,128)(2,1)S(1)}, bf16[4,512,1,72]{1,3,2,0:T(8,128)(2,1)S(1)}, bf16[2048,1,72]{0,2,1:T(8,128)(2,1)S(1)}, bf16[2048,1,72]{0,2,1:T(8,128)(2,1)S(1)}, /*index=5*/s32[]{:T(128)}) while((s32[]{:T(128)}, bf16[4,512,1,72]{1,3,2,0:T(8,128)(2,1)S(1)}, bf16[4,512,1,72]{1,3,2,0:T(8,128)(2,1)S(1)}, ...), condition=%wide.region_3.4_spmd, body=%wide.region_0.3_spmd.sunk | while | flops 311462912 | bytes 13330517 | solution.py:35
  73.6 1.1 fusion.123
  76.4 1.1 fusion.123
  79.2 1.1 fusion.123
  81.9 1.1 fusion.123
  84.4 11.5 %reduce.17 = bf16[2048,72]{1,0:T(8,128)(2,1)S(1)} reduce(bf16[2048,1,72]{2,1,0:T(2,128)(2,1)S(1)} %bitcast.292, bf16[]{:T(256)} %broadcast.247), dimensions={1}, to_apply=%bitcast.223.reduce_sub_computation | reduce | bytes 589826
  95.9 1.8 reshape.425
  97.7 5.3 all-to-all-start.3
  103.6 7.8 %all-to-all-done.3 = bf16[16,2,4608]{2,1,0:T(2,128)(2,1)S(1)} async-done(((bf16[16,2,4608]{2,1,0:T(2,128)(2,1)}), bf16[16,2,4608]{2,1,0:T(2,128)(2,1)S(1)}, u32[]{:S(2)}, u32[]{:S(2)}) %all-to-all-start.3) | async-done | bytes 294944 | tf_op jit(solution)/shard_map/all_to_all | solution.py:131
  111.4 1.8 reshape.426
  115.9 1.4 fusion.43
  118.0 12.3 %all_to_all.147 = bf16[16,2,576]{2,1,0:T(2,128)(2,1)S(1)} all-to-all(bf16[16,2,576]{2,1,0:T(2,128)(2,1)S(1)} %reshape.427), channel_id=1, replica_groups=mesh['dp'=32,'seq'=16] {'seq'}, dimensions={0} | all-to-all | bytes 73728 | tf_op jit(solution)/shard_map/all_to_all | solution.py:141
  132.1 11.1 %all_to_all.148 = bf16[16,2,576]{2,1,0:T(2,128)(2,1)S(1)} all-to-all(bf16[16,2,576]{2,1,0:T(2,128)(2,1)S(1)} %reshape.429), channel_id=1, replica_groups=mesh['dp'=32,'seq'=16] {'seq'}, dimensions={0} | all-to-all | bytes 73728 | tf_op jit(solution)/shard_map/all_to_all | solution.py:142
  144.7 4.7 all-to-all-start.4
  150.7 5.8 all-to-all-done.4
  156.9 65.2 %all-reduce = bf16[512]{0:T(512)(128)(2,1)S(1)} all-reduce(bf16[512]{0:T(512)(128)(2,1)S(1)} %dynamic-update-slice), channel_id=2, replica_groups=mesh['dp'=32,'seq'=16] {'dp'}, use_global_device_ids=true, to_apply=%add | all-reduce | flops 512 | bytes 2048
  222.1 1.8 fusion.46
  223.9 2.5 fusion.48
  226.5 68.3 %all-gather.6.cloned.1.call-done = bf16[512,1,1152]{2,0,1:T(8,128)(2,1)} async-done(((bf16[16,1,1152]{2,0,1:T(8,128)(2,1)}), bf16[512,1,1152]{2,0,1:T(8,128)(2,1)}) %all-gather.6.cloned.1.call-update) | async-done | bytes 1179664 | tf_op jit(solution)/shard_map/all_gather | solution.py:147
  294.8 2.7 multiply_reduce_fusion.7
  298.0 1.6 fusion.38
  299.6 119.4 %reduce-scatter.2.cloned.1.call-done = bf16[1,16,1152]{2,1,0:T(8,128)(2,1)} async-done(((bf16[32,16,1152]{2,1,0:T(8,128)(2,1)}), bf16[1,16,1152]{2,1,0:T(8,128)(2,1)}) %reduce-scatter.2.cloned.1.call-update) | async-done | bytes 36880 | tf_op jit(solution)/shard_map/reduce_scatter | solution.py:193
  419.1 1.4 reduce.20
  420.6 15.9 %all_to_all.149 = bf16[16,2,576]{2,1,0:T(2,128)(2,1)S(1)} all-to-all(bf16[16,2,576]{2,1,0:T(2,128)(2,1)S(1)} %reshape.431), channel_id=1, replica_groups=mesh['dp'=32,'seq'=16] {'seq'}, dimensions={0} | all-to-all | bytes 73728 | tf_op jit(solution)/shard_map/all_to_all | solution.py:201
  438.2 6.8 reduce.21
  445.8 5.0 all-to-all-start.8
  450.8 8.0 %all-to-all-done.8 = bf16[16,2,4608]{2,1,0:T(2,128)(2,1)S(1)} async-done(((bf16[16,2,4608]{2,1,0:T(2,128)(2,1)}), bf16[16,2,4608]{2,1,0:T(2,128)(2,1)S(1)}, u32[]{:S(2)}, u32[]{:S(2)}) %all-to-all-start.8) | async-done | bytes 294944 | tf_op jit(solution)/shard_map/all_to_all | solution.py:213
  459.4 24.0 %while.26 = (s32[]{:T(128)}, f32[2048,1,72]{0,2,1:T(8,128)S(1)}, f32[2048,1,72]{0,2,1:T(8,128)}, bf16[4,512,1,72]{1,3,2,0:T(8,128)(2,1)S(1)}, bf16[4,512,1,72]{1...) while((s32[]{:T(128)}, f32[2048,1,72]{0,2,1:T(8,128)S(1)}, ...), condition=%wide.region_13.14_spmd.clone, body=%wide.region_9.0_spmd.clone.sunk | while | flops 771660288 | bytes 31566032 | solution.py:75
  461.2 1.2 fusion.134
  462.3 1.7 multiply_convert_fusion.8
  467.1 1.2 fusion.134
  468.3 1.7 multiply_convert_fusion.8
  473.1 1.2 fusion.134
  474.3 1.7 multiply_convert_fusion.8
  479.1 1.2 fusion.134
  480.3 1.7 multiply_convert_fusion.8
  484.0 11.5 %reduce.22 = bf16[2048,72]{1,0:T(8,128)(2,1)S(1)} reduce(bf16[2048,1,72]{2,1,0:T(2,128)(2,1)S(1)} %bitcast.294, bf16[]{:T(256)} %broadcast.247), dimensions={1}, to_apply=%bitcast.227.reduce_sub_computation | reduce | bytes 589826
  495.5 1.8 reshape.435
  497.3 5.8 all-to-all-start.9
  504.0 12.4 %reduce.24 = bf16[2048,72]{1,0:T(8,128)(2,1)} reduce(bf16[2048,1,72]{2,1,0:T(2,128)(2,1)S(1)} %bitcast.295, bf16[]{:T(256)} %broadcast.247), dimensions={1}, to_apply=%bitcast.231.reduce_sub_computation | reduce | bytes 589826
  516.4 2.8 reshape.439
  519.3 8.1 %all-to-all-start.11 = ((bf16[16,2,4608]{2,1,0:T(2,128)(2,1)}), bf16[16,2,4608]{2,1,0:T(2,128)(2,1)}, u32[]{:S(2)}, u32[]{:S(2)}) async-start(bf16[16,2,4608]{2,1,0:T(2,128)(2,1)} %reshape.439), calls=%async_computation.12 | async-start | bytes 589824 | tf_op jit(solution)/shard_map/all_to_all | solution.py:224
  527.5 128.8 %all-reduce.1 = f32[32,16]{1,0:T(8,128)S(1)} all-reduce(f32[32,16]{1,0:T(8,128)S(1)} %reshape.387), channel_id=6, replica_groups=mesh['dp'=32,'seq'=16] {'dp'}, use_global_device_ids=true, to_apply=%region_19.20.clone | all-reduce | flops 512 | bytes 4096
  657.0 11.5 %reduce.23 = bf16[2048,72]{1,0:T(8,128)(2,1)S(1)} reduce(bf16[2048,1,72]{2,1,0:T(2,128)(2,1)S(1)} %bitcast.291, bf16[]{:T(256)} %broadcast.247), dimensions={1}, to_apply=%bitcast.229.reduce_sub_computation | reduce | bytes 589826
  668.6 1.8 reshape.437
  670.4 8.2 %all-to-all-start.10 = ((bf16[16,2,4608]{2,1,0:T(2,128)(2,1)}), bf16[16,2,4608]{2,1,0:T(2,128)(2,1)S(1)}, u32[]{:S(2)}, u32[]{:S(2)}) async-start(bf16[16,2,4608]{2,1,0:T(2,128)(2,1)} %reshape.437), calls=%async_computation.11 | async-start | bytes 589824 | tf_op jit(solution)/shard_map/all_to_all | solution.py:221
  678.6 1.2 dynamic-slice_bitcast_fusion
  679.8 2.0 fusion.39
  681.8 2.0 fusion.40
  683.8 2.5 fusion.41
  686.3 34.8 %all-reduce.2 = (f32[1,1152]{1,0:T(1,128)}, f32[1,1152]{1,0:T(1,128)}) all-reduce(f32[1,1152]{1,0:T(1,128)S(1)} %broadcast_in_dim.62, f32[1,1152]{1,0:T(1,128)S(1)} %broadcast_in_dim.63), channel_id=1, replica_groups=mesh['dp'=32,'seq'=16] {'seq'}, use_global_device_ids=true, to_apply=%region_15.16 | all-reduce | flops 2304 | bytes 18432 | tf_op jit(solution)/shard_map/psum | solution.py:205
  721.2 3.2 reshape.436
  726.1 3.2 reshape.440
  731.0 1.8 reshape.438
  (177 shorter events, 44.9 us)
Async XLA Ops:
  7.2 215.0 %copy-start = (bf16[1,144,1152]{2,1,0:T(8,128)(2,1)S(1)}, bf16[1,144,1152]{2,1,0:T(8,128)(2,1)}, u32[]{:S(2)}) copy-start(bf16[1,144,1152]{2,1,0:T(8,128)(2,1)} %param.27) | copy-start | bytes 995332
  7.2 38.7 %copy-start.11 = (bf16[1,128,1152]{2,1,0:T(8,128)(2,1)S(1)}, bf16[1,128,1152]{2,1,0:T(8,128)(2,1)}, u32[]{:S(2)}) copy-start(bf16[1,128,1152]{2,1,0:T(8,128)(2,1)} %param.19) | copy-start | bytes 884740
  16.9 21.7 %all-to-all-start = ((bf16[16,2,4608]{2,1,0:T(2,128)(2,1)}), bf16[16,2,4608]{2,1,0:T(2,128)(2,1)S(1)}, u32[]{:S(2)}, u32[]{:S(2)}) async-start(bf16[16,2,4608]{2,1,0:T(2,128)(2,1)} %reshape.419), calls=%async_computation | async-start | bytes 589824 | tf_op jit(solution)/shard_map/all_to_all | solution.py:121
  38.6 16.7 %all-to-all-start.1 = ((bf16[16,2,4608]{2,1,0:T(2,128)(2,1)}), bf16[16,2,4608]{2,1,0:T(2,128)(2,1)S(1)}, u32[]{:S(2)}, u32[]{:S(2)}) async-start(bf16[16,2,4608]{2,1,0:T(2,128)(2,1)} %reshape.421), calls=%async_computation.1 | async-start | bytes 589824 | tf_op jit(solution)/shard_map/all_to_all | solution.py:122
  55.3 16.1 %all-to-all-start.2 = ((bf16[16,2,4608]{2,1,0:T(2,128)(2,1)}), bf16[16,2,4608]{2,1,0:T(2,128)(2,1)S(1)}, u32[]{:S(2)}, u32[]{:S(2)}) async-start(bf16[16,2,4608]{2,1,0:T(2,128)(2,1)} %reshape.423), calls=%async_computation.2 | async-start | bytes 589824 | tf_op jit(solution)/shard_map/all_to_all | solution.py:123
  83.1 0.7 copy-start.12
  83.8 19.7 %copy-start.15 = (f32[1,1152]{1,0:T(1,128)S(1)}, f32[1,1152]{1,0:T(1,128)}, u32[]{:S(2)}) copy-start(f32[1,1152]{1,0:T(1,128)} %param.22) | copy-start | bytes 13828
  83.8 19.7 %copy-start.14 = (f32[1,1152]{1,0:T(1,128)S(1)}, f32[1,1152]{1,0:T(1,128)}, u32[]{:S(2)}) copy-start(f32[1,1152]{1,0:T(1,128)} %param.23) | copy-start | bytes 13828
  83.8 19.8 %copy-start.19 = (s32[1,1,16]{2,1,0:T(1,128)S(1)}, s32[1,1,16]{2,1,0:T(1,128)}, u32[]{:S(2)}) copy-start(s32[1,1,16]{2,1,0:T(1,128)} %param.25) | copy-start | bytes 196
  95.9 18.5 %copy-start.2 = (bf16[1,128,1152]{2,1,0:T(8,128)(2,1)S(1)}, bf16[1,128,1152]{2,1,0:T(8,128)(2,1)}, u32[]{:S(2)}) copy-start(bf16[1,128,1152]{2,1,0:T(8,128)(2,1)} %param.20) | copy-start | bytes 884740
  97.7 13.6 %all-to-all-start.3 = ((bf16[16,2,4608]{2,1,0:T(2,128)(2,1)}), bf16[16,2,4608]{2,1,0:T(2,128)(2,1)S(1)}, u32[]{:S(2)}, u32[]{:S(2)}) async-start(bf16[16,2,4608]{2,1,0:T(2,128)(2,1)} %reshape.425), calls=%async_computation.3 | async-start | bytes 589824 | tf_op jit(solution)/shard_map/all_to_all | solution.py:131
  103.1 119.1 %all-gather.8.cloned.1.call-start = ((), (), s32[]{:S(2)}) async-start(), calls=%async_computation.15 | async-start | bytes 1216512 | tf_op jit(solution)/shard_map/all_gather | solution.py:146
  113.2 2.7 copy-start.16
  113.8 17.3 %copy-start.10 = (bf16[1,128,1152]{2,1,0:T(8,128)(2,1)S(1)}, bf16[1,128,1152]{2,1,0:T(8,128)(2,1)}, u32[]{:S(2)}) copy-start(bf16[1,128,1152]{2,1,0:T(8,128)(2,1)} %param.21) | copy-start | bytes 884740
  113.9 30.1 %copy-start.18 = (bf16[1,1,16,1]{2,3,1,0:T(2,128)(2,1)S(1)}, bf16[1,1,16,1]{2,3,1,0:T(2,128)(2,1)}, u32[]{:S(2)}) copy-start(bf16[1,1,16,1]{2,3,1,0:T(2,128)(2,1)} %param.26) | copy-start | bytes 100
  113.9 35.6 %copy-start.17 = (u32[512]{0:T(512)S(1)}, u32[512]{0:T(512)}, u32[]{:S(2)}) copy-start(u32[512]{0:T(512)} %constant.67) | copy-start | bytes 6148
  114.2 109.7 %copy-start.3 = (bf16[1,144,1152]{2,1,0:T(8,128)(2,1)S(1)}, bf16[1,144,1152]{2,1,0:T(8,128)(2,1)}, u32[]{:S(2)}) copy-start(bf16[1,144,1152]{2,1,0:T(8,128)(2,1)} %param.28) | copy-start | bytes 995332
  131.1 163.7 %all-gather.6.cloned.1.call-start = ((), (), s32[]{:S(2)}) async-start(), calls=%async_computation.14 | async-start | bytes 1216512 | tf_op jit(solution)/shard_map/all_gather | solution.py:147
  144.7 11.8 %all-to-all-start.4 = ((bf16[16,1,1]{2,1,0:T(2,128)(2,1)}), bf16[16,1,1]{2,1,0:T(2,128)(2,1)S(1)}, u32[]{:S(2)}, u32[]{:S(2)}) async-start(bf16[16,1,1]{2,1,0:T(2,128)(2,1)} %copy.157), calls=%async_computation.4 | async-start | bytes 16384 | tf_op jit(solution)/shard_map/all_to_all | solution.py:143
  149.4 269.7 %reduce-scatter.2.cloned.1.call-start = ((), (), s32[]{:S(2)}) async-start(), calls=%async_computation.13 | async-start | bytes 1216512 | tf_op jit(solution)/shard_map/reduce_scatter | solution.py:193
  297.4 139.0 %copy-start.5 = (bf16[512,144]{0,1:T(8,128)(2,1)}, bf16[512,144]{0,1:T(8,128)(2,1)S(1)}, u32[]{:S(2)}) copy-start(bf16[512,144]{0,1:T(8,128)(2,1)S(1)} %get-tuple-element.290) | copy-start | bytes 442372
  297.4 139.0 %copy-start.6 = (bf16[512,144]{0,1:T(8,128)(2,1)}, bf16[512,144]{0,1:T(8,128)(2,1)S(1)}, u32[]{:S(2)}) copy-start(bf16[512,144]{0,1:T(8,128)(2,1)S(1)} %get-tuple-element.289) | copy-start | bytes 442372
  437.5 21.9 %copy-start.4 = (bf16[1,128,1152]{2,1,0:T(8,128)(2,1)}, bf16[1,128,1152]{2,1,0:T(8,128)(2,1)S(1)}, u32[]{:S(2)}) copy-start(bf16[1,128,1152]{2,1,0:T(8,128)(2,1)S(1)} %fusion.66) | copy-start | bytes 884740
  437.5 21.9 %copy-start.13 = (bf16[2048,1,72]{0,2,1:T(8,128)(2,1)S(1)}, bf16[2048,1,72]{0,2,1:T(8,128)(2,1)}, u32[]{:S(2)}) copy-start(bf16[2048,1,72]{0,2,1:T(8,128)(2,1)} %copy-done.12) | copy-start | bytes 884740
  445.8 13.1 %all-to-all-start.8 = ((bf16[16,2,4608]{2,1,0:T(2,128)(2,1)}), bf16[16,2,4608]{2,1,0:T(2,128)(2,1)S(1)}, u32[]{:S(2)}, u32[]{:S(2)}) async-start(bf16[16,2,4608]{2,1,0:T(2,128)(2,1)} %reshape.433), calls=%async_computation.9 | async-start | bytes 589824 | tf_op jit(solution)/shard_map/all_to_all | solution.py:213
  459.5 1.7 copy-start.7
  462.3 1.7 copy-start.8
  465.5 1.7 copy-start.7
  468.3 1.7 copy-start.8
  471.5 1.7 copy-start.7
  474.3 1.7 copy-start.8
  477.5 1.7 copy-start.7
  480.3 1.7 copy-start.8
  483.4 19.8 %copy-start.9 = (f32[2048,1,72]{0,2,1:T(8,128)S(1)}, f32[2048,1,72]{0,2,1:T(8,128)}, u32[]{:S(2)}) copy-start(f32[2048,1,72]{0,2,1:T(8,128)} %get-tuple-element.89) | copy-start | bytes 1769476
  497.3 21.9 %all-to-all-start.9 = ((bf16[16,2,4608]{2,1,0:T(2,128)(2,1)}), bf16[16,2,4608]{2,1,0:T(2,128)(2,1)}, u32[]{:S(2)}, u32[]{:S(2)}) async-start(bf16[16,2,4608]{2,1,0:T(2,128)(2,1)} %reshape.435), calls=%async_computation.10 | async-start | bytes 589824 | tf_op jit(solution)/shard_map/all_to_all | solution.py:218
  504.0 175.8 %copy-start.1 = (bf16[512,1,1152]{2,0,1:T(8,128)(2,1)S(1)}, bf16[512,1,1152]{2,0,1:T(8,128)(2,1)}, u32[]{:S(2)}) copy-start(bf16[512,1,1152]{2,0,1:T(8,128)(2,1)} %all-gather.8.cloned.1.call-done) | copy-start | bytes 3538948
  519.3 151.1 %all-to-all-start.11 = ((bf16[16,2,4608]{2,1,0:T(2,128)(2,1)}), bf16[16,2,4608]{2,1,0:T(2,128)(2,1)}, u32[]{:S(2)}, u32[]{:S(2)}) async-start(bf16[16,2,4608]{2,1,0:T(2,128)(2,1)} %reshape.439), calls=%async_computation.12 | async-start | bytes 589824 | tf_op jit(solution)/shard_map/all_to_all | solution.py:224
  670.4 60.6 %all-to-all-start.10 = ((bf16[16,2,4608]{2,1,0:T(2,128)(2,1)}), bf16[16,2,4608]{2,1,0:T(2,128)(2,1)S(1)}, u32[]{:S(2)}, u32[]{:S(2)}) async-start(bf16[16,2,4608]{2,1,0:T(2,128)(2,1)} %reshape.437), calls=%async_computation.11 | async-start | bytes 589824 | tf_op jit(solution)/shard_map/all_to_all | solution.py:221
Sparse Core Ops, SparseCore 0:
  131.2 79.4 all-gather.7
  214.6 80.1 all-gather.5
  299.8 119.2 reduce-scatter.1
where the time goes:
time: 750 us; the launch traced here: 741 us
  blocking collectives  268 us (36%)
  waiting for transfers between devices  219 us (29%)
  other arithmetic  84.7 us (11%)
  starting transfers between devices  64.2 us (9%)
  matrix products  45.8 us (6%)
  local copies, waits for them, and re-layouts  43.7 us (6%)
  between operations  15.6 us (2%)
    unnamed x2, blocking collectives  194 us
    reduce_scatter x1, waiting for transfers between devices, shards(): lax.psum_scatter(partial_back.reshape(video_count, -1, model_width).astyp...  119 us
    unnamed x12, other arithmetic  74.2 us
    all_gather x1, waiting for transfers between devices, shards(): lax.all_gather(sent_grad[None], 'dp', axis=0, tiled=True)  68.3 us
    psum x1, blocking collectives, shards(): shift_grad, scale_grad = lax.psum((shift_part, scale_part), 'seq')  34.8 us
    unnamed x78, local copies, waits for them, and re-layouts  32.4 us
    all_to_all x1, blocking collectives, shards(): lax.all_to_all(back_send, 'seq', split_axis=0, concat_axis=0, tiled=True)  15.9 us
  transfers between devices with their start and end apart: 12, of which 8 were waited for; matrix products, arithmetic and copies ran while one was open for 10% of the time, Pallas kernels for 0%

commit v1 on v0

v1 whole, which is shorter than its diff:
```python
import functools

import jax
import jax.numpy as jnp
from jax import lax
from jax.experimental import pallas as pl
from jax.experimental.pallas import tpu as pltpu
from jax.sharding import Mesh
from jax.sharding import PartitionSpec as P

HEAD = 72
EPS = 1e-06
LANES = 128
LOG2E = 1.4426950408889634
BF = jnp.bfloat16
F32 = jnp.float32
NN = (((1,), (0,)), ((), ()))
NT = (((1,), (1,)), ((), ()))
TN = (((0,), (0,)), ((), ()))
DP = ("yh", "yl", "xh", "core")
ROWS = ("yh", "xh")
SEQ = ("xl", "z")


def mm(left, right, dims):
    return lax.dot_general(left, right, dims, preferred_element_type=F32)


def iota(shape, dim):
    return lax.broadcasted_iota(jnp.int32, shape, dim)


def pad_lanes(block, lanes=LANES):
    rows, have = block.shape
    return jnp.concatenate([block, jnp.zeros((rows, lanes - have), block.dtype)], axis=1)


def call(kernel, outs, flops=1_000_000, mib=16, **kwargs):
    return pl.pallas_call(
        kernel,
        out_shape=outs,
        compiler_params=pltpu.CompilerParams(vmem_limit_bytes=mib * 1024 * 1024),
        cost_estimate=pl.CostEstimate(flops=flops, bytes_accessed=2_000_000, transcendentals=0),
        **kwargs,
    )


def vmem(*arrays):
    return [pltpu.with_memory_space_constraint(a, pltpu.VMEM) for a in arrays]


def hbm(*arrays):
    return [pltpu.with_memory_space_constraint(a, pltpu.HBM) for a in arrays]


ANY = pl.BlockSpec(memory_space=pl.ANY)
HBM = pl.BlockSpec(memory_space=pltpu.HBM)


def whole(shape):
    return pl.BlockSpec(shape, lambda *_: (0,) * len(shape))


def to_column(row):
    n = row.shape[1]
    eye = iota((n, n), 0) == iota((n, n), 1)
    return jnp.sum(jnp.where(eye, jnp.broadcast_to(row, (n, n)), 0.0), axis=1, keepdims=True)


def to_row(column):
    n = column.shape[0]
    eye = iota((n, n), 0) == iota((n, n), 1)
    return jnp.sum(jnp.where(eye, jnp.broadcast_to(column, (n, n)), 0.0), axis=0, keepdims=True)


def fold(rows):
    count, width = rows.shape
    return [
        jnp.concatenate(
            [rows[r : r + 1, c : c + LANES] for c in range(0, width, LANES)], axis=0
        )
        for r in range(count)
    ]


def unfold(blocks):
    depth = blocks[0].shape[0]
    return jnp.concatenate(
        [jnp.concatenate([b[i : i + 1] for b in blocks], axis=0) for i in range(depth)], axis=1
    )


def selector(tok_ref, cnt_ref, tokens):
    experts = tok_ref.shape[2]
    live = to_column(cnt_ref[0].astype(F32)) > 0.0
    named = to_column(tok_ref[0].astype(F32))
    hit = (named == iota((experts, tokens), 1).astype(F32)) & live
    return jnp.where(hit, 1.0, 0.0).astype(BF), jnp.where(live, 1.0, 0.0)


def keys_kernel(q_ref, k_ref, v_ref, tok_ref, cnt_ref, sent_ref):
    tokens, width = q_ref.shape[1:]
    heads = width // HEAD
    sel, _ = selector(tok_ref, cnt_ref, tokens)
    rows_q = mm(sel, q_ref[0], NN)
    key_t = k_ref[0].astype(F32).T
    value_t = v_ref[0].astype(F32).T
    for h in range(heads):
        part = slice(h * HEAD, (h + 1) * HEAD)
        block = jnp.concatenate([key_t[part], value_t[part], pad_lanes(rows_q[:, part])], axis=0)
        sent_ref[h] = block.astype(BF)


def queries_kernel(q_ref, g_ref, x_ref, tok_ref, cnt_ref, gate_ref, sent_ref, sel_ref):
    tokens, width = x_ref.shape[1:]
    sel, live = selector(tok_ref, cnt_ref, tokens)
    sel_ref[...] = sel
    experts = sel.shape[0]
    folded_x = fold(mm(sel, x_ref[0], NN))
    folded_g = fold(mm(sel, g_ref[0], NN))
    lane = iota((experts, LANES), 1)
    gate = to_column(gate_ref[0].astype(F32))
    extra = jnp.where(lane == 0, gate, jnp.where(lane == 1, live, 0.0))
    query_t = q_ref[0].astype(F32).T
    grad_t = g_ref[0].astype(F32).T
    used = 2 * (width // LANES) + 1
    blank = jnp.zeros((2 * experts - used, LANES), F32)
    for h in range(width // HEAD):
        part = slice(h * HEAD, (h + 1) * HEAD)
        block = jnp.concatenate(
            [query_t[part], grad_t[part], folded_x[h], folded_g[h], extra[h : h + 1], blank], axis=0
        )
        sent_ref[h, experts:, :] = block.astype(BF)


def lay_out(ref, rows, first=0):
    return jnp.concatenate([ref[i, first : first + rows, :] for i in range(ref.shape[0])], axis=1)


def row_softmax(scores):
    lowered = (scores - jnp.max(scores, axis=1, keepdims=True)) * (HEAD ** (-0.5) * LOG2E)
    expo = jnp.exp2(lowered)
    return expo, 1.0 / jnp.sum(expo, axis=1, keepdims=True)


def slot_order(frames, experts):
    total = frames * experts
    row, col = iota((total, total), 0), iota((total, total), 1)
    return jnp.where(col == (row % frames) * experts + row // frames, 1.0, 0.0).astype(BF)


def slot_forward_kernel(
    got_ref, _, w_0, w_1, w_2, next_ref, out_ref, query_ref, kv_ref, sem
):
    frames, rows = got_ref.shape[:2]
    experts = rows - 2 * HEAD
    kv_ref[...] = lay_out(got_ref, 2 * HEAD)
    query = jnp.concatenate([got_ref[i, 2 * HEAD :, :] for i in range(frames)], axis=0)
    query = mm(slot_order(frames, experts), query, NN).astype(BF)
    query_ref[...] = query
    total = frames * experts
    wide = jnp.concatenate([query, jnp.zeros((total, 2 * HEAD - LANES), BF)], axis=1)
    kv = kv_ref[...]
    step = 128
    for start in range(0, total, step):
        expo, inv = row_softmax(mm(wide[start : start + step], kv, NN))
        attended = mm(expo.astype(BF), kv, NT) * inv
        attended = pad_lanes(attended[:, HEAD:]).astype(BF)
        out_ref[start // frames : (start + step) // frames] = attended.reshape(
            step // frames, frames, LANES
        )
    copy = pltpu.make_async_copy(out_ref, next_ref.at[:, 0:frames, :], sem)
    copy.start()
    copy.wait()


def head_lanes(ref, rows):
    return jnp.concatenate(
        [ref[h, 0:rows, :].astype(F32)[:, :HEAD] for h in range(ref.shape[0])], axis=1
    )


def norm_kernel(got_ref, shift_ref, scale_ref, w_0, w_1, sent_ref, normed_ref, inv_ref):
    frames = got_ref.shape[0]
    width = shift_ref.shape[1]
    depth = width // LANES
    first = frames + 2 * HEAD
    blocks = [got_ref[i, first:, :].astype(F32) for i in range(frames)]
    inputs = unfold([b[0:depth] for b in blocks])
    grads = unfold([b[depth : 2 * depth + 1] for b in blocks])
    live = grads[:, width + 1 : width + 2]
    residual = inputs + head_lanes(got_ref, frames)
    centered = residual - jnp.mean(residual, axis=1, keepdims=True)
    inv = lax.rsqrt(jnp.mean(centered * centered, axis=1, keepdims=True) + EPS)
    normed = centered * inv
    modulated = (normed * (1.0 + scale_ref[...]) + shift_ref[...]) * live
    sent = jnp.concatenate([modulated, grads], axis=1).astype(BF)
    for i in range(sent_ref.shape[0]):
        sent_ref[i] = sent
    normed_ref[...] = normed
    inv_ref[...] = jnp.broadcast_to(inv, inv_ref.shape)


def expert_rows(rows_ref):
    groups, frames, size = rows_ref.shape
    width = (size - LANES) // 2
    both = rows_ref[...].reshape(groups * frames, size)
    gates = both[:, 2 * width :].astype(F32)[:, 0:1]
    return both[:, :width], both[:, width : 2 * width], gates


def expert_kernel(rows_ref, *refs):
    weights, (early, back_ref, hidden_ref, gate_ref, up_ref, held, sems) = refs[:-7], refs[-7:]
    copies = [
        pltpu.make_async_copy(ref.at[0], held.at[i], sems.at[i])
        for i, ref in enumerate(weights[:3])
    ]
    for copy in copies:
        copy.start()
    groups, frames = rows_ref.shape[:2]
    rows, grads, gates = expert_rows(rows_ref)
    total, width = rows.shape
    back = jnp.zeros((total, width), F32)
    gate_part = jnp.zeros((total, 1), F32)
    for part in (1, 2, 3, 0):
        if part == 0:
            for copy in copies:
                copy.wait()
            gate_w, up_w, down_w = (held[i] for i in range(3))
        else:
            gate_w, up_w, down_w = (ref[0] for ref in weights[3 * part : 3 * part + 3])
        gate_pre = mm(rows, gate_w, NT)
        up_pre = mm(rows, up_w, NT)
        back_hidden = mm(grads, down_w, NT)
        sig = jax.nn.sigmoid(gate_pre)
        silu = gate_pre * sig
        hidden = (silu * up_pre).astype(BF)
        gate_part += jnp.sum(hidden.astype(F32) * back_hidden, axis=1, keepdims=True)
        hidden_grad = gates * back_hidden
        gate_delta = (hidden_grad * up_pre * sig * (1.0 + gate_pre * (1.0 - sig))).astype(BF)
        up_delta = (hidden_grad * silu).astype(BF)
        back += mm(gate_delta, gate_w, NN) + mm(up_delta, up_w, NN)
        hidden_ref[part] = hidden
        gate_ref[part] = gate_delta
        up_ref[part] = up_delta
    lane = iota((total, LANES), 1)
    high = gate_part.astype(BF).astype(F32)
    extra = jnp.where(lane == 0, high, jnp.where(lane == 1, gate_part - high, 0.0))
    back_ref[...] = (
        jnp.concatenate([back, extra], axis=1).astype(BF).reshape(groups, frames, width + LANES)
    )


def weight_grads_kernel(rows_ref, hidden_ref, gate_ref, up_ref, late, own_ref, other_ref):
    rows, grads, gates = expert_rows(rows_ref)
    scaled = (gates * grads.astype(F32)).astype(BF)
    for part in range(hidden_ref.shape[0]):
        out = (own_ref, other_ref)[part % 2]
        out[part // 2, 0] = mm(gate_ref[part], rows, TN).astype(out.dtype)
        out[part // 2, 1] = mm(up_ref[part], rows, TN).astype(out.dtype)
        out[part // 2, 2] = mm(hidden_ref[part], scaled, TN).astype(out.dtype)


def back_kernel(
    got_ref, normed_ref, inv_ref, scale_ref, _, _others, sent_ref, gate_ref, others, send_ref, sem
):
    frames, width = normed_ref.shape
    total = got_ref[0].astype(F32)
    for i in range(1, got_ref.shape[0]):
        total += got_ref[i].astype(F32)
    gate_ref[0] = to_row(total[:, width : width + 1] + total[:, width + 1 : width + 2])
    back = total[:, :width].astype(BF).astype(F32)
    normed = normed_ref[...]
    shift_part = jnp.sum(back, axis=0, keepdims=True)
    scale_part = jnp.sum(back * normed, axis=0, keepdims=True)
    grad = back * (1.0 + scale_ref[...])
    delta = inv_ref[:, 0:1] * (
        grad
        - jnp.mean(grad, axis=1, keepdims=True)
        - normed * jnp.mean(grad * normed, axis=1, keepdims=True)
    )
    parts = []
    for part in (shift_part, scale_part):
        high = part.astype(BF).astype(F32)
        parts += [high, part - high]
    block = jnp.concatenate([delta] + parts, axis=0)
    folded = fold(delta)
    depth = width // LANES
    blank = jnp.zeros((frames - 4 - depth, LANES), F32)
    for h in range(send_ref.shape[0]):
        head = pad_lanes(block[:, h * HEAD : (h + 1) * HEAD])
        send_ref[h] = jnp.concatenate([head, folded[h], blank], axis=0).astype(BF)
    copy = pltpu.make_async_copy(send_ref, sent_ref.at[:, 0 : 2 * frames, :], sem)
    copy.start()
    copy.wait()


def attention_kernel(started, kv_in_ref, qg_ref, *refs):
    frames = kv_in_ref.shape[0]
    refs, (dq_ref, sums_ref, kv_ref) = refs[:-3], refs[-3:]

    @pl.when(pl.program_id(0) == 0)
    def _():
        sums_ref[...] = refs[2][...] if started else jnp.zeros_like(sums_ref)
        kv_ref[...] = lay_out(kv_in_ref, 2 * HEAD)

    kv = kv_ref[...]
    factor = HEAD ** (-0.5)
    wide = lay_out(qg_ref, 2 * HEAD, frames).astype(F32)
    tall = wide.T
    lane = iota(tall.shape, 1)
    query = jnp.where(lane < HEAD, tall, 0.0).astype(BF)
    grad_f = jnp.where(lane >= HEAD, tall, 0.0)
    grad = grad_f.astype(BF)
    expo, inv = row_softmax(mm(query, kv, NN))
    expo_b = expo.astype(BF)
    attended = (mm(expo_b, kv, NT) * inv).astype(BF).astype(F32)
    row_terms = jnp.sum(grad_f * attended, axis=1, keepdims=True)
    score_grad = (expo * (mm(grad, kv, NN) - row_terms)).astype(BF)
    dq_t = (mm(score_grad, kv, NT) * (inv * factor)).T
    blank = jnp.zeros((dq_ref.shape[1] - 2 * frames - HEAD, LANES), F32)
    for i in range(dq_ref.shape[0]):
        block = jnp.concatenate([dq_t[0:HEAD, i * LANES : (i + 1) * LANES], blank], axis=0)
        dq_ref[i, 2 * frames :, :] = block.astype(BF)
    scaled = (tall * jnp.where(lane < HEAD, inv * factor, inv)).T
    sums_ref[0:HEAD, :] += mm(scaled[0:HEAD].astype(BF), score_grad, NN)
    sums_ref[HEAD:, :] += mm(scaled[HEAD:].astype(BF), expo_b, NN)


def late_kernel(got_ref, kv_in_ref, query_ref, att_ref, sums_ref, near, sent_ref):
    experts = got_ref.shape[0]
    frames = sent_ref.shape[0]
    total = experts * frames
    factor = HEAD ** (-0.5)
    kv = lay_out(kv_in_ref, 2 * HEAD)
    got = [got_ref[e].astype(F32) for e in range(experts)]
    delta = jnp.concatenate([block[0:frames] for block in got], axis=0)
    attended = att_ref[...].reshape(total, LANES).astype(F32)
    row_terms = jnp.sum(delta * attended, axis=1, keepdims=True)
    wide = jnp.concatenate([jnp.zeros((total, HEAD), F32), delta[:, :HEAD]], axis=1).astype(BF)
    query = query_ref[...]
    query_wide = jnp.concatenate([query, jnp.zeros((total, 2 * HEAD - LANES), BF)], axis=1)
    expo, inv = row_softmax(mm(query_wide, kv, NN))
    score_grad = (expo * (mm(wide, kv, NN) - row_terms)).astype(BF)
    dq = (mm(score_grad, kv, NT)[:, :LANES] * (inv * factor)).astype(BF)
    query_t = (query.astype(F32) * (inv * factor)).T[0:HEAD].astype(BF)
    delta_t = (delta * inv).T[0:HEAD].astype(BF)
    dk = mm(query_t, score_grad, NN)
    dv = mm(delta_t, expo.astype(BF), NN)
    both = sums_ref[...] + jnp.concatenate([dk, dv], axis=0)
    dq = mm(slot_order(experts, frames), dq, NN).astype(BF)
    sums = got[0][frames : frames + 4]
    for block in got[1:]:
        sums = sums + block[frames : frames + 4]
    parts = []
    for part in (sums[0:1] + sums[1:2], sums[2:3] + sums[3:4]):
        high = part.astype(BF).astype(F32)
        parts += [high, part - high]
    tail = jnp.concatenate(parts + [jnp.zeros((12, LANES), F32)], axis=0).astype(BF)
    body = 2 * HEAD
    for s in range(frames):
        rows = slice(s * experts, (s + 1) * experts)
        sent_ref[s, 0:body, :] = both[:, s * LANES : (s + 1) * LANES].astype(BF)
        sent_ref[s, body : body + experts, :] = dq[rows]
        sent_ref[s, body + experts :, :] = tail


def inputs_kernel(got_ref, g_ref, sel_ref, di_ref, dq_ref):
    heads = got_ref.shape[0]
    frames, width = heads, g_ref.shape[2]
    depth = width // LANES
    first = frames + 4
    blocks = [got_ref[e, frames : 2 * frames, :].astype(F32)[4 : 4 + depth] for e in range(heads)]
    delta = unfold(blocks).astype(BF)
    di_ref[0] = (g_ref[0].astype(F32) + mm(sel_ref[...], delta, TN)).astype(BF)
    parts = [got_ref[h, 2 * frames :, :].astype(F32)[0:HEAD] for h in range(heads)]
    dq_ref[...] = jnp.concatenate(parts, axis=0).T.astype(BF)


def final_kernel(got_ref, early_ref, sel_ref, dq_ref, dk_ref, dv_ref, sh_ref, sc_ref):
    heads = got_ref.shape[0]
    experts = sel_ref.shape[0]
    body = 2 * HEAD
    got = [got_ref[h, 0:body, :].astype(F32) for h in range(heads)]
    dk_ref[0] = jnp.concatenate([b[0:HEAD] for b in got], axis=0).T.astype(BF)
    dv_ref[0] = jnp.concatenate([b[HEAD:] for b in got], axis=0).T.astype(BF)
    tails = [got_ref[h, body:, :].astype(F32)[:, :HEAD] for h in range(heads)]
    tail = jnp.concatenate(tails, axis=1)
    late = tail[0:experts].astype(BF)
    sums = tail[experts:]
    dq_ref[0] = (early_ref[...].astype(F32) + mm(sel_ref[...], late, TN)).astype(BF)
    sh_ref[...] = sums[0:1] + sums[1:2]
    sc_ref[...] = sums[2:3] + sums[3:4]


def swap(block, axes):
    return lax.all_to_all(block, axes, split_axis=0, concat_axis=0, tiled=True)


def shards(
    queries,
    keys,
    values_in,
    inputs_x,
    out_grad,
    shift,
    scale,
    slot_tokens,
    slot_counts,
    gate_values,
    w_gate,
    w_up,
    w_down,
):
    tokens, width = queries.shape[1:]
    frames = lax.axis_size(SEQ)
    groups = lax.axis_size(ROWS)
    experts = slot_tokens.shape[2]
    heads = width // HEAD
    length = frames * tokens
    hidden = w_gate.shape[1]
    body = 2 * HEAD
    total = frames * experts
    slot_tokens = slot_tokens.reshape(1, 1, experts)
    gate_values = gate_values.reshape(1, 1, experts)

    other = [(0, 1), (1, 0)]

    def across(block, axis):
        return lax.ppermute(block, axis, other)

    w_own = [w_gate, w_up, w_down]
    w_near = [across(w, "yl") for w in w_own]
    w_core = [across(w, "core") for w in w_own]
    w_far = [across(w, "core") for w in w_near]

    (keys_sent,) = call(keys_kernel, [pltpu.HBM((heads, body + experts, tokens), BF)], mib=60)(
        queries, keys, values_in, slot_tokens, slot_counts
    )
    keys_got = swap(keys_sent, SEQ)
    rows_next = experts + body + 2 * experts
    qg_sent, sel = call(
        queries_kernel, [pltpu.HBM((heads, rows_next, tokens), BF), pltpu.HBM((experts, tokens), BF)]
    )(queries, out_grad, inputs_x, slot_tokens, slot_counts, gate_values)

    qg_sent, att, slot_query = call(
        slot_forward_kernel,
        [
            pltpu.HBM((heads, rows_next, tokens), BF),
            pltpu.HBM((experts, frames, LANES), BF),
            pltpu.HBM((total, LANES), BF),
        ],
        in_specs=[whole(keys_got.shape)] + [ANY] * 4,
        out_specs=[
            ANY,
            whole((experts, frames, LANES)),
            whole((total, LANES)),
        ],
        input_output_aliases={1: 0},
        scratch_shapes=[pltpu.VMEM((body, length), BF), pltpu.SemaphoreType.DMA],
    )(keys_got, *hbm(qg_sent), w_near[0], w_core[0], w_core[1])
    qg_got = swap(qg_sent, SEQ)

    sent_width = 2 * width + LANES
    rows_sent, normed, inv = call(
        norm_kernel,
        [
            pltpu.HBM((groups, frames, sent_width), BF),
            pltpu.HBM((frames, width), F32),
            pltpu.HBM((frames, LANES), F32),
        ],
        in_specs=[whole(qg_got.shape), whole(shift.shape), whole(scale.shape)] + [ANY] * 2,
    )(qg_got, shift, scale, w_near[1], w_near[2])
    rows_all = swap(rows_sent, ROWS)

    block = 2
    first_steps = 5
    rows_back = 2 * frames + HEAD + 8
    early_outs = [pltpu.HBM((frames, rows_back, tokens), BF), pltpu.HBM((body, length), F32)]

    def early(started, steps, skip, extra, extra_specs, **kwargs):
        return call(
            functools.partial(attention_kernel, started),
            early_outs,
            flops=20_000_000_000 * steps,
            grid=(steps,),
            in_specs=[
                whole(keys_got.shape),
                pl.BlockSpec((block, rows_next, tokens), lambda i: (i + skip, 0, 0)),
            ]
            + extra_specs,
            out_specs=[
                pl.BlockSpec((block, rows_back, tokens), lambda i: (i + skip, 0, 0)),
                whole((body, length)),
            ],
            scratch_shapes=[pltpu.VMEM((body, length), BF)],
            **kwargs,
        )(keys_got, qg_got, *extra)

    back_next, sums = early(False, first_steps, 0, hbm(inv), [ANY])

    back_sent, hid, gate_delta, up_delta = call(
        expert_kernel,
        [pltpu.HBM((groups, frames, width + LANES), BF)]
        + [pltpu.HBM((4, groups * frames, hidden), BF)] * 3,
        in_specs=[whole(rows_all.shape)] + [HBM] * 3 + [whole(w_gate.shape)] * 9 + [ANY],
        scratch_shapes=[pltpu.VMEM((3, hidden, width), BF), pltpu.SemaphoreType.DMA((3,))],
    )(rows_all, *hbm(*w_own), *vmem(*w_core, *w_near, *w_far), *hbm(sums))
    back_got = swap(back_sent, ROWS)

    back_next, sums = early(
        True,
        frames // block - first_steps,
        first_steps,
        hbm(back_next, back_sent, sums),
        [ANY, ANY, whole((body, length))],
        input_output_aliases={2: 0},
    )

    own, others = call(
        weight_grads_kernel,
        [pltpu.HBM((2, 3, hidden, width), BF)] * 2,
        in_specs=[whole(a.shape) for a in (rows_all, hid, gate_delta, up_delta)] + [ANY],
    )(rows_all, *hbm(hid, gate_delta, up_delta, sums))
    back_next, gate_grad, others = call(
        back_kernel,
        [
            pltpu.HBM((heads, rows_back, LANES), BF),
            jax.ShapeDtypeStruct((1, 1, frames), F32),
            pltpu.HBM(others.shape, BF),
        ],
        in_specs=[
            whole(back_got.shape),
            whole(normed.shape),
            whole(inv.shape),
            whole(scale.shape),
            ANY,
            ANY,
        ],
        out_specs=[ANY, whole((1, 1, frames)), ANY],
        input_output_aliases={4: 0, 5: 2},
        scratch_shapes=[
            pltpu.VMEM((heads, 2 * frames, LANES), BF),
            pltpu.SemaphoreType.DMA,
        ],
    )(back_got, *hbm(normed, inv), scale, *hbm(back_next, others))
    delta_got = swap(back_next, SEQ)

    got_core = across(others, "core")
    near = (own[1].astype(F32) + got_core[1].astype(F32)).astype(BF)
    got_near = across(near, "yl")
    w_grads = [
        (own[0, i].astype(F32) + got_core[0, i].astype(F32) + got_near[i].astype(F32)).astype(BF)[
            None
        ]
        for i in range(3)
    ]


    (late_sent,) = call(
        late_kernel,
        [pltpu.HBM((frames, body + 2 * experts, tokens), BF)],
        grid=(1,),
        in_specs=[whole((experts, 2 * frames, LANES))]
        + [whole(a.shape) for a in (keys_got, slot_query, att)]
        + [whole((body, length)), ANY],
        out_specs=[whole((frames, body + 2 * experts, tokens))],
    )(delta_got, keys_got, *hbm(slot_query, att, sums, near))
    late_got = swap(late_sent, SEQ)

    block_shape = jax.ShapeDtypeStruct((1, tokens, width), BF)
    input_grad, query_early = call(inputs_kernel, [block_shape, pltpu.HBM((tokens, width), BF)])(
        delta_got, out_grad, *hbm(sel)
    )
    query_grad, key_grad, value_grad, shift_grad, scale_grad = call(
        final_kernel, [block_shape] * 3 + [jax.ShapeDtypeStruct((1, width), F32)] * 2
    )(late_got, *hbm(query_early, sel))
    return (
        query_grad,
        key_grad,
        value_grad,
        input_grad,
        shift_grad,
        scale_grad,
        *w_grads,
        gate_grad.reshape(1, 1, frames, 1),
    )


def solution(mesh):
    dp_size, seq_size = mesh.devices.shape
    fine = Mesh(
        mesh.devices.reshape(dp_size // 8, 2, 2, 2, 2, seq_size // 2),
        ("yh", "yl", "xh", "core", "xl", "z"),
    )
    rows = P(DP, SEQ, None)
    flat = P(DP, None)
    slots = P(DP, SEQ, None, None)
    weights = P(SEQ, DP, None)
    in_specs = (rows,) * 5 + (flat, flat, slots, rows, slots) + (weights,) * 3
    out_specs = (rows,) * 4 + (flat, flat) + (weights,) * 3 + (slots,)
    return jax.shard_map(
        functools.partial(shards), mesh=fine, in_specs=in_specs, out_specs=out_specs, check_vma=False
    )
```

time: 750 us -> 175 us (0.23)
  the two profiles are of different devices: /device:TPU:2 before, /device:TPU:4 now
where the time goes in v1:
time: 175 us; the launch traced here: 173 us
  starting transfers between devices  69.8 us (40%)
  Pallas kernels  49.1 us (28%)
  waiting for transfers between devices  47.4 us (27%)
  other arithmetic  4.7 us (3%)
    all_to_all x6, starting transfers between devices, swap(): return lax.all_to_all(block, axes, split_axis=0, concat_axis=0, tiled=True)  44.1 us
    all_to_all x6, waiting for transfers between devices, swap(): return lax.all_to_all(block, axes, split_axis=0, concat_axis=0, tiled=True)  35.3 us
    ppermute x11, starting transfers between devices, across(): return lax.ppermute(block, axis, other)  25.7 us
    pallas_call x2, Pallas kernels, early(): call(functools.partial(attention_kernel, started), early_outs, flops=2000...  21.3 us
    ppermute x11, waiting for transfers between devices, across(): return lax.ppermute(block, axis, other)  12 us
    pallas_call x1, Pallas kernels, shards(): call(expert_kernel, [pltpu.HBM((groups, frames, width + LANES), BF)] + [p...  6.12 us
    pallas_call x1, Pallas kernels, shards(): call(late_kernel, [pltpu.HBM((frames, body + 2 * experts, tokens), BF)],...  4.09 us
    pallas_call x1, Pallas kernels, shards(): call(weight_grads_kernel, [pltpu.HBM((2, 3, hidden, width), BF)] * 2, in_...  4.08 us
  transfers between devices with their start and end apart: 17, of which 9 were waited for; matrix products, arithmetic and copies ran while one was open for 3% of the time, Pallas kernels for 19%

profile of v1, /device:TPU:4, one launch (start us, length us, event | category | flops | bytes accessed | tf_op | source)
XLA Modules:
  0.0 173.3 jit_solution(11914965080531504786)
XLA Ops:
  0.6 0.0 copy-start.8
  0.7 0.0 copy-start
  0.7 0.0 copy-start.7
  0.7 0.0 copy-start.12
  0.7 0.0 copy-start.13
  0.7 0.0 copy-start.1
  0.7 0.0 copy-start.9
  0.7 0.0 copy-start.3
  0.7 2.4 %shard_map.204 = bf16[16,160,128]{2,1,0:T(8,128)(2,1)} custom-call(bf16[1,128,1152]{2,1,0:T(8,128)(2,1)} %q_ref.3, bf16[1,128,1152]{2,1,0:T(8,128)(2,1)} %k_ref.1, bf16[1,128,1152]{2,1,0:T(8,128)(2,1)} %v_ref.1, s32[1,1,16]{2,1,0:T(1,128)} %bitcast.17, s32[1,1,16]{2,1,0:T(1,128)} %cnt_ref.3), custom_call_target="tpu_custom_call" | custom-call | flops 1000000 | bytes 2000000 | tf_op jit(solution)/shard_map/pallas_call | solution.py:437
  3.1 11.1 %all-to-all-start = ((bf16[16,160,128]{2,1,0:T(8,128)(2,1)}), bf16[16,160,128]{2,1,0:T(8,128)(2,1)S(1)}, u32[]{:S(2)}, u32[]{:S(2)}) async-start(bf16[16,160,128]{2,1,0:T(8,128)(2,1)} %shard_map.204), calls=%async_computation | async-start | bytes 1310720 | tf_op jit(solution)/shard_map/all_to_all | solution.py:397
  14.2 0.0 copy-done.12
  14.2 3.5 %collective-permute-start = (bf16[1,144,1152]{2,1,0:T(8,128)(2,1)S(1)}, bf16[1,144,1152]{2,1,0:T(8,128)(2,1)S(1)}, u32[]{:S(2)}, u32[]{:S(2)}) collective-permute-start(bf16[1,144,1152]{2,1,0:T(8,128)(2,1)S(1)} %copy-done.12), channel_id=1, source_target_pairs={{0,64},{64,0},{1,65},{65,1},{2,66},{66,2},{3,67},{67,3},{4,68},{68... | collective-permute-start | bytes 995336 | tf_op jit(solution)/shard_map/ppermute | solution.py:430
  17.7 1.9 %collective-permute-start.1 = (bf16[1,144,1152]{2,1,0:T(8,128)(2,1)S(1)}, bf16[1,144,1152]{2,1,0:T(8,128)(2,1)S(1)}, u32[]{:S(2)}, u32[]{:S(2)}) collective-permute-start(bf16[1,144,1152]{2,1,0:T(8,128)(2,1)S(1)} %copy-done.12), channel_id=1, source_target_pairs={{0,16},{16,0},{1,17},{17,1},{2,18},{18,2},{3,19},{19,3},{4,20},{20... | collective-permute-start | bytes 995336 | tf_op jit(solution)/shard_map/ppermute | solution.py:430
  19.6 0.0 copy-done.13
  19.6 2.4 %collective-permute-start.2 = (bf16[1,144,1152]{2,1,0:T(8,128)(2,1)S(1)}, bf16[1,144,1152]{2,1,0:T(8,128)(2,1)S(1)}, u32[]{:S(2)}, u32[]{:S(2)}) collective-permute-start(bf16[1,144,1152]{2,1,0:T(8,128)(2,1)S(1)} %copy-done.13), channel_id=1, source_target_pairs={{0,16},{16,0},{1,17},{17,1},{2,18},{18,2},{3,19},{19,3},{4,20},{20... | collective-permute-start | bytes 995336 | tf_op jit(solution)/shard_map/ppermute | solution.py:430
  22.1 0.0 copy-done.8
  22.1 0.0 copy-done
  22.1 0.0 copy-done.7
  22.1 1.2 shard_map.205
  23.3 2.0 %collective-permute-done.w_0.refs_6_ = bf16[1,144,1152]{2,1,0:T(8,128)(2,1)S(1)} collective-permute-done((bf16[1,144,1152]{2,1,0:T(8,128)(2,1)S(1)}, bf16[1,144,1152]{2,1,0:T(8,128)(2,1)S(1)}, u32[]{:S(2)}, u32[]{:S(2)}) %collective-permute-start) | collective-permute-done | bytes 331808 | tf_op jit(solution)/shard_map/ppermute | solution.py:430
  25.4 0.0 collective-permute-done.1.w_1.refs_3_
  25.4 0.0 collective-permute-done.2.w_2.refs_4_
  25.4 7.0 %all-to-all-done.got_ref.kv_in_ref = bf16[16,160,128]{2,1,0:T(8,128)(2,1)S(1)} async-done(((bf16[16,160,128]{2,1,0:T(8,128)(2,1)}), bf16[16,160,128]{2,1,0:T(8,128)(2,1)S(1)}, u32[]{:S(2)}, u32[]{:S(2)}) %all-to-all-start) | async-done | bytes 655392 | tf_op jit(solution)/shard_map/all_to_all | solution.py:397
  32.4 2.5 %shard_map.206 = (bf16[16,192,128]{2,1,0:T(8,128)(2,1)}, bf16[16,16,128]{2,1,0:T(8,128)(2,1)}, bf16[256,128]{1,0:T(8,128)(2,1)}) custom-call(bf16[16,160,128]{2,1,0:T(8,128)(2,1)S(1)} %all-to-all-done.got_ref.kv_in_ref, bf16[16,192,128]{2,1,0:T(8,128)(2,1)} %get-tuple-element.38._, ...), custom_call_target="tpu_custom_call", output_to_operand_aliasing={{0}: (1, {})} | custom-call | flops 1000000 | bytes 2000000 | tf_op jit(solution)/shard_map/pallas_call | solution.py:446
  35.0 4.9 %all-to-all-start.1 = ((bf16[16,192,128]{2,1,0:T(8,128)(2,1)}), bf16[16,192,128]{2,1,0:T(8,128)(2,1)S(1)}, u32[]{:S(2)}, u32[]{:S(2)}) async-start(bf16[16,192,128]{2,1,0:T(8,128)(2,1)} %get-tuple-element.39), calls=%async_computation.1 | async-start | bytes 1572864 | tf_op jit(solution)/shard_map/all_to_all | solution.py:397
  39.8 3.5 %collective-permute-start.3 = (bf16[1,144,1152]{2,1,0:T(8,128)(2,1)S(1)}, bf16[1,144,1152]{2,1,0:T(8,128)(2,1)S(1)}, u32[]{:S(2)}, u32[]{:S(2)}) collective-permute-start(bf16[1,144,1152]{2,1,0:T(8,128)(2,1)S(1)} %copy-done.13), channel_id=1, source_target_pairs={{0,64},{64,0},{1,65},{65,1},{2,66},{66,2},{3,67},{67,3},{4,68},{68... | collective-permute-start | bytes 995336 | tf_op jit(solution)/shard_map/ppermute | solution.py:430
  43.3 2.4 %collective-permute-start.4 = (bf16[1,144,1152]{2,1,0:T(8,128)(2,1)}, bf16[1,144,1152]{2,1,0:T(8,128)(2,1)}, u32[]{:S(2)}, u32[]{:S(2)}) collective-permute-start(bf16[1,144,1152]{2,1,0:T(8,128)(2,1)} %refs_2_.1), channel_id=1, source_target_pairs={{0,64},{64,0},{1,65},{65,1},{2,66},{66,2},{3,67},{67,3},{4,68},{68... | collective-permute-start | bytes 995336 | tf_op jit(solution)/shard_map/ppermute | solution.py:430
  45.7 1.9 %collective-permute-start.5 = (bf16[1,144,1152]{2,1,0:T(8,128)(2,1)}, bf16[1,144,1152]{2,1,0:T(8,128)(2,1)}, u32[]{:S(2)}, u32[]{:S(2)}) collective-permute-start(bf16[1,144,1152]{2,1,0:T(8,128)(2,1)} %refs_2_.1), channel_id=1, source_target_pairs={{0,16},{16,0},{1,17},{17,1},{2,18},{18,2},{3,19},{19,3},{4,20},{20... | collective-permute-start | bytes 995336 | tf_op jit(solution)/shard_map/ppermute | solution.py:430
  47.6 2.4 %collective-permute-start.6 = (bf16[1,144,1152]{2,1,0:T(8,128)(2,1)S(1)}, bf16[1,144,1152]{2,1,0:T(8,128)(2,1)}, u32[]{:S(2)}, u32[]{:S(2)}) collective-permute-start(bf16[1,144,1152]{2,1,0:T(8,128)(2,1)S(1)} %collective-permute-done.w_0.refs_6_), channel_id=1, source_target_pairs={{0,16},{16,0},{1,17},{17,1},{2,18},{18,2},{3,19},{19,3},{4,20},{20... | collective-permute-start | bytes 995336 | tf_op jit(solution)/shard_map/ppermute | solution.py:430
  50.0 2.4 %collective-permute-done.3.w_0.refs_7_ = bf16[1,144,1152]{2,1,0:T(8,128)(2,1)S(1)} collective-permute-done((bf16[1,144,1152]{2,1,0:T(8,128)(2,1)S(1)}, bf16[1,144,1152]{2,1,0:T(8,128)(2,1)S(1)}, u32[]{:S(2)}, u32[]{:S(2)}) %collective-permute-start.3) | collective-permute-done | bytes 331808 | tf_op jit(solution)/shard_map/ppermute | solution.py:430
  52.4 1.9 %collective-permute-start.7 = (bf16[1,144,1152]{2,1,0:T(8,128)(2,1)S(1)}, bf16[1,144,1152]{2,1,0:T(8,128)(2,1)}, u32[]{:S(2)}, u32[]{:S(2)}) collective-permute-start(bf16[1,144,1152]{2,1,0:T(8,128)(2,1)S(1)} %collective-permute-done.3.w_0.refs_7_), channel_id=1, source_target_pairs={{0,16},{16,0},{1,17},{17,1},{2,18},{18,2},{3,19},{19,3},{4,20},{20... | collective-permute-start | bytes 995336 | tf_op jit(solution)/shard_map/ppermute | solution.py:430
  54.4 3.7 %collective-permute-done.4.w_1.refs_8_ = bf16[1,144,1152]{2,1,0:T(8,128)(2,1)} collective-permute-done((bf16[1,144,1152]{2,1,0:T(8,128)(2,1)}, bf16[1,144,1152]{2,1,0:T(8,128)(2,1)}, u32[]{:S(2)}, u32[]{:S(2)}) %collective-permute-start.4) | collective-permute-done | bytes 331808 | tf_op jit(solution)/shard_map/ppermute | solution.py:430
  58.1 1.9 %collective-permute-start.8 = (bf16[1,144,1152]{2,1,0:T(8,128)(2,1)}, bf16[1,144,1152]{2,1,0:T(8,128)(2,1)}, u32[]{:S(2)}, u32[]{:S(2)}) collective-permute-start(bf16[1,144,1152]{2,1,0:T(8,128)(2,1)} %collective-permute-done.4.w_1.refs_8_), channel_id=1, source_target_pairs={{0,16},{16,0},{1,17},{17,1},{2,18},{18,2},{3,19},{19,3},{4,20},{20... | collective-permute-start | bytes 995336 | tf_op jit(solution)/shard_map/ppermute | solution.py:430
  60.0 0.8 all-to-all-done.1.got_ref.qg_ref
  60.8 1.1 shard_map.207
  61.9 10.1 %all-to-all-start.2 = ((bf16[8,16,2432]{2,1,0:T(8,128)(2,1)}), bf16[8,16,2432]{2,1,0:T(8,128)(2,1)S(1)}, u32[]{:S(2)}, u32[]{:S(2)}) async-start(bf16[8,16,2432]{2,1,0:T(8,128)(2,1)} %get-tuple-element.40), calls=%async_computation.2 | async-start | bytes 1245184 | tf_op jit(solution)/shard_map/all_to_all | solution.py:397
  72.0 12.2 %shard_map.208 = (bf16[16,112,128]{2,1,0:T(8,128)(2,1)}, f32[144,2048]{1,0:T(8,128)}) custom-call(bf16[16,160,128]{2,1,0:T(8,128)(2,1)S(1)} %all-to-all-done.got_ref.kv_in_ref, bf16[16,192,128]{2,1,0:T(8,128)(2,1)S(1)} %all-to-all-done.1.got_ref.qg_ref, f32[16,128]{1,0:T(8,128)} %get-tuple-element.41.refs_0_.inv_ref), custom_call_target="tpu_custom_call" | custom-call | flops 99999997952 | bytes 2000000 | tf_op jit(solution)/shard_map/pallas_call | solution.py:482
  84.2 0.0 collective-permute-done.5.refs_5_
  84.2 0.0 collective-permute-done.6.refs_9_
  84.2 0.0 collective-permute-done.7.refs_10_
  84.2 0.0 collective-permute-done.8.refs_11_
  84.3 6.0 %all-to-all-done.2.rows_ref = bf16[8,16,2432]{2,1,0:T(8,128)(2,1)S(1)} async-done(((bf16[8,16,2432]{2,1,0:T(8,128)(2,1)}), bf16[8,16,2432]{2,1,0:T(8,128)(2,1)S(1)}, u32[]{:S(2)}, u32[]{:S(2)}) %all-to-all-start.2) | async-done | bytes 622624 | tf_op jit(solution)/shard_map/all_to_all | solution.py:397
  90.2 6.1 %shard_map.209 = (bf16[8,16,1280]{2,1,0:T(8,128)(2,1)}, bf16[4,128,144]{2,1,0:T(8,128)(2,1)}, bf16[4,128,144]{2,1,0:T(8,128)(2,1)}, bf16[4,128,144]{2,1,0:T(8,128)(2,1)}) custom-call(bf16[8,16,2432]{2,1,0:T(8,128)(2,1)S(1)} %all-to-all-done.2.rows_ref, bf16[1,144,1152]{2,1,0:T(8,128)(2,1)} %refs_0_.1, bf16[1,144,1152]{2,1,0:T(8,128)(2,1)} %refs_1_.1, ...), custom_call_target="tpu_custom_call" | custom-call | flops 1000000 | bytes 2000000 | tf_op jit(solution)/shard_map/pallas_call | solution.py:502
  96.4 5.6 %all-to-all-start.3 = ((bf16[8,16,1280]{2,1,0:T(8,128)(2,1)}), bf16[8,16,1280]{2,1,0:T(8,128)(2,1)S(1)}, u32[]{:S(2)}, u32[]{:S(2)}) async-start(bf16[8,16,1280]{2,1,0:T(8,128)(2,1)} %get-tuple-element.43.refs_1_), calls=%async_computation.3 | async-start | bytes 655360 | tf_op jit(solution)/shard_map/all_to_all | solution.py:397
  101.9 9.1 %shard_map.210 = (bf16[16,112,128]{2,1,0:T(8,128)(2,1)}, f32[144,2048]{1,0:T(8,128)}) custom-call(bf16[16,160,128]{2,1,0:T(8,128)(2,1)S(1)} %all-to-all-done.got_ref.kv_in_ref, bf16[16,192,128]{2,1,0:T(8,128)(2,1)S(1)} %all-to-all-done.1.got_ref.qg_ref, bf16[16,112,128]{2,1,0:T(8,128)(2,1)} %get-tuple-element.45.refs_0_, ...), custom_call_target="tpu_custom_call", output_to_operand_aliasing={{0}: (2, {})} | custom-call | flops 60000002048 | bytes 2000000 | tf_op jit(solution)/shard_map/pallas_call | solution.py:482
  111.0 4.1 %shard_map.211 = (bf16[2,3,144,1152]{3,2,1,0:T(8,128)(2,1)}, bf16[2,3,144,1152]{3,2,1,0:T(8,128)(2,1)}) custom-call(bf16[8,16,2432]{2,1,0:T(8,128)(2,1)S(1)} %all-to-all-done.2.rows_ref, bf16[4,128,144]{2,1,0:T(8,128)(2,1)} %get-tuple-element.47.hidden_ref, bf16[4,128,144]{2,1,0:T(8,128)(2,1)} %get-tuple-element.48.gate_ref, ...), custom_call_target="tpu_custom_call" | custom-call | flops 1000000 | bytes 2000000 | tf_op jit(solution)/shard_map/pallas_call | solution.py:520
  115.1 0.0 all-to-all-done.3.got_ref
  115.1 0.0 copy-done.5
  115.1 2.4 %shard_map.212 = (bf16[16,112,128]{2,1,0:T(8,128)(2,1)}, f32[1,1,16]{2,1,0:T(1,128)}, bf16[2,3,144,1152]{3,2,1,0:T(8,128)(2,1)}) custom-call(bf16[8,16,1280]{2,1,0:T(8,128)(2,1)S(1)} %all-to-all-done.3.got_ref, f32[16,1152]{1,0:T(8,128)} %get-tuple-element.44.normed_ref, ...), custom_call_target="tpu_custom_call", output_to_operand_aliasing={{0}: (4, {}), {2}: (5, {})} | custom-call | flops 1000000 | bytes 2000000 | tf_op jit(solution)/shard_map/pallas_call | solution.py:525
  117.5 1.9 %collective-permute-start.9 = (bf16[2,3,144,1152]{3,2,1,0:T(8,128)(2,1)}, bf16[2,3,144,1152]{3,2,1,0:T(8,128)(2,1)S(1)}, u32[]{:S(2)}, u32[]{:S(2)}) collective-permute-start(bf16[2,3,144,1152]{3,2,1,0:T(8,128)(2,1)} %get-tuple-element.56), channel_id=1, source_target_pairs={{0,16},{16,0},{1,17},{17,1},{2,18},{18,2},{3,19},{19,3},{4,20},{20... | collective-permute-start | bytes 5971976 | tf_op jit(solution)/shard_map/ppermute | solution.py:430
  119.4 7.9 %all-to-all-start.4 = ((bf16[16,112,128]{2,1,0:T(8,128)(2,1)}), bf16[16,112,128]{2,1,0:T(8,128)(2,1)S(1)}, u32[]{:S(2)}, u32[]{:S(2)}) async-start(bf16[16,112,128]{2,1,0:T(8,128)(2,1)} %get-tuple-element.52), calls=%async_computation.4 | async-start | bytes 917504 | tf_op jit(solution)/shard_map/all_to_all | solution.py:397
  127.3 0.0 collective-permute-done.9
  127.3 0.0 copy-start.11
  127.3 1.3 copy-done.11
  128.6 1.7 %fusion.near = bf16[3,144,1152]{2,1,0:T(8,128)(2,1)S(1)} fusion(bf16[2,3,144,1152]{3,2,1,0:T(8,128)(2,1)} %copy-done.11, bf16[2,3,144,1152]{3,2,1,0:T(8,128)(2,1)} %get-tuple-element.55), kind=kLoop, calls=%fused_computation.1 | loop fusion | flops 1990656 | bytes 2985984 | tf_op jit(solution)/shard_map/convert_element_type | solution.py:550
  130.4 1.9 %collective-permute-start.10 = (bf16[3,144,1152]{2,1,0:T(8,128)(2,1)S(1)}, bf16[3,144,1152]{2,1,0:T(8,128)(2,1)}, u32[]{:S(2)}, u32[]{:S(2)}) collective-permute-start(bf16[3,144,1152]{2,1,0:T(8,128)(2,1)S(1)} %fusion.near), channel_id=1, source_target_pairs={{0,64},{64,0},{1,65},{65,1},{2,66},{66,2},{3,67},{67,3},{4,68},{68... | collective-permute-start | bytes 2985992 | tf_op jit(solution)/shard_map/ppermute | solution.py:430
  132.3 9.8 %all-to-all-done.4.got_ref = bf16[16,112,128]{2,1,0:T(8,128)(2,1)S(1)} async-done(((bf16[16,112,128]{2,1,0:T(8,128)(2,1)}), bf16[16,112,128]{2,1,0:T(8,128)(2,1)S(1)}, u32[]{:S(2)}, u32[]{:S(2)}) %all-to-all-start.4) | async-done | bytes 458784 | tf_op jit(solution)/shard_map/all_to_all | solution.py:397
  142.1 4.1 %shard_map.213 = bf16[16,176,128]{2,1,0:T(8,128)(2,1)} custom-call(bf16[16,112,128]{2,1,0:T(8,128)(2,1)S(1)} %all-to-all-done.4.got_ref, bf16[16,160,128]{2,1,0:T(8,128)(2,1)S(1)} %all-to-all-done.got_ref.kv_in_ref, bf16[256,128]{1,0:T(8,128)(2,1)} %get-tuple-element.53.query_ref, bf16[16,16,128]{2,1,0:T(8,128)(2,1)} %get-tuple-element.54.att_ref, ...), custom_call_target="tpu_custom_call" | custom-call | flops 1000000 | bytes 2000000 | tf_op jit(solution)/shard_map/pallas_call | solution.py:560
  146.2 4.7 %all-to-all-start.5 = ((bf16[16,176,128]{2,1,0:T(8,128)(2,1)}), bf16[16,176,128]{2,1,0:T(8,128)(2,1)S(1)}, u32[]{:S(2)}, u32[]{:S(2)}) async-start(bf16[16,176,128]{2,1,0:T(8,128)(2,1)} %shard_map.213), calls=%async_computation.5 | async-start | bytes 1441792 | tf_op jit(solution)/shard_map/all_to_all | solution.py:397
  150.9 1.7 %shard_map.214 = (bf16[1,128,1152]{2,1,0:T(8,128)(2,1)}, bf16[128,1152]{1,0:T(8,128)(2,1)}) custom-call(bf16[16,112,128]{2,1,0:T(8,128)(2,1)S(1)} %all-to-all-done.4.got_ref, bf16[1,128,1152]{2,1,0:T(8,128)(2,1)S(1)} %copy-done.2, bf16[16,128]{1,0:T(8,128)(2,1)} %get-tuple-element.57.sel_ref), custom_call_target="tpu_custom_call" | custom-call | flops 1000000 | bytes 2000000 | tf_op jit(solution)/shard_map/pallas_call | solution.py:572
  152.7 3.8 %collective-permute-done.10 = bf16[3,144,1152]{2,1,0:T(8,128)(2,1)} collective-permute-done((bf16[3,144,1152]{2,1,0:T(8,128)(2,1)S(1)}, bf16[3,144,1152]{2,1,0:T(8,128)(2,1)}, u32[]{:S(2)}, u32[]{:S(2)}) %collective-permute-start.10) | collective-permute-done | bytes 995360 | tf_op jit(solution)/shard_map/ppermute | solution.py:430
  156.5 3.0 %fusion.1 = (bf16[1,144,1152]{2,1,0:T(8,128)(2,1)}, bf16[1,144,1152]{2,1,0:T(8,128)(2,1)}, bf16[1,144,1152]{2,1,0:T(8,128)(2,1)}) fusion(bf16[3,144,1152]{2,1,0:T(8,128)(2,1)} %collective-permute-done.10, bf16[2,3,144,1152]{3,2,1,0:T(8,128)(2,1)} %copy-done.11, bf16[2,3,144,1152]{3,2,1,0:T(8,128)(2,1)} %get-tuple-element.55), kind=kLoop, calls=%fused_computation.3 | loop fusion | flops 2985984 | bytes 3981312 | tf_op jit(solution)/shard_map/convert_element_type | solution.py:553
  159.5 11.7 %all-to-all-done.5.got_ref = bf16[16,176,128]{2,1,0:T(8,128)(2,1)S(1)} async-done(((bf16[16,176,128]{2,1,0:T(8,128)(2,1)}), bf16[16,176,128]{2,1,0:T(8,128)(2,1)S(1)}, u32[]{:S(2)}, u32[]{:S(2)}) %all-to-all-start.5) | async-done | bytes 720928 | tf_op jit(solution)/shard_map/all_to_all | solution.py:397
  171.1 2.1 %shard_map.215 = (bf16[1,128,1152]{2,1,0:T(8,128)(2,1)}, bf16[1,128,1152]{2,1,0:T(8,128)(2,1)}, bf16[1,128,1152]{2,1,0:T(8,128)(2,1)}, f32[1,1152]{1,0:T(1,128)}, f32[1,1152]{1,0:T(1,128)}) custom-call(bf16[16,176,128]{2,1,0:T(8,128)(2,1)S(1)} %all-to-all-done.5.got_ref, bf16[128,1152]{1,0:T(8,128)(2,1)} %get-tuple-element.58.early_ref, ...), custom_call_target="tpu_custom_call" | custom-call | flops 1000000 | bytes 2000000 | tf_op jit(solution)/shard_map/pallas_call | solution.py:575
  (12 shorter events, 0.0 us)
Async XLA Ops:
  0.6 21.4 %copy-start.8 = (s32[1,1,16]{2,1,0:T(1,128)S(1)}, s32[1,1,16]{2,1,0:T(1,128)}, u32[]{:S(2)}) copy-start(s32[1,1,16]{2,1,0:T(1,128)} %cnt_ref.3) | copy-start | bytes 196
  0.7 21.4 %copy-start = (bf16[1,128,1152]{2,1,0:T(8,128)(2,1)S(1)}, bf16[1,128,1152]{2,1,0:T(8,128)(2,1)}, u32[]{:S(2)}) copy-start(bf16[1,128,1152]{2,1,0:T(8,128)(2,1)} %q_ref.3) | copy-start | bytes 884740
  0.7 21.4 %copy-start.7 = (s32[1,1,16,1]{2,3,1,0:T(1,128)S(1)}, s32[1,1,16,1]{2,3,1,0:T(1,128)}, u32[]{:S(2)}) copy-start(s32[1,1,16,1]{2,3,1,0:T(1,128)} %param.20) | copy-start | bytes 196
  0.7 13.5 %copy-start.12 = (bf16[1,144,1152]{2,1,0:T(8,128)(2,1)S(1)}, bf16[1,144,1152]{2,1,0:T(8,128)(2,1)}, u32[]{:S(2)}) copy-start(bf16[1,144,1152]{2,1,0:T(8,128)(2,1)} %refs_0_.1) | copy-start | bytes 995332
  0.7 18.9 %copy-start.13 = (bf16[1,144,1152]{2,1,0:T(8,128)(2,1)S(1)}, bf16[1,144,1152]{2,1,0:T(8,128)(2,1)}, u32[]{:S(2)}) copy-start(bf16[1,144,1152]{2,1,0:T(8,128)(2,1)} %refs_1_.1) | copy-start | bytes 995332
  0.7 21.4 %copy-start.1 = (bf16[1,128,1152]{2,1,0:T(8,128)(2,1)S(1)}, bf16[1,128,1152]{2,1,0:T(8,128)(2,1)}, u32[]{:S(2)}) copy-start(bf16[1,128,1152]{2,1,0:T(8,128)(2,1)} %g_ref.3) | copy-start | bytes 884740
  0.7 21.4 %copy-start.9 = (bf16[1,1,16,1]{2,3,1,0:T(2,128)(2,1)S(1)}, bf16[1,1,16,1]{2,3,1,0:T(2,128)(2,1)}, u32[]{:S(2)}) copy-start(bf16[1,1,16,1]{2,3,1,0:T(2,128)(2,1)} %param.22) | copy-start | bytes 100
  0.7 21.4 %copy-start.3 = (bf16[1,128,1152]{2,1,0:T(8,128)(2,1)S(1)}, bf16[1,128,1152]{2,1,0:T(8,128)(2,1)}, u32[]{:S(2)}) copy-start(bf16[1,128,1152]{2,1,0:T(8,128)(2,1)} %x_ref.1) | copy-start | bytes 884740
  3.1 29.3 %all-to-all-start = ((bf16[16,160,128]{2,1,0:T(8,128)(2,1)}), bf16[16,160,128]{2,1,0:T(8,128)(2,1)S(1)}, u32[]{:S(2)}, u32[]{:S(2)}) async-start(bf16[16,160,128]{2,1,0:T(8,128)(2,1)} %shard_map.204), calls=%async_computation | async-start | bytes 1310720 | tf_op jit(solution)/shard_map/all_to_all | solution.py:397
  14.2 11.2 %collective-permute-start = (bf16[1,144,1152]{2,1,0:T(8,128)(2,1)S(1)}, bf16[1,144,1152]{2,1,0:T(8,128)(2,1)S(1)}, u32[]{:S(2)}, u32[]{:S(2)}) collective-permute-start(bf16[1,144,1152]{2,1,0:T(8,128)(2,1)S(1)} %copy-done.12), channel_id=1, source_target_pairs={{0,64},{64,0},{1,65},{65,1},{2,66},{66,2},{3,67},{67,3},{4,68},{68... | collective-permute-start | bytes 995336 | tf_op jit(solution)/shard_map/ppermute | solution.py:430
  17.7 7.7 %collective-permute-start.1 = (bf16[1,144,1152]{2,1,0:T(8,128)(2,1)S(1)}, bf16[1,144,1152]{2,1,0:T(8,128)(2,1)S(1)}, u32[]{:S(2)}, u32[]{:S(2)}) collective-permute-start(bf16[1,144,1152]{2,1,0:T(8,128)(2,1)S(1)} %copy-done.12), channel_id=1, source_target_pairs={{0,16},{16,0},{1,17},{17,1},{2,18},{18,2},{3,19},{19,3},{4,20},{20... | collective-permute-start | bytes 995336 | tf_op jit(solution)/shard_map/ppermute | solution.py:430
  19.6 5.7 %collective-permute-start.2 = (bf16[1,144,1152]{2,1,0:T(8,128)(2,1)S(1)}, bf16[1,144,1152]{2,1,0:T(8,128)(2,1)S(1)}, u32[]{:S(2)}, u32[]{:S(2)}) collective-permute-start(bf16[1,144,1152]{2,1,0:T(8,128)(2,1)S(1)} %copy-done.13), channel_id=1, source_target_pairs={{0,16},{16,0},{1,17},{17,1},{2,18},{18,2},{3,19},{19,3},{4,20},{20... | collective-permute-start | bytes 995336 | tf_op jit(solution)/shard_map/ppermute | solution.py:430
  32.4 28.4 %copy-start.4 = (f32[1,1152]{1,0:T(1,128)S(1)}, f32[1,1152]{1,0:T(1,128)}, u32[]{:S(2)}) copy-start(f32[1,1152]{1,0:T(1,128)} %scale_ref.3) | copy-start | bytes 13828
  32.4 28.4 %copy-start.6 = (f32[1,1152]{1,0:T(1,128)S(1)}, f32[1,1152]{1,0:T(1,128)}, u32[]{:S(2)}) copy-start(f32[1,1152]{1,0:T(1,128)} %shift_ref.1) | copy-start | bytes 13828
  35.0 25.9 %all-to-all-start.1 = ((bf16[16,192,128]{2,1,0:T(8,128)(2,1)}), bf16[16,192,128]{2,1,0:T(8,128)(2,1)S(1)}, u32[]{:S(2)}, u32[]{:S(2)}) async-start(bf16[16,192,128]{2,1,0:T(8,128)(2,1)} %get-tuple-element.39), calls=%async_computation.1 | async-start | bytes 1572864 | tf_op jit(solution)/shard_map/all_to_all | solution.py:397
  39.8 12.6 %collective-permute-start.3 = (bf16[1,144,1152]{2,1,0:T(8,128)(2,1)S(1)}, bf16[1,144,1152]{2,1,0:T(8,128)(2,1)S(1)}, u32[]{:S(2)}, u32[]{:S(2)}) collective-permute-start(bf16[1,144,1152]{2,1,0:T(8,128)(2,1)S(1)} %copy-done.13), channel_id=1, source_target_pairs={{0,64},{64,0},{1,65},{65,1},{2,66},{66,2},{3,67},{67,3},{4,68},{68... | collective-permute-start | bytes 995336 | tf_op jit(solution)/shard_map/ppermute | solution.py:430
  43.3 14.8 %collective-permute-start.4 = (bf16[1,144,1152]{2,1,0:T(8,128)(2,1)}, bf16[1,144,1152]{2,1,0:T(8,128)(2,1)}, u32[]{:S(2)}, u32[]{:S(2)}) collective-permute-start(bf16[1,144,1152]{2,1,0:T(8,128)(2,1)} %refs_2_.1), channel_id=1, source_target_pairs={{0,64},{64,0},{1,65},{65,1},{2,66},{66,2},{3,67},{67,3},{4,68},{68... | collective-permute-start | bytes 995336 | tf_op jit(solution)/shard_map/ppermute | solution.py:430
  45.7 38.5 %collective-permute-start.5 = (bf16[1,144,1152]{2,1,0:T(8,128)(2,1)}, bf16[1,144,1152]{2,1,0:T(8,128)(2,1)}, u32[]{:S(2)}, u32[]{:S(2)}) collective-permute-start(bf16[1,144,1152]{2,1,0:T(8,128)(2,1)} %refs_2_.1), channel_id=1, source_target_pairs={{0,16},{16,0},{1,17},{17,1},{2,18},{18,2},{3,19},{19,3},{4,20},{20... | collective-permute-start | bytes 995336 | tf_op jit(solution)/shard_map/ppermute | solution.py:430
  47.6 36.6 %collective-permute-start.6 = (bf16[1,144,1152]{2,1,0:T(8,128)(2,1)S(1)}, bf16[1,144,1152]{2,1,0:T(8,128)(2,1)}, u32[]{:S(2)}, u32[]{:S(2)}) collective-permute-start(bf16[1,144,1152]{2,1,0:T(8,128)(2,1)S(1)} %collective-permute-done.w_0.refs_6_), channel_id=1, source_target_pairs={{0,16},{16,0},{1,17},{17,1},{2,18},{18,2},{3,19},{19,3},{4,20},{20... | collective-permute-start | bytes 995336 | tf_op jit(solution)/shard_map/ppermute | solution.py:430
  52.4 31.8 %collective-permute-start.7 = (bf16[1,144,1152]{2,1,0:T(8,128)(2,1)S(1)}, bf16[1,144,1152]{2,1,0:T(8,128)(2,1)}, u32[]{:S(2)}, u32[]{:S(2)}) collective-permute-start(bf16[1,144,1152]{2,1,0:T(8,128)(2,1)S(1)} %collective-permute-done.3.w_0.refs_7_), channel_id=1, source_target_pairs={{0,16},{16,0},{1,17},{17,1},{2,18},{18,2},{3,19},{19,3},{4,20},{20... | collective-permute-start | bytes 995336 | tf_op jit(solution)/shard_map/ppermute | solution.py:430
  58.1 26.1 %collective-permute-start.8 = (bf16[1,144,1152]{2,1,0:T(8,128)(2,1)}, bf16[1,144,1152]{2,1,0:T(8,128)(2,1)}, u32[]{:S(2)}, u32[]{:S(2)}) collective-permute-start(bf16[1,144,1152]{2,1,0:T(8,128)(2,1)} %collective-permute-done.4.w_1.refs_8_), channel_id=1, source_target_pairs={{0,16},{16,0},{1,17},{17,1},{2,18},{18,2},{3,19},{19,3},{4,20},{20... | collective-permute-start | bytes 995336 | tf_op jit(solution)/shard_map/ppermute | solution.py:430
  61.9 28.3 %all-to-all-start.2 = ((bf16[8,16,2432]{2,1,0:T(8,128)(2,1)}), bf16[8,16,2432]{2,1,0:T(8,128)(2,1)S(1)}, u32[]{:S(2)}, u32[]{:S(2)}) async-start(bf16[8,16,2432]{2,1,0:T(8,128)(2,1)} %get-tuple-element.40), calls=%async_computation.2 | async-start | bytes 1245184 | tf_op jit(solution)/shard_map/all_to_all | solution.py:397
  96.4 18.7 %all-to-all-start.3 = ((bf16[8,16,1280]{2,1,0:T(8,128)(2,1)}), bf16[8,16,1280]{2,1,0:T(8,128)(2,1)S(1)}, u32[]{:S(2)}, u32[]{:S(2)}) async-start(bf16[8,16,1280]{2,1,0:T(8,128)(2,1)} %get-tuple-element.43.refs_1_), calls=%async_computation.3 | async-start | bytes 655360 | tf_op jit(solution)/shard_map/all_to_all | solution.py:397
  111.0 4.1 %copy-start.5 = (f32[1,1152]{1,0:T(1,128)S(1)}, f32[1,1152]{1,0:T(1,128)}, u32[]{:S(2)}) copy-start(f32[1,1152]{1,0:T(1,128)} %scale_ref.3) | copy-start | bytes 13828
  117.5 9.8 %collective-permute-start.9 = (bf16[2,3,144,1152]{3,2,1,0:T(8,128)(2,1)}, bf16[2,3,144,1152]{3,2,1,0:T(8,128)(2,1)S(1)}, u32[]{:S(2)}, u32[]{:S(2)}) collective-permute-start(bf16[2,3,144,1152]{3,2,1,0:T(8,128)(2,1)} %get-tuple-element.56), channel_id=1, source_target_pairs={{0,16},{16,0},{1,17},{17,1},{2,18},{18,2},{3,19},{19,3},{4,20},{20... | collective-permute-start | bytes 5971976 | tf_op jit(solution)/shard_map/ppermute | solution.py:430
  119.4 22.7 %all-to-all-start.4 = ((bf16[16,112,128]{2,1,0:T(8,128)(2,1)}), bf16[16,112,128]{2,1,0:T(8,128)(2,1)S(1)}, u32[]{:S(2)}, u32[]{:S(2)}) async-start(bf16[16,112,128]{2,1,0:T(8,128)(2,1)} %get-tuple-element.52), calls=%async_computation.4 | async-start | bytes 917504 | tf_op jit(solution)/shard_map/all_to_all | solution.py:397
  127.3 1.3 copy-start.11
  130.3 11.8 %copy-start.10 = (bf16[3,144,1152]{2,1,0:T(8,128)(2,1)}, bf16[3,144,1152]{2,1,0:T(8,128)(2,1)S(1)}, u32[]{:S(2)}) copy-start(bf16[3,144,1152]{2,1,0:T(8,128)(2,1)S(1)} %fusion.near) | copy-start | bytes 2985988
  130.4 26.1 %collective-permute-start.10 = (bf16[3,144,1152]{2,1,0:T(8,128)(2,1)S(1)}, bf16[3,144,1152]{2,1,0:T(8,128)(2,1)}, u32[]{:S(2)}, u32[]{:S(2)}) collective-permute-start(bf16[3,144,1152]{2,1,0:T(8,128)(2,1)S(1)} %fusion.near), channel_id=1, source_target_pairs={{0,64},{64,0},{1,65},{65,1},{2,66},{66,2},{3,67},{67,3},{4,68},{68... | collective-permute-start | bytes 2985992 | tf_op jit(solution)/shard_map/ppermute | solution.py:430
  142.1 8.8 %copy-start.2 = (bf16[1,128,1152]{2,1,0:T(8,128)(2,1)S(1)}, bf16[1,128,1152]{2,1,0:T(8,128)(2,1)}, u32[]{:S(2)}) copy-start(bf16[1,128,1152]{2,1,0:T(8,128)(2,1)} %g_ref.3) | copy-start | bytes 884740
  146.2 24.9 %all-to-all-start.5 = ((bf16[16,176,128]{2,1,0:T(8,128)(2,1)}), bf16[16,176,128]{2,1,0:T(8,128)(2,1)S(1)}, u32[]{:S(2)}, u32[]{:S(2)}) async-start(bf16[16,176,128]{2,1,0:T(8,128)(2,1)} %shard_map.213), calls=%async_computation.5 | async-start | bytes 1441792 | tf_op jit(solution)/shard_map/all_to_all | solution.py:397

commit v2 on v1

--- a/solution.py
+++ b/solution.py
@@ -124,7 +124,7 @@
     query_t = q_ref[0].astype(F32).T
     grad_t = g_ref[0].astype(F32).T
     used = 2 * (width // LANES) + 1
-    blank = jnp.zeros((2 * experts - used, LANES), F32)
+    blank = jnp.zeros((sent_ref.shape[1] - experts - 2 * HEAD - used, LANES), F32)
     for h in range(width // HEAD):
         part = slice(h * HEAD, (h + 1) * HEAD)
         block = jnp.concatenate(
@@ -150,7 +150,7 @@
 
 
 def slot_forward_kernel(
-    got_ref, _, w_0, w_1, w_2, next_ref, out_ref, query_ref, kv_ref, sem
+    got_ref, _, w_0, w_1, w_2, w_3, next_ref, out_ref, query_ref, kv_ref, sem
 ):
     frames, rows = got_ref.shape[:2]
     experts = rows - 2 * HEAD
@@ -180,7 +180,7 @@
     )
 
 
-def norm_kernel(got_ref, shift_ref, scale_ref, w_0, w_1, sent_ref, normed_ref, inv_ref):
+def norm_kernel(got_ref, shift_ref, scale_ref, w_0, sent_ref, normed_ref, inv_ref):
     frames = got_ref.shape[0]
     width = shift_ref.shape[1]
     depth = width // LANES
@@ -213,7 +213,7 @@
     weights, (early, back_ref, hidden_ref, gate_ref, up_ref, held, sems) = refs[:-7], refs[-7:]
     copies = [
         pltpu.make_async_copy(ref.at[0], held.at[i], sems.at[i])
-        for i, ref in enumerate(weights[:3])
+        for i, ref in enumerate(weights[:6])
     ]
     for copy in copies:
         copy.start()
@@ -222,25 +222,29 @@
     total, width = rows.shape
     back = jnp.zeros((total, width), F32)
     gate_part = jnp.zeros((total, 1), F32)
-    for part in (1, 2, 3, 0):
-        if part == 0:
-            for copy in copies:
+    for part in (2, 3, 0, 1):
+        if part < 2:
+            for copy in copies[3 * part : 3 * part + 3]:
                 copy.wait()
-            gate_w, up_w, down_w = (held[i] for i in range(3))
+            gate_w, up_w, down_w = (held[3 * part + i] for i in range(3))
         else:
-            gate_w, up_w, down_w = (ref[0] for ref in weights[3 * part : 3 * part + 3])
+            first, second = weights[2 * part + 2 : 2 * part + 4]
+            hidden = held.shape[1]
+            kept = first.shape[0] - hidden
+            gate_w, down_w = first[0:hidden, :], second[hidden - kept :, :]
+            up_w = jnp.concatenate([first[hidden:, :], second[0 : hidden - kept, :]], axis=0)
         gate_pre = mm(rows, gate_w, NT)
         up_pre = mm(rows, up_w, NT)
         back_hidden = mm(grads, down_w, NT)
         sig = jax.nn.sigmoid(gate_pre)
         silu = gate_pre * sig
-        hidden = (silu * up_pre).astype(BF)
-        gate_part += jnp.sum(hidden.astype(F32) * back_hidden, axis=1, keepdims=True)
+        active = (silu * up_pre).astype(BF)
+        gate_part += jnp.sum(active.astype(F32) * back_hidden, axis=1, keepdims=True)
         hidden_grad = gates * back_hidden
         gate_delta = (hidden_grad * up_pre * sig * (1.0 + gate_pre * (1.0 - sig))).astype(BF)
         up_delta = (hidden_grad * silu).astype(BF)
         back += mm(gate_delta, gate_w, NN) + mm(up_delta, up_w, NN)
-        hidden_ref[part] = hidden
+        hidden_ref[part] = active
         gate_ref[part] = gate_delta
         up_ref[part] = up_delta
     lane = iota((total, LANES), 1)
@@ -318,10 +322,8 @@
     row_terms = jnp.sum(grad_f * attended, axis=1, keepdims=True)
     score_grad = (expo * (mm(grad, kv, NN) - row_terms)).astype(BF)
     dq_t = (mm(score_grad, kv, NT) * (inv * factor)).T
-    blank = jnp.zeros((dq_ref.shape[1] - 2 * frames - HEAD, LANES), F32)
     for i in range(dq_ref.shape[0]):
-        block = jnp.concatenate([dq_t[0:HEAD, i * LANES : (i + 1) * LANES], blank], axis=0)
-        dq_ref[i, 2 * frames :, :] = block.astype(BF)
+        dq_ref[i, 2 * frames :, :] = dq_t[0:HEAD, i * LANES : (i + 1) * LANES].astype(BF)
     scaled = (tall * jnp.where(lane < HEAD, inv * factor, inv)).T
     sums_ref[0:HEAD, :] += mm(scaled[0:HEAD].astype(BF), score_grad, NN)
     sums_ref[HEAD:, :] += mm(scaled[HEAD:].astype(BF), expo_b, NN)
@@ -348,7 +350,7 @@
     dk = mm(query_t, score_grad, NN)
     dv = mm(delta_t, expo.astype(BF), NN)
     both = sums_ref[...] + jnp.concatenate([dk, dv], axis=0)
-    dq = mm(slot_order(experts, frames), dq, NN).astype(BF)
+    dq = mm(slot_order(experts, frames), dq, NN)
     sums = got[0][frames : frames + 4]
     for block in got[1:]:
         sums = sums + block[frames : frames + 4]
@@ -356,13 +358,18 @@
     for part in (sums[0:1] + sums[1:2], sums[2:3] + sums[3:4]):
         high = part.astype(BF).astype(F32)
         parts += [high, part - high]
-    tail = jnp.concatenate(parts + [jnp.zeros((12, LANES), F32)], axis=0).astype(BF)
+    half = HEAD // 2
+    tail = jnp.concatenate(
+        [p[:, 0:half] for p in parts] + [p[:, half:HEAD] for p in parts], axis=0
+    )
+    tail = pad_lanes(
+        jnp.concatenate([tail, jnp.zeros((experts - 8, half), F32)], axis=0), LANES - HEAD
+    )
     body = 2 * HEAD
     for s in range(frames):
-        rows = slice(s * experts, (s + 1) * experts)
+        rows = dq[s * experts : (s + 1) * experts, 0:HEAD]
         sent_ref[s, 0:body, :] = both[:, s * LANES : (s + 1) * LANES].astype(BF)
-        sent_ref[s, body : body + experts, :] = dq[rows]
-        sent_ref[s, body + experts :, :] = tail
+        sent_ref[s, body:, :] = jnp.concatenate([rows, tail], axis=1).astype(BF)
 
 
 def inputs_kernel(got_ref, g_ref, sel_ref, di_ref, dq_ref):
@@ -373,7 +380,7 @@
     blocks = [got_ref[e, frames : 2 * frames, :].astype(F32)[4 : 4 + depth] for e in range(heads)]
     delta = unfold(blocks).astype(BF)
     di_ref[0] = (g_ref[0].astype(F32) + mm(sel_ref[...], delta, TN)).astype(BF)
-    parts = [got_ref[h, 2 * frames :, :].astype(F32)[0:HEAD] for h in range(heads)]
+    parts = [got_ref[h, 2 * frames :, :].astype(F32) for h in range(heads)]
     dq_ref[...] = jnp.concatenate(parts, axis=0).T.astype(BF)
 
 
@@ -384,10 +391,11 @@
     got = [got_ref[h, 0:body, :].astype(F32) for h in range(heads)]
     dk_ref[0] = jnp.concatenate([b[0:HEAD] for b in got], axis=0).T.astype(BF)
     dv_ref[0] = jnp.concatenate([b[HEAD:] for b in got], axis=0).T.astype(BF)
-    tails = [got_ref[h, body:, :].astype(F32)[:, :HEAD] for h in range(heads)]
-    tail = jnp.concatenate(tails, axis=1)
-    late = tail[0:experts].astype(BF)
-    sums = tail[experts:]
+    tails = [got_ref[h, body:, :].astype(F32) for h in range(heads)]
+    late = jnp.concatenate([t[:, :HEAD] for t in tails], axis=1).astype(BF)
+    half = HEAD // 2
+    halves = [t[0:8, HEAD : HEAD + half] for t in tails]
+    sums = jnp.concatenate([part for h in halves for part in (h[0:4], h[4:8])], axis=1)
     dq_ref[0] = (early_ref[...].astype(F32) + mm(sel_ref[...], late, TN)).astype(BF)
     sh_ref[...] = sums[0:1] + sums[1:2]
     sc_ref[...] = sums[2:3] + sums[3:4]
@@ -429,16 +437,18 @@
     def across(block, axis):
         return lax.ppermute(block, axis, other)
 
-    w_own = [w_gate, w_up, w_down]
-    w_near = [across(w, "yl") for w in w_own]
-    w_core = [across(w, "core") for w in w_own]
-    w_far = [across(w, "core") for w in w_near]
+    cut = hidden // 2 - 8
+    w_first = jnp.concatenate([w_gate[0], w_up[0, :cut]], axis=0)
+    w_second = jnp.concatenate([w_up[0, cut:], w_down[0]], axis=0)
+    near = [across(w_first, "yl"), across(w_second, "yl")]
+    core = [across(w, "core") for w in (w_gate, w_up, w_down)]
+    far = [across(w, "core") for w in near]
 
     (keys_sent,) = call(keys_kernel, [pltpu.HBM((heads, body + experts, tokens), BF)], mib=60)(
         queries, keys, values_in, slot_tokens, slot_counts
     )
     keys_got = swap(keys_sent, SEQ)
-    rows_next = experts + body + 2 * experts
+    rows_next = experts + body + 8 * (-(-(2 * (width // LANES) + 1) // 8))
     qg_sent, sel = call(
         queries_kernel, [pltpu.HBM((heads, rows_next, tokens), BF), pltpu.HBM((experts, tokens), BF)]
     )(queries, out_grad, inputs_x, slot_tokens, slot_counts, gate_values)
@@ -450,7 +460,7 @@
             pltpu.HBM((experts, frames, LANES), BF),
             pltpu.HBM((total, LANES), BF),
         ],
-        in_specs=[whole(keys_got.shape)] + [ANY] * 4,
+        in_specs=[whole(keys_got.shape)] + [ANY] * 5,
         out_specs=[
             ANY,
             whole((experts, frames, LANES)),
@@ -458,7 +468,7 @@
         ],
         input_output_aliases={1: 0},
         scratch_shapes=[pltpu.VMEM((body, length), BF), pltpu.SemaphoreType.DMA],
-    )(keys_got, *hbm(qg_sent), w_near[0], w_core[0], w_core[1])
+    )(keys_got, *hbm(qg_sent), near[0], *core)
     qg_got = swap(qg_sent, SEQ)
 
     sent_width = 2 * width + LANES
@@ -469,13 +479,13 @@
             pltpu.HBM((frames, width), F32),
             pltpu.HBM((frames, LANES), F32),
         ],
-        in_specs=[whole(qg_got.shape), whole(shift.shape), whole(scale.shape)] + [ANY] * 2,
-    )(qg_got, shift, scale, w_near[1], w_near[2])
+        in_specs=[whole(qg_got.shape), whole(shift.shape), whole(scale.shape), ANY],
+    )(qg_got, shift, scale, near[1])
     rows_all = swap(rows_sent, ROWS)
 
     block = 2
-    first_steps = 5
-    rows_back = 2 * frames + HEAD + 8
+    first_steps = 6
+    rows_back = 2 * frames + HEAD
     early_outs = [pltpu.HBM((frames, rows_back, tokens), BF), pltpu.HBM((body, length), F32)]
 
     def early(started, steps, skip, extra, extra_specs, **kwargs):
@@ -503,9 +513,12 @@
         expert_kernel,
         [pltpu.HBM((groups, frames, width + LANES), BF)]
         + [pltpu.HBM((4, groups * frames, hidden), BF)] * 3,
-        in_specs=[whole(rows_all.shape)] + [HBM] * 3 + [whole(w_gate.shape)] * 9 + [ANY],
-        scratch_shapes=[pltpu.VMEM((3, hidden, width), BF), pltpu.SemaphoreType.DMA((3,))],
-    )(rows_all, *hbm(*w_own), *vmem(*w_core, *w_near, *w_far), *hbm(sums))
+        in_specs=[whole(rows_all.shape)]
+        + [HBM] * 6
+        + [whole(w_first.shape), whole(w_second.shape)] * 2
+        + [ANY],
+        scratch_shapes=[pltpu.VMEM((6, hidden, width), BF), pltpu.SemaphoreType.DMA((6,))],
+    )(rows_all, *hbm(w_gate, w_up, w_down, *core), *vmem(*near, *far), *hbm(sums))
     back_got = swap(back_sent, ROWS)
 
     back_next, sums = early(
@@ -547,8 +560,8 @@
     delta_got = swap(back_next, SEQ)
 
     got_core = across(others, "core")
-    near = (own[1].astype(F32) + got_core[1].astype(F32)).astype(BF)
-    got_near = across(near, "yl")
+    own_near = (own[1].astype(F32) + got_core[1].astype(F32)).astype(BF)
+    got_near = across(own_near, "yl")
     w_grads = [
         (own[0, i].astype(F32) + got_core[0, i].astype(F32) + got_near[i].astype(F32)).astype(BF)[
             None
@@ -559,13 +572,13 @@
 
     (late_sent,) = call(
         late_kernel,
-        [pltpu.HBM((frames, body + 2 * experts, tokens), BF)],
+        [pltpu.HBM((frames, body + experts, tokens), BF)],
         grid=(1,),
         in_specs=[whole((experts, 2 * frames, LANES))]
         + [whole(a.shape) for a in (keys_got, slot_query, att)]
         + [whole((body, length)), ANY],
-        out_specs=[whole((frames, body + 2 * experts, tokens))],
-    )(delta_got, keys_got, *hbm(slot_query, att, sums, near))
+        out_specs=[whole((frames, body + experts, tokens))],
+    )(delta_got, keys_got, *hbm(slot_query, att, sums, own_near))
     late_got = swap(late_sent, SEQ)
 
     block_shape = jax.ShapeDtypeStruct((1, tokens, width), BF)

time: 175 us -> 170 us (0.971)
  the two profiles are of different devices: /device:TPU:4 before, /device:TPU:16 now
where the time goes in v2:
time: 170 us; the launch traced here: 168 us
  starting transfers between devices  65.1 us (38%)
  Pallas kernels  49 us (29%)
  waiting for transfers between devices  44.6 us (26%)
  other arithmetic  6.46 us (4%)
  local copies, waits for them, and re-layouts  2.08 us (1%)
    all_to_all x6, starting transfers between devices, swap(): return lax.all_to_all(block, axes, split_axis=0, concat_axis=0, tiled=True)  44.2 us
    all_to_all x6, waiting for transfers between devices, swap(): return lax.all_to_all(block, axes, split_axis=0, concat_axis=0, tiled=True)  27.3 us
    pallas_call x2, Pallas kernels, early(): call(functools.partial(attention_kernel, started), early_outs, flops=2000...  21.3 us
    ppermute x9, starting transfers between devices, across(): return lax.ppermute(block, axis, other)  20.9 us
    ppermute x9, waiting for transfers between devices, across(): return lax.ppermute(block, axis, other)  17.3 us
    pallas_call x1, Pallas kernels, shards(): call(expert_kernel, [pltpu.HBM((groups, frames, width + LANES), BF)] + [p...  6.13 us
    pallas_call x1, Pallas kernels, shards(): call(weight_grads_kernel, [pltpu.HBM((2, 3, hidden, width), BF)] * 2, in_...  4.08 us
    pallas_call x1, Pallas kernels, shards(): call(late_kernel, [pltpu.HBM((frames, body + experts, tokens), BF)], grid...  4.01 us
  transfers between devices with their start and end apart: 15, of which 9 were waited for; matrix products, arithmetic and copies ran while one was open for 4% of the time, Pallas kernels for 20%

profile of v2, /device:TPU:16, one launch (start us, length us, event | category | flops | bytes accessed | tf_op | source)
XLA Modules:
  0.0 168.2 jit_solution(1209396024427803111)
XLA Ops:
  0.6 0.0 copy-start.14
  0.7 0.0 copy-start.3
  0.7 0.0 copy-start.5
  0.7 0.0 copy-start.6
  0.7 0.0 copy-start.9
  0.7 0.0 copy-start.10
  0.7 0.0 copy-start.11
  0.7 2.4 %shard_map.204 = bf16[16,160,128]{2,1,0:T(8,128)(2,1)} custom-call(bf16[1,128,1152]{2,1,0:T(8,128)(2,1)} %q_ref.3, bf16[1,128,1152]{2,1,0:T(8,128)(2,1)} %k_ref.1, bf16[1,128,1152]{2,1,0:T(8,128)(2,1)} %v_ref.1, s32[1,1,16]{2,1,0:T(1,128)} %bitcast.23, s32[1,1,16]{2,1,0:T(1,128)} %cnt_ref.3), custom_call_target="tpu_custom_call" | custom-call | flops 1000000 | bytes 2000000 | tf_op jit(solution)/shard_map/pallas_call | solution.py:447
  3.1 11.3 %all-to-all-start = ((bf16[16,160,128]{2,1,0:T(8,128)(2,1)}), bf16[16,160,128]{2,1,0:T(8,128)(2,1)S(1)}, u32[]{:S(2)}, u32[]{:S(2)}) async-start(bf16[16,160,128]{2,1,0:T(8,128)(2,1)} %shard_map.204), calls=%async_computation | async-start | bytes 1310720 | tf_op jit(solution)/shard_map/all_to_all | solution.py:405
  14.4 0.0 copy-done.14
  14.5 1.0 pad_maximum_fusion.1
  15.5 3.5 %collective-permute-start = (bf16[208,1152]{1,0:T(8,128)(2,1)S(1)}, bf16[208,1152]{1,0:T(8,128)(2,1)S(1)}, u32[]{:S(2)}, u32[]{:S(2)}) collective-permute-start(bf16[208,1152]{1,0:T(8,128)(2,1)S(1)} %pad_maximum_fusion.1), channel_id=1, source_target_pairs={{0,64},{64,0},{1,65},{65,1},{2,66},{66,2},{3,67},{67,3},{4,68},{68... | collective-permute-start | bytes 1437704 | tf_op jit(solution)/shard_map/ppermute | solution.py:438
  19.0 1.9 %collective-permute-start.1 = (bf16[1,144,1152]{2,1,0:T(8,128)(2,1)}, bf16[1,144,1152]{2,1,0:T(8,128)(2,1)S(1)}, u32[]{:S(2)}, u32[]{:S(2)}) collective-permute-start(bf16[1,144,1152]{2,1,0:T(8,128)(2,1)} %refs_0_.1), channel_id=1, source_target_pairs={{0,16},{16,0},{1,17},{17,1},{2,18},{18,2},{3,19},{19,3},{4,20},{20... | collective-permute-start | bytes 995336 | tf_op jit(solution)/shard_map/ppermute | solution.py:438
  20.9 2.4 %collective-permute-start.3 = (bf16[1,144,1152]{2,1,0:T(8,128)(2,1)}, bf16[1,144,1152]{2,1,0:T(8,128)(2,1)S(1)}, u32[]{:S(2)}, u32[]{:S(2)}) collective-permute-start(bf16[1,144,1152]{2,1,0:T(8,128)(2,1)} %refs_2_.1), channel_id=1, source_target_pairs={{0,16},{16,0},{1,17},{17,1},{2,18},{18,2},{3,19},{19,3},{4,20},{20... | collective-permute-start | bytes 995336 | tf_op jit(solution)/shard_map/ppermute | solution.py:438
  23.3 1.9 %collective-permute-start.2 = (bf16[1,144,1152]{2,1,0:T(8,128)(2,1)S(1)}, bf16[1,144,1152]{2,1,0:T(8,128)(2,1)S(1)}, u32[]{:S(2)}, u32[]{:S(2)}) collective-permute-start(bf16[1,144,1152]{2,1,0:T(8,128)(2,1)S(1)} %copy-done.14), channel_id=1, source_target_pairs={{0,16},{16,0},{1,17},{17,1},{2,18},{18,2},{3,19},{19,3},{4,20},{20... | collective-permute-start | bytes 995336 | tf_op jit(solution)/shard_map/ppermute | solution.py:438
  25.3 0.0 copy-done.3
  25.3 0.0 copy-done.5
  25.3 0.0 copy-done.6
  25.3 0.0 copy-done.9
  25.3 0.0 copy-done.10
  25.3 0.0 copy-done.11
  25.3 1.2 shard_map.205
  26.5 0.0 collective-permute-done.1.w_1.refs_3_
  26.5 0.0 collective-permute-done.3.w_3.refs_5_
  26.5 0.0 copy-start.1
  26.6 0.3 collective-permute-done.2.w_2.refs_4_
  26.9 2.9 %collective-permute-done.w_0.refs_6_ = bf16[208,1152]{1,0:T(8,128)(2,1)S(1)} collective-permute-done((bf16[208,1152]{1,0:T(8,128)(2,1)S(1)}, bf16[208,1152]{1,0:T(8,128)(2,1)S(1)}, u32[]{:S(2)}, u32[]{:S(2)}) %collective-permute-start) | collective-permute-done | bytes 479264 | tf_op jit(solution)/shard_map/ppermute | solution.py:438
  29.8 2.8 %all-to-all-done.got_ref.kv_in_ref = bf16[16,160,128]{2,1,0:T(8,128)(2,1)S(1)} async-done(((bf16[16,160,128]{2,1,0:T(8,128)(2,1)}), bf16[16,160,128]{2,1,0:T(8,128)(2,1)S(1)}, u32[]{:S(2)}, u32[]{:S(2)}) %all-to-all-start) | async-done | bytes 655392 | tf_op jit(solution)/shard_map/all_to_all | solution.py:405
  32.6 2.5 %shard_map.206 = (bf16[16,184,128]{2,1,0:T(8,128)(2,1)}, bf16[16,16,128]{2,1,0:T(8,128)(2,1)}, bf16[256,128]{1,0:T(8,128)(2,1)}) custom-call(bf16[16,160,128]{2,1,0:T(8,128)(2,1)S(1)} %all-to-all-done.got_ref.kv_in_ref, bf16[16,184,128]{2,1,0:T(8,128)(2,1)} %get-tuple-element.38._, ...), custom_call_target="tpu_custom_call", output_to_operand_aliasing={{0}: (1, {})} | custom-call | flops 1000000 | bytes 2000000 | tf_op jit(solution)/shard_map/pallas_call | solution.py:456
  35.2 0.0 copy-start.7
  35.2 5.0 %all-to-all-start.1 = ((bf16[16,184,128]{2,1,0:T(8,128)(2,1)}), bf16[16,184,128]{2,1,0:T(8,128)(2,1)S(1)}, u32[]{:S(2)}, u32[]{:S(2)}) async-start(bf16[16,184,128]{2,1,0:T(8,128)(2,1)} %get-tuple-element.39), calls=%async_computation.1 | async-start | bytes 1507328 | tf_op jit(solution)/shard_map/all_to_all | solution.py:405
  40.3 1.0 pad_maximum_fusion
  41.3 3.5 %collective-permute-start.4 = (bf16[224,1152]{1,0:T(8,128)(2,1)S(1)}, bf16[224,1152]{1,0:T(8,128)(2,1)S(1)}, u32[]{:S(2)}, u32[]{:S(2)}) collective-permute-start(bf16[224,1152]{1,0:T(8,128)(2,1)S(1)} %pad_maximum_fusion), channel_id=1, source_target_pairs={{0,64},{64,0},{1,65},{65,1},{2,66},{66,2},{3,67},{67,3},{4,68},{68... | collective-permute-start | bytes 1548296 | tf_op jit(solution)/shard_map/ppermute | solution.py:438
  44.8 1.9 %collective-permute-start.5 = (bf16[208,1152]{1,0:T(8,128)(2,1)S(1)}, bf16[208,1152]{1,0:T(8,128)(2,1)}, u32[]{:S(2)}, u32[]{:S(2)}) collective-permute-start(bf16[208,1152]{1,0:T(8,128)(2,1)S(1)} %collective-permute-done.w_0.refs_6_), channel_id=1, source_target_pairs={{0,16},{16,0},{1,17},{17,1},{2,18},{18,2},{3,19},{19,3},{4,20},{20... | collective-permute-start | bytes 1437704 | tf_op jit(solution)/shard_map/ppermute | solution.py:438
  46.7 9.5 %collective-permute-done.4.w_0.refs_7_ = bf16[224,1152]{1,0:T(8,128)(2,1)S(1)} collective-permute-done((bf16[224,1152]{1,0:T(8,128)(2,1)S(1)}, bf16[224,1152]{1,0:T(8,128)(2,1)S(1)}, u32[]{:S(2)}, u32[]{:S(2)}) %collective-permute-start.4) | collective-permute-done | bytes 516128 | tf_op jit(solution)/shard_map/ppermute | solution.py:438
  56.2 1.9 %collective-permute-start.6 = (bf16[224,1152]{1,0:T(8,128)(2,1)S(1)}, bf16[224,1152]{1,0:T(8,128)(2,1)S(1)}, u32[]{:S(2)}, u32[]{:S(2)}) collective-permute-start(bf16[224,1152]{1,0:T(8,128)(2,1)S(1)} %collective-permute-done.4.w_0.refs_7_), channel_id=1, source_target_pairs={{0,16},{16,0},{1,17},{17,1},{2,18},{18,2},{3,19},{19,3},{4,20},{20... | collective-permute-start | bytes 1548296 | tf_op jit(solution)/shard_map/ppermute | solution.py:438
  58.1 2.2 %all-to-all-done.1.got_ref.qg_ref = bf16[16,184,128]{2,1,0:T(8,128)(2,1)S(1)} async-done(((bf16[16,184,128]{2,1,0:T(8,128)(2,1)}), bf16[16,184,128]{2,1,0:T(8,128)(2,1)S(1)}, u32[]{:S(2)}, u32[]{:S(2)}) %all-to-all-start.1) | async-done | bytes 753696 | tf_op jit(solution)/shard_map/all_to_all | solution.py:405
  60.3 0.7 copy-done.8
  60.9 1.1 shard_map.207
  62.1 9.6 %all-to-all-start.2 = ((bf16[8,16,2432]{2,1,0:T(8,128)(2,1)}), bf16[8,16,2432]{2,1,0:T(8,128)(2,1)S(1)}, u32[]{:S(2)}, u32[]{:S(2)}) async-start(bf16[8,16,2432]{2,1,0:T(8,128)(2,1)} %get-tuple-element.40), calls=%async_computation.2 | async-start | bytes 1245184 | tf_op jit(solution)/shard_map/all_to_all | solution.py:405
  71.7 14.4 %shard_map.208 = (bf16[16,104,128]{2,1,0:T(8,128)(2,1)}, f32[144,2048]{1,0:T(8,128)}) custom-call(bf16[16,160,128]{2,1,0:T(8,128)(2,1)S(1)} %all-to-all-done.got_ref.kv_in_ref, bf16[16,184,128]{2,1,0:T(8,128)(2,1)S(1)} %all-to-all-done.1.got_ref.qg_ref, f32[16,128]{1,0:T(8,128)} %get-tuple-element.41.refs_0_.inv_ref), custom_call_target="tpu_custom_call" | custom-call | flops 120000004096 | bytes 2000000 | tf_op jit(solution)/shard_map/pallas_call | solution.py:492
  86.1 0.0 collective-permute-done.5.refs_8_
  86.1 0.0 collective-permute-done.6.refs_9_
  86.1 3.7 %all-to-all-done.2.rows_ref = bf16[8,16,2432]{2,1,0:T(8,128)(2,1)S(1)} async-done(((bf16[8,16,2432]{2,1,0:T(8,128)(2,1)}), bf16[8,16,2432]{2,1,0:T(8,128)(2,1)S(1)}, u32[]{:S(2)}, u32[]{:S(2)}) %all-to-all-start.2) | async-done | bytes 622624 | tf_op jit(solution)/shard_map/all_to_all | solution.py:405
  89.8 6.1 %shard_map.209 = (bf16[8,16,1280]{2,1,0:T(8,128)(2,1)}, bf16[4,128,144]{2,1,0:T(8,128)(2,1)}, bf16[4,128,144]{2,1,0:T(8,128)(2,1)}, bf16[4,128,144]{2,1,0:T(8,128)(2,1)}) custom-call(bf16[8,16,2432]{2,1,0:T(8,128)(2,1)S(1)} %all-to-all-done.2.rows_ref, bf16[1,144,1152]{2,1,0:T(8,128)(2,1)} %refs_0_.1, bf16[1,144,1152]{2,1,0:T(8,128)(2,1)} %refs_1_.1, ...), custom_call_target="tpu_custom_call" | custom-call | flops 1000000 | bytes 2000000 | tf_op jit(solution)/shard_map/pallas_call | solution.py:512
  96.0 6.0 %all-to-all-start.3 = ((bf16[8,16,1280]{2,1,0:T(8,128)(2,1)}), bf16[8,16,1280]{2,1,0:T(8,128)(2,1)S(1)}, u32[]{:S(2)}, u32[]{:S(2)}) async-start(bf16[8,16,1280]{2,1,0:T(8,128)(2,1)} %get-tuple-element.43.refs_1_), calls=%async_computation.3 | async-start | bytes 655360 | tf_op jit(solution)/shard_map/all_to_all | solution.py:405
  101.9 6.9 %shard_map.210 = (bf16[16,104,128]{2,1,0:T(8,128)(2,1)}, f32[144,2048]{1,0:T(8,128)}) custom-call(bf16[16,160,128]{2,1,0:T(8,128)(2,1)S(1)} %all-to-all-done.got_ref.kv_in_ref, bf16[16,184,128]{2,1,0:T(8,128)(2,1)S(1)} %all-to-all-done.1.got_ref.qg_ref, bf16[16,104,128]{2,1,0:T(8,128)(2,1)} %get-tuple-element.45.refs_0_, ...), custom_call_target="tpu_custom_call", output_to_operand_aliasing={{0}: (2, {})} | custom-call | flops 40000000000 | bytes 2000000 | tf_op jit(solution)/shard_map/pallas_call | solution.py:492
  108.8 4.1 %shard_map.211 = (bf16[2,3,144,1152]{3,2,1,0:T(8,128)(2,1)}, bf16[2,3,144,1152]{3,2,1,0:T(8,128)(2,1)}) custom-call(bf16[8,16,2432]{2,1,0:T(8,128)(2,1)S(1)} %all-to-all-done.2.rows_ref, bf16[4,128,144]{2,1,0:T(8,128)(2,1)} %get-tuple-element.47.hidden_ref, bf16[4,128,144]{2,1,0:T(8,128)(2,1)} %get-tuple-element.48.gate_ref, ...), custom_call_target="tpu_custom_call" | custom-call | flops 1000000 | bytes 2000000 | tf_op jit(solution)/shard_map/pallas_call | solution.py:533
  112.9 0.0 all-to-all-done.3.got_ref
  112.9 2.3 %shard_map.212 = (bf16[16,104,128]{2,1,0:T(8,128)(2,1)}, f32[1,1,16]{2,1,0:T(1,128)}, bf16[2,3,144,1152]{3,2,1,0:T(8,128)(2,1)}) custom-call(bf16[8,16,1280]{2,1,0:T(8,128)(2,1)S(1)} %all-to-all-done.3.got_ref, f32[16,1152]{1,0:T(8,128)} %get-tuple-element.44.normed_ref, ...), custom_call_target="tpu_custom_call", output_to_operand_aliasing={{0}: (4, {}), {2}: (5, {})} | custom-call | flops 1000000 | bytes 2000000 | tf_op jit(solution)/shard_map/pallas_call | solution.py:538
  115.2 1.9 %collective-permute-start.7 = (bf16[2,3,144,1152]{3,2,1,0:T(8,128)(2,1)}, bf16[2,3,144,1152]{3,2,1,0:T(8,128)(2,1)S(1)}, u32[]{:S(2)}, u32[]{:S(2)}) collective-permute-start(bf16[2,3,144,1152]{3,2,1,0:T(8,128)(2,1)} %get-tuple-element.56), channel_id=1, source_target_pairs={{0,16},{16,0},{1,17},{17,1},{2,18},{18,2},{3,19},{19,3},{4,20},{20... | collective-permute-start | bytes 5971976 | tf_op jit(solution)/shard_map/ppermute | solution.py:438
  117.2 7.6 %all-to-all-start.4 = ((bf16[16,104,128]{2,1,0:T(8,128)(2,1)}), bf16[16,104,128]{2,1,0:T(8,128)(2,1)S(1)}, u32[]{:S(2)}, u32[]{:S(2)}) async-start(bf16[16,104,128]{2,1,0:T(8,128)(2,1)} %get-tuple-element.52), calls=%async_computation.4 | async-start | bytes 851968 | tf_op jit(solution)/shard_map/all_to_all | solution.py:405
  124.8 0.0 collective-permute-done.7
  124.8 1.3 copy-done.13
  126.1 1.7 %fusion.near = bf16[3,144,1152]{2,1,0:T(8,128)(2,1)S(1)} fusion(bf16[2,3,144,1152]{3,2,1,0:T(8,128)(2,1)} %copy-done.13, bf16[2,3,144,1152]{3,2,1,0:T(8,128)(2,1)} %get-tuple-element.55), kind=kLoop, calls=%fused_computation.1 | loop fusion | flops 1990656 | bytes 2985984 | tf_op jit(solution)/shard_map/convert_element_type | solution.py:563
  127.9 1.9 %collective-permute-start.8 = (bf16[3,144,1152]{2,1,0:T(8,128)(2,1)S(1)}, bf16[3,144,1152]{2,1,0:T(8,128)(2,1)S(1)}, u32[]{:S(2)}, u32[]{:S(2)}) collective-permute-start(bf16[3,144,1152]{2,1,0:T(8,128)(2,1)S(1)} %fusion.near), channel_id=1, source_target_pairs={{0,64},{64,0},{1,65},{65,1},{2,66},{66,2},{3,67},{67,3},{4,68},{68... | collective-permute-start | bytes 2985992 | tf_op jit(solution)/shard_map/ppermute | solution.py:438
  129.8 9.2 %all-to-all-done.4.got_ref = bf16[16,104,128]{2,1,0:T(8,128)(2,1)S(1)} async-done(((bf16[16,104,128]{2,1,0:T(8,128)(2,1)}), bf16[16,104,128]{2,1,0:T(8,128)(2,1)S(1)}, u32[]{:S(2)}, u32[]{:S(2)}) %all-to-all-start.4) | async-done | bytes 426016 | tf_op jit(solution)/shard_map/all_to_all | solution.py:405
  139.0 4.0 %shard_map.213 = bf16[16,160,128]{2,1,0:T(8,128)(2,1)} custom-call(bf16[16,104,128]{2,1,0:T(8,128)(2,1)S(1)} %all-to-all-done.4.got_ref, bf16[16,160,128]{2,1,0:T(8,128)(2,1)S(1)} %all-to-all-done.got_ref.kv_in_ref, bf16[256,128]{1,0:T(8,128)(2,1)} %get-tuple-element.53.query_ref, bf16[16,16,128]{2,1,0:T(8,128)(2,1)} %get-tuple-element.54.att_ref, ...), custom_call_target="tpu_custom_call" | custom-call | flops 1000000 | bytes 2000000 | tf_op jit(solution)/shard_map/pallas_call | solution.py:573
  143.0 4.6 %all-to-all-start.5 = ((bf16[16,160,128]{2,1,0:T(8,128)(2,1)}), bf16[16,160,128]{2,1,0:T(8,128)(2,1)S(1)}, u32[]{:S(2)}, u32[]{:S(2)}) async-start(bf16[16,160,128]{2,1,0:T(8,128)(2,1)} %shard_map.213), calls=%async_computation.5 | async-start | bytes 1310720 | tf_op jit(solution)/shard_map/all_to_all | solution.py:405
  147.6 1.7 %shard_map.214 = (bf16[1,128,1152]{2,1,0:T(8,128)(2,1)}, bf16[128,1152]{1,0:T(8,128)(2,1)}) custom-call(bf16[16,104,128]{2,1,0:T(8,128)(2,1)S(1)} %all-to-all-done.4.got_ref, bf16[1,128,1152]{2,1,0:T(8,128)(2,1)S(1)} %copy-done.4, bf16[16,128]{1,0:T(8,128)(2,1)} %get-tuple-element.57.sel_ref), custom_call_target="tpu_custom_call" | custom-call | flops 1000000 | bytes 2000000 | tf_op jit(solution)/shard_map/pallas_call | solution.py:585
  149.4 4.5 %collective-permute-done.8 = bf16[3,144,1152]{2,1,0:T(8,128)(2,1)S(1)} collective-permute-done((bf16[3,144,1152]{2,1,0:T(8,128)(2,1)S(1)}, bf16[3,144,1152]{2,1,0:T(8,128)(2,1)S(1)}, u32[]{:S(2)}, u32[]{:S(2)}) %collective-permute-start.8) | collective-permute-done | bytes 995360 | tf_op jit(solution)/shard_map/ppermute | solution.py:438
  153.9 2.7 %fusion.1 = (bf16[1,144,1152]{2,1,0:T(8,128)(2,1)}, bf16[1,144,1152]{2,1,0:T(8,128)(2,1)}, bf16[1,144,1152]{2,1,0:T(8,128)(2,1)}) fusion(bf16[3,144,1152]{2,1,0:T(8,128)(2,1)S(1)} %collective-permute-done.8, bf16[2,3,144,1152]{3,2,1,0:T(8,128)(2,1)} %copy-done.13, bf16[2,3,144,1152]{3,2,1,0:T(8,128)(2,1)} %get-tuple-element.55), kind=kLoop, calls=%fused_computation.3 | loop fusion | flops 2985984 | bytes 3981312 | tf_op jit(solution)/shard_map/convert_element_type | solution.py:566
  156.6 9.4 %all-to-all-done.5.got_ref = bf16[16,160,128]{2,1,0:T(8,128)(2,1)S(1)} async-done(((bf16[16,160,128]{2,1,0:T(8,128)(2,1)}), bf16[16,160,128]{2,1,0:T(8,128)(2,1)S(1)}, u32[]{:S(2)}, u32[]{:S(2)}) %all-to-all-start.5) | async-done | bytes 655392 | tf_op jit(solution)/shard_map/all_to_all | solution.py:405
  166.0 2.2 %shard_map.215 = (bf16[1,128,1152]{2,1,0:T(8,128)(2,1)}, bf16[1,128,1152]{2,1,0:T(8,128)(2,1)}, bf16[1,128,1152]{2,1,0:T(8,128)(2,1)}, f32[1,1152]{1,0:T(1,128)}, f32[1,1152]{1,0:T(1,128)}) custom-call(bf16[16,160,128]{2,1,0:T(8,128)(2,1)S(1)} %all-to-all-done.5.got_ref, bf16[128,1152]{1,0:T(8,128)(2,1)} %get-tuple-element.58.early_ref, ...), custom_call_target="tpu_custom_call" | custom-call | flops 1000000 | bytes 2000000 | tf_op jit(solution)/shard_map/pallas_call | solution.py:588
  (14 shorter events, 0.1 us)
Async XLA Ops:
  0.6 13.8 %copy-start.14 = (bf16[1,144,1152]{2,1,0:T(8,128)(2,1)S(1)}, bf16[1,144,1152]{2,1,0:T(8,128)(2,1)}, u32[]{:S(2)}) copy-start(bf16[1,144,1152]{2,1,0:T(8,128)(2,1)} %refs_1_.1) | copy-start | bytes 995332
  0.7 24.6 %copy-start.3 = (bf16[1,128,1152]{2,1,0:T(8,128)(2,1)S(1)}, bf16[1,128,1152]{2,1,0:T(8,128)(2,1)}, u32[]{:S(2)}) copy-start(bf16[1,128,1152]{2,1,0:T(8,128)(2,1)} %g_ref.3) | copy-start | bytes 884740
  0.7 24.6 %copy-start.5 = (bf16[1,128,1152]{2,1,0:T(8,128)(2,1)S(1)}, bf16[1,128,1152]{2,1,0:T(8,128)(2,1)}, u32[]{:S(2)}) copy-start(bf16[1,128,1152]{2,1,0:T(8,128)(2,1)} %q_ref.3) | copy-start | bytes 884740
  0.7 24.6 %copy-start.6 = (bf16[1,128,1152]{2,1,0:T(8,128)(2,1)S(1)}, bf16[1,128,1152]{2,1,0:T(8,128)(2,1)}, u32[]{:S(2)}) copy-start(bf16[1,128,1152]{2,1,0:T(8,128)(2,1)} %x_ref.1) | copy-start | bytes 884740
  0.7 24.6 %copy-start.9 = (s32[1,1,16,1]{2,3,1,0:T(1,128)S(1)}, s32[1,1,16,1]{2,3,1,0:T(1,128)}, u32[]{:S(2)}) copy-start(s32[1,1,16,1]{2,3,1,0:T(1,128)} %param.20) | copy-start | bytes 196
  0.7 24.6 %copy-start.10 = (s32[1,1,16]{2,1,0:T(1,128)S(1)}, s32[1,1,16]{2,1,0:T(1,128)}, u32[]{:S(2)}) copy-start(s32[1,1,16]{2,1,0:T(1,128)} %cnt_ref.3) | copy-start | bytes 196
  0.7 24.6 %copy-start.11 = (bf16[1,1,16,1]{2,3,1,0:T(2,128)(2,1)S(1)}, bf16[1,1,16,1]{2,3,1,0:T(2,128)(2,1)}, u32[]{:S(2)}) copy-start(bf16[1,1,16,1]{2,3,1,0:T(2,128)(2,1)} %param.22) | copy-start | bytes 100
  3.1 29.6 %all-to-all-start = ((bf16[16,160,128]{2,1,0:T(8,128)(2,1)}), bf16[16,160,128]{2,1,0:T(8,128)(2,1)S(1)}, u32[]{:S(2)}, u32[]{:S(2)}) async-start(bf16[16,160,128]{2,1,0:T(8,128)(2,1)} %shard_map.204), calls=%async_computation | async-start | bytes 1310720 | tf_op jit(solution)/shard_map/all_to_all | solution.py:405
  15.5 14.3 %collective-permute-start = (bf16[208,1152]{1,0:T(8,128)(2,1)S(1)}, bf16[208,1152]{1,0:T(8,128)(2,1)S(1)}, u32[]{:S(2)}, u32[]{:S(2)}) collective-permute-start(bf16[208,1152]{1,0:T(8,128)(2,1)S(1)} %pad_maximum_fusion.1), channel_id=1, source_target_pairs={{0,64},{64,0},{1,65},{65,1},{2,66},{66,2},{3,67},{67,3},{4,68},{68... | collective-permute-start | bytes 1437704 | tf_op jit(solution)/shard_map/ppermute | solution.py:438
  19.0 7.6 %collective-permute-start.1 = (bf16[1,144,1152]{2,1,0:T(8,128)(2,1)}, bf16[1,144,1152]{2,1,0:T(8,128)(2,1)S(1)}, u32[]{:S(2)}, u32[]{:S(2)}) collective-permute-start(bf16[1,144,1152]{2,1,0:T(8,128)(2,1)} %refs_0_.1), channel_id=1, source_target_pairs={{0,16},{16,0},{1,17},{17,1},{2,18},{18,2},{3,19},{19,3},{4,20},{20... | collective-permute-start | bytes 995336 | tf_op jit(solution)/shard_map/ppermute | solution.py:438
  20.9 5.6 %collective-permute-start.3 = (bf16[1,144,1152]{2,1,0:T(8,128)(2,1)}, bf16[1,144,1152]{2,1,0:T(8,128)(2,1)S(1)}, u32[]{:S(2)}, u32[]{:S(2)}) collective-permute-start(bf16[1,144,1152]{2,1,0:T(8,128)(2,1)} %refs_2_.1), channel_id=1, source_target_pairs={{0,16},{16,0},{1,17},{17,1},{2,18},{18,2},{3,19},{19,3},{4,20},{20... | collective-permute-start | bytes 995336 | tf_op jit(solution)/shard_map/ppermute | solution.py:438
  23.3 3.5 %collective-permute-start.2 = (bf16[1,144,1152]{2,1,0:T(8,128)(2,1)S(1)}, bf16[1,144,1152]{2,1,0:T(8,128)(2,1)S(1)}, u32[]{:S(2)}, u32[]{:S(2)}) collective-permute-start(bf16[1,144,1152]{2,1,0:T(8,128)(2,1)S(1)} %copy-done.14), channel_id=1, source_target_pairs={{0,16},{16,0},{1,17},{17,1},{2,18},{18,2},{3,19},{19,3},{4,20},{20... | collective-permute-start | bytes 995336 | tf_op jit(solution)/shard_map/ppermute | solution.py:438
  26.5 8.7 %copy-start = (bf16[1,144,1152]{2,1,0:T(8,128)(2,1)}, bf16[1,144,1152]{2,1,0:T(8,128)(2,1)S(1)}, u32[]{:S(2)}) copy-start(bf16[1,144,1152]{2,1,0:T(8,128)(2,1)S(1)} %collective-permute-done.1.w_1.refs_3_) | copy-start | bytes 995332
  26.5 8.7 %copy-start.1 = (bf16[1,144,1152]{2,1,0:T(8,128)(2,1)}, bf16[1,144,1152]{2,1,0:T(8,128)(2,1)S(1)}, u32[]{:S(2)}) copy-start(bf16[1,144,1152]{2,1,0:T(8,128)(2,1)S(1)} %collective-permute-done.3.w_3.refs_5_) | copy-start | bytes 995332
  26.9 8.3 %copy-start.2 = (bf16[1,144,1152]{2,1,0:T(8,128)(2,1)}, bf16[1,144,1152]{2,1,0:T(8,128)(2,1)S(1)}, u32[]{:S(2)}) copy-start(bf16[1,144,1152]{2,1,0:T(8,128)(2,1)S(1)} %collective-permute-done.2.w_2.refs_4_) | copy-start | bytes 995332
  35.2 25.1 %copy-start.7 = (f32[1,1152]{1,0:T(1,128)S(1)}, f32[1,1152]{1,0:T(1,128)}, u32[]{:S(2)}) copy-start(f32[1,1152]{1,0:T(1,128)} %scale_ref.3) | copy-start | bytes 13828
  35.2 25.0 %all-to-all-start.1 = ((bf16[16,184,128]{2,1,0:T(8,128)(2,1)}), bf16[16,184,128]{2,1,0:T(8,128)(2,1)S(1)}, u32[]{:S(2)}, u32[]{:S(2)}) async-start(bf16[16,184,128]{2,1,0:T(8,128)(2,1)} %get-tuple-element.39), calls=%async_computation.1 | async-start | bytes 1507328 | tf_op jit(solution)/shard_map/all_to_all | solution.py:405
  41.3 14.9 %collective-permute-start.4 = (bf16[224,1152]{1,0:T(8,128)(2,1)S(1)}, bf16[224,1152]{1,0:T(8,128)(2,1)S(1)}, u32[]{:S(2)}, u32[]{:S(2)}) collective-permute-start(bf16[224,1152]{1,0:T(8,128)(2,1)S(1)} %pad_maximum_fusion), channel_id=1, source_target_pairs={{0,64},{64,0},{1,65},{65,1},{2,66},{66,2},{3,67},{67,3},{4,68},{68... | collective-permute-start | bytes 1548296 | tf_op jit(solution)/shard_map/ppermute | solution.py:438
  44.8 41.3 %collective-permute-start.5 = (bf16[208,1152]{1,0:T(8,128)(2,1)S(1)}, bf16[208,1152]{1,0:T(8,128)(2,1)}, u32[]{:S(2)}, u32[]{:S(2)}) collective-permute-start(bf16[208,1152]{1,0:T(8,128)(2,1)S(1)} %collective-permute-done.w_0.refs_6_), channel_id=1, source_target_pairs={{0,16},{16,0},{1,17},{17,1},{2,18},{18,2},{3,19},{19,3},{4,20},{20... | collective-permute-start | bytes 1437704 | tf_op jit(solution)/shard_map/ppermute | solution.py:438
  56.2 30.0 %collective-permute-start.6 = (bf16[224,1152]{1,0:T(8,128)(2,1)S(1)}, bf16[224,1152]{1,0:T(8,128)(2,1)S(1)}, u32[]{:S(2)}, u32[]{:S(2)}) collective-permute-start(bf16[224,1152]{1,0:T(8,128)(2,1)S(1)} %collective-permute-done.4.w_0.refs_7_), channel_id=1, source_target_pairs={{0,16},{16,0},{1,17},{17,1},{2,18},{18,2},{3,19},{19,3},{4,20},{20... | collective-permute-start | bytes 1548296 | tf_op jit(solution)/shard_map/ppermute | solution.py:438
  60.3 0.7 copy-start.8
  62.1 27.8 %all-to-all-start.2 = ((bf16[8,16,2432]{2,1,0:T(8,128)(2,1)}), bf16[8,16,2432]{2,1,0:T(8,128)(2,1)S(1)}, u32[]{:S(2)}, u32[]{:S(2)}) async-start(bf16[8,16,2432]{2,1,0:T(8,128)(2,1)} %get-tuple-element.40), calls=%async_computation.2 | async-start | bytes 1245184 | tf_op jit(solution)/shard_map/all_to_all | solution.py:405
  96.0 16.9 %all-to-all-start.3 = ((bf16[8,16,1280]{2,1,0:T(8,128)(2,1)}), bf16[8,16,1280]{2,1,0:T(8,128)(2,1)S(1)}, u32[]{:S(2)}, u32[]{:S(2)}) async-start(bf16[8,16,1280]{2,1,0:T(8,128)(2,1)} %get-tuple-element.43.refs_1_), calls=%async_computation.3 | async-start | bytes 655360 | tf_op jit(solution)/shard_map/all_to_all | solution.py:405
  115.2 9.6 %collective-permute-start.7 = (bf16[2,3,144,1152]{3,2,1,0:T(8,128)(2,1)}, bf16[2,3,144,1152]{3,2,1,0:T(8,128)(2,1)S(1)}, u32[]{:S(2)}, u32[]{:S(2)}) collective-permute-start(bf16[2,3,144,1152]{3,2,1,0:T(8,128)(2,1)} %get-tuple-element.56), channel_id=1, source_target_pairs={{0,16},{16,0},{1,17},{17,1},{2,18},{18,2},{3,19},{19,3},{4,20},{20... | collective-permute-start | bytes 5971976 | tf_op jit(solution)/shard_map/ppermute | solution.py:438
  117.2 21.8 %all-to-all-start.4 = ((bf16[16,104,128]{2,1,0:T(8,128)(2,1)}), bf16[16,104,128]{2,1,0:T(8,128)(2,1)S(1)}, u32[]{:S(2)}, u32[]{:S(2)}) async-start(bf16[16,104,128]{2,1,0:T(8,128)(2,1)} %get-tuple-element.52), calls=%async_computation.4 | async-start | bytes 851968 | tf_op jit(solution)/shard_map/all_to_all | solution.py:405
  124.8 1.3 copy-start.13
  127.9 11.1 %copy-start.12 = (bf16[3,144,1152]{2,1,0:T(8,128)(2,1)}, bf16[3,144,1152]{2,1,0:T(8,128)(2,1)S(1)}, u32[]{:S(2)}) copy-start(bf16[3,144,1152]{2,1,0:T(8,128)(2,1)S(1)} %fusion.near) | copy-start | bytes 2985988
  127.9 26.0 %collective-permute-start.8 = (bf16[3,144,1152]{2,1,0:T(8,128)(2,1)S(1)}, bf16[3,144,1152]{2,1,0:T(8,128)(2,1)S(1)}, u32[]{:S(2)}, u32[]{:S(2)}) collective-permute-start(bf16[3,144,1152]{2,1,0:T(8,128)(2,1)S(1)} %fusion.near), channel_id=1, source_target_pairs={{0,64},{64,0},{1,65},{65,1},{2,66},{66,2},{3,67},{67,3},{4,68},{68... | collective-permute-start | bytes 2985992 | tf_op jit(solution)/shard_map/ppermute | solution.py:438
  139.0 8.6 %copy-start.4 = (bf16[1,128,1152]{2,1,0:T(8,128)(2,1)S(1)}, bf16[1,128,1152]{2,1,0:T(8,128)(2,1)}, u32[]{:S(2)}) copy-start(bf16[1,128,1152]{2,1,0:T(8,128)(2,1)} %g_ref.3) | copy-start | bytes 884740
  143.0 23.0 %all-to-all-start.5 = ((bf16[16,160,128]{2,1,0:T(8,128)(2,1)}), bf16[16,160,128]{2,1,0:T(8,128)(2,1)S(1)}, u32[]{:S(2)}, u32[]{:S(2)}) async-start(bf16[16,160,128]{2,1,0:T(8,128)(2,1)} %shard_map.213), calls=%async_computation.5 | async-start | bytes 1310720 | tf_op jit(solution)/shard_map/all_to_all | solution.py:405

commit v3 on v2

--- a/solution.py
+++ b/solution.py
@@ -255,19 +255,30 @@
     )
 
 
-def weight_grads_kernel(rows_ref, hidden_ref, gate_ref, up_ref, late, own_ref, other_ref):
+def weight_grads_kernel(
+    rows_ref, hidden_ref, gate_ref, up_ref, late, own_ref, other_ref, far_0, far_1, far_2
+):
     rows, grads, gates = expert_rows(rows_ref)
     scaled = (gates * grads.astype(F32)).astype(BF)
-    for part in range(hidden_ref.shape[0]):
-        out = (own_ref, other_ref)[part % 2]
-        out[part // 2, 0] = mm(gate_ref[part], rows, TN).astype(out.dtype)
-        out[part // 2, 1] = mm(up_ref[part], rows, TN).astype(out.dtype)
-        out[part // 2, 2] = mm(hidden_ref[part], scaled, TN).astype(out.dtype)
-
-
-def back_kernel(
-    got_ref, normed_ref, inv_ref, scale_ref, _, _others, sent_ref, gate_ref, others, send_ref, sem
-):
+    outs = (
+        [own_ref.at[0, i] for i in range(3)],
+        [other_ref.at[i] for i in range(3)],
+        [own_ref.at[1, i] for i in range(3)],
+        [far_0, far_1, far_2],
+    )
+    for part, (out_gate, out_up, out_down) in enumerate(outs):
+        out_gate[...] = mm(gate_ref[part], rows, TN).astype(BF)
+        out_up[...] = mm(up_ref[part], rows, TN).astype(BF)
+        out_down[...] = mm(hidden_ref[part], scaled, TN).astype(BF)
+
+
+def near_sum_kernel(own_ref, got_0, got_1, got_2, sum_ref):
+    for i, got in enumerate((got_0, got_1, got_2)):
+        sum_ref[i] = (own_ref[0, i].astype(F32) + got[...].astype(F32)).astype(BF)
+
+
+def back_kernel(got_ref, normed_ref, inv_ref, scale_ref, *refs):
+    sent_ref, gate_ref, send_ref, sem = refs[5], refs[6], refs[-2], refs[-1]
     frames, width = normed_ref.shape
     total = got_ref[0].astype(F32)
     for i in range(1, got_ref.shape[0]):
@@ -483,8 +494,8 @@
     )(qg_got, shift, scale, near[1])
     rows_all = swap(rows_sent, ROWS)
 
-    block = 2
-    first_steps = 6
+    block = 4
+    first_steps = 3
     rows_back = 2 * frames + HEAD
     early_outs = [pltpu.HBM((frames, rows_back, tokens), BF), pltpu.HBM((body, length), F32)]
 
@@ -492,7 +503,8 @@
         return call(
             functools.partial(attention_kernel, started),
             early_outs,
-            flops=20_000_000_000 * steps,
+            flops=40_000_000_000 * steps,
+            mib=32,
             grid=(steps,),
             in_specs=[
                 whole(keys_got.shape),
@@ -530,45 +542,53 @@
         input_output_aliases={2: 0},
     )
 
-    own, others = call(
+    grad_shape = (hidden, width)
+    own, *others = call(
         weight_grads_kernel,
-        [pltpu.HBM((2, 3, hidden, width), BF)] * 2,
+        [pltpu.HBM((2, 3) + grad_shape, BF), pltpu.HBM((3,) + grad_shape, BF)]
+        + [pltpu.HBM(grad_shape, BF)] * 3,
         in_specs=[whole(a.shape) for a in (rows_all, hid, gate_delta, up_delta)] + [ANY],
     )(rows_all, *hbm(hid, gate_delta, up_delta, sums))
-    back_next, gate_grad, others = call(
+
+    back_next, gate_grad, *others = call(
         back_kernel,
         [
             pltpu.HBM((heads, rows_back, LANES), BF),
             jax.ShapeDtypeStruct((1, 1, frames), F32),
-            pltpu.HBM(others.shape, BF),
-        ],
+            pltpu.HBM((3,) + grad_shape, BF),
+        ]
+        + [pltpu.HBM(grad_shape, BF)] * 3,
         in_specs=[
             whole(back_got.shape),
             whole(normed.shape),
             whole(inv.shape),
             whole(scale.shape),
-            ANY,
-            ANY,
-        ],
-        out_specs=[ANY, whole((1, 1, frames)), ANY],
-        input_output_aliases={4: 0, 5: 2},
+        ]
+        + [ANY] * 5,
+        out_specs=[ANY, whole((1, 1, frames))] + [ANY] * 4,
+        input_output_aliases={4: 0, 5: 2, 6: 3, 7: 4, 8: 5},
         scratch_shapes=[
             pltpu.VMEM((heads, 2 * frames, LANES), BF),
             pltpu.SemaphoreType.DMA,
         ],
-    )(back_got, *hbm(normed, inv), scale, *hbm(back_next, others))
+    )(back_got, *hbm(normed, inv), scale, *hbm(back_next, *others))
     delta_got = swap(back_next, SEQ)
 
-    got_core = across(others, "core")
-    own_near = (own[1].astype(F32) + got_core[1].astype(F32)).astype(BF)
+    far_got = [across(o, "core") for o in others[1:]]
+    (own_near,) = call(
+        near_sum_kernel,
+        [pltpu.HBM((3,) + grad_shape, BF)],
+        grid=(1,),
+        in_specs=[pl.BlockSpec((1, 3) + grad_shape, lambda _: (1, 0, 0, 0))]
+        + [whole(grad_shape)] * 3,
+        out_specs=[whole((3,) + grad_shape)],
+    )(*hbm(own), *far_got)
     got_near = across(own_near, "yl")
+    got_core = across(others[0], "core")
     w_grads = [
-        (own[0, i].astype(F32) + got_core[0, i].astype(F32) + got_near[i].astype(F32)).astype(BF)[
-            None
-        ]
+        (own[0, i].astype(F32) + got_core[i].astype(F32) + got_near[i].astype(F32)).astype(BF)[None]
         for i in range(3)
     ]
-
 
     (late_sent,) = call(
         late_kernel,

time: 170 us -> 169 us (level)
  the two profiles are of different devices: /device:TPU:16 before, /device:TPU:12 now
where the time goes in v3:
time: 169 us; the launch traced here: 168 us
  starting transfers between devices  76.9 us (46%)
  Pallas kernels  49 us (29%)
  waiting for transfers between devices  35.3 us (21%)
  other arithmetic  4.7 us (3%)
    all_to_all x6, starting transfers between devices, swap(): return lax.all_to_all(block, axes, split_axis=0, concat_axis=0, tiled=True)  47.8 us
    ppermute x12, starting transfers between devices, across(): return lax.ppermute(block, axis, other)  29.1 us
    ppermute x12, waiting for transfers between devices, across(): return lax.ppermute(block, axis, other)  23.4 us
    pallas_call x2, Pallas kernels, early(): call(functools.partial(attention_kernel, started), early_outs, flops=4000...  18.8 us
    all_to_all x6, waiting for transfers between devices, swap(): return lax.all_to_all(block, axes, split_axis=0, concat_axis=0, tiled=True)  11.9 us
    pallas_call x1, Pallas kernels, shards(): call(expert_kernel, [pltpu.HBM((groups, frames, width + LANES), BF)] + [p...  6.12 us
    pallas_call x1, Pallas kernels, shards(): call(weight_grads_kernel, [pltpu.HBM((2, 3) + grad_shape, BF), pltpu.HBM(...  4.09 us
    pallas_call x1, Pallas kernels, shards(): call(late_kernel, [pltpu.HBM((frames, body + experts, tokens), BF)], grid...  4.03 us
  transfers between devices with their start and end apart: 18, of which 9 were waited for; matrix products, arithmetic and copies ran while one was open for 3% of the time, Pallas kernels for 20%

profile of v3, /device:TPU:12, one launch (start us, length us, event | category | flops | bytes accessed | tf_op | source)
XLA Modules:
  0.0 167.7 jit_solution(1242318424768816758)
XLA Ops:
  0.6 0.0 copy-start.13
  0.7 0.0 copy-start.3
  0.7 0.0 copy-start.5
  0.7 0.0 copy-start.6
  0.7 0.0 copy-start.9
  0.7 0.0 copy-start.10
  0.7 0.0 copy-start.11
  0.7 2.4 %shard_map.204 = bf16[16,160,128]{2,1,0:T(8,128)(2,1)} custom-call(bf16[1,128,1152]{2,1,0:T(8,128)(2,1)} %q_ref.3, bf16[1,128,1152]{2,1,0:T(8,128)(2,1)} %k_ref.1, bf16[1,128,1152]{2,1,0:T(8,128)(2,1)} %v_ref.1, s32[1,1,16]{2,1,0:T(1,128)} %bitcast.18, s32[1,1,16]{2,1,0:T(1,128)} %cnt_ref.3), custom_call_target="tpu_custom_call" | custom-call | flops 1000000 | bytes 2000000 | tf_op jit(solution)/shard_map/pallas_call | solution.py:458
  3.1 11.1 %all-to-all-start = ((bf16[16,160,128]{2,1,0:T(8,128)(2,1)}), bf16[16,160,128]{2,1,0:T(8,128)(2,1)S(1)}, u32[]{:S(2)}, u32[]{:S(2)}) async-start(bf16[16,160,128]{2,1,0:T(8,128)(2,1)} %shard_map.204), calls=%async_computation | async-start | bytes 1310720 | tf_op jit(solution)/shard_map/all_to_all | solution.py:416
  14.2 1.0 pad_maximum_fusion.1
  15.2 2.4 %collective-permute-start = (bf16[208,1152]{1,0:T(8,128)(2,1)S(1)}, bf16[208,1152]{1,0:T(8,128)(2,1)S(1)}, u32[]{:S(2)}, u32[]{:S(2)}) collective-permute-start(bf16[208,1152]{1,0:T(8,128)(2,1)S(1)} %pad_maximum_fusion.1), channel_id=1, source_target_pairs={{0,64},{64,0},{1,65},{65,1},{2,66},{66,2},{3,67},{67,3},{4,68},{68... | collective-permute-start | bytes 1437704 | tf_op jit(solution)/shard_map/ppermute | solution.py:449
  17.6 1.9 %collective-permute-start.1 = (bf16[1,144,1152]{2,1,0:T(8,128)(2,1)}, bf16[1,144,1152]{2,1,0:T(8,128)(2,1)S(1)}, u32[]{:S(2)}, u32[]{:S(2)}) collective-permute-start(bf16[1,144,1152]{2,1,0:T(8,128)(2,1)} %refs_0_.1), channel_id=1, source_target_pairs={{0,16},{16,0},{1,17},{17,1},{2,18},{18,2},{3,19},{19,3},{4,20},{20... | collective-permute-start | bytes 995336 | tf_op jit(solution)/shard_map/ppermute | solution.py:449
  19.5 2.4 %collective-permute-start.3 = (bf16[1,144,1152]{2,1,0:T(8,128)(2,1)}, bf16[1,144,1152]{2,1,0:T(8,128)(2,1)S(1)}, u32[]{:S(2)}, u32[]{:S(2)}) collective-permute-start(bf16[1,144,1152]{2,1,0:T(8,128)(2,1)} %refs_2_.1), channel_id=1, source_target_pairs={{0,16},{16,0},{1,17},{17,1},{2,18},{18,2},{3,19},{19,3},{4,20},{20... | collective-permute-start | bytes 995336 | tf_op jit(solution)/shard_map/ppermute | solution.py:449
  21.9 1.9 %collective-permute-start.2 = (bf16[1,144,1152]{2,1,0:T(8,128)(2,1)S(1)}, bf16[1,144,1152]{2,1,0:T(8,128)(2,1)S(1)}, u32[]{:S(2)}, u32[]{:S(2)}) collective-permute-start(bf16[1,144,1152]{2,1,0:T(8,128)(2,1)S(1)} %copy-done.13), channel_id=1, source_target_pairs={{0,16},{16,0},{1,17},{17,1},{2,18},{18,2},{3,19},{19,3},{4,20},{20... | collective-permute-start | bytes 995336 | tf_op jit(solution)/shard_map/ppermute | solution.py:449
  23.9 1.2 shard_map.205
  25.1 0.0 collective-permute-done.1.w_1.refs_3_
  25.1 0.0 collective-permute-done.3.w_3.refs_5_
  25.1 0.0 copy-start.1
  25.2 0.3 collective-permute-done.2.w_2.refs_4_
  25.5 4.1 %collective-permute-done.w_0.refs_6_ = bf16[208,1152]{1,0:T(8,128)(2,1)S(1)} collective-permute-done((bf16[208,1152]{1,0:T(8,128)(2,1)S(1)}, bf16[208,1152]{1,0:T(8,128)(2,1)S(1)}, u32[]{:S(2)}, u32[]{:S(2)}) %collective-permute-start) | collective-permute-done | bytes 479264 | tf_op jit(solution)/shard_map/ppermute | solution.py:449
  29.5 2.8 %all-to-all-done.got_ref.kv_in_ref = bf16[16,160,128]{2,1,0:T(8,128)(2,1)S(1)} async-done(((bf16[16,160,128]{2,1,0:T(8,128)(2,1)}), bf16[16,160,128]{2,1,0:T(8,128)(2,1)S(1)}, u32[]{:S(2)}, u32[]{:S(2)}) %all-to-all-start) | async-done | bytes 655392 | tf_op jit(solution)/shard_map/all_to_all | solution.py:416
  32.4 2.5 %shard_map.206 = (bf16[16,184,128]{2,1,0:T(8,128)(2,1)}, bf16[16,16,128]{2,1,0:T(8,128)(2,1)}, bf16[256,128]{1,0:T(8,128)(2,1)}) custom-call(bf16[16,160,128]{2,1,0:T(8,128)(2,1)S(1)} %all-to-all-done.got_ref.kv_in_ref, bf16[16,184,128]{2,1,0:T(8,128)(2,1)} %get-tuple-element.44._, ...), custom_call_target="tpu_custom_call", output_to_operand_aliasing={{0}: (1, {})} | custom-call | flops 1000000 | bytes 2000000 | tf_op jit(solution)/shard_map/pallas_call | solution.py:467
  34.9 0.0 copy-start.7
  35.0 5.0 %all-to-all-start.1 = ((bf16[16,184,128]{2,1,0:T(8,128)(2,1)}), bf16[16,184,128]{2,1,0:T(8,128)(2,1)S(1)}, u32[]{:S(2)}, u32[]{:S(2)}) async-start(bf16[16,184,128]{2,1,0:T(8,128)(2,1)} %get-tuple-element.45), calls=%async_computation.1 | async-start | bytes 1507328 | tf_op jit(solution)/shard_map/all_to_all | solution.py:416
  40.0 1.0 pad_maximum_fusion
  41.0 2.4 %collective-permute-start.4 = (bf16[224,1152]{1,0:T(8,128)(2,1)S(1)}, bf16[224,1152]{1,0:T(8,128)(2,1)S(1)}, u32[]{:S(2)}, u32[]{:S(2)}) collective-permute-start(bf16[224,1152]{1,0:T(8,128)(2,1)S(1)} %pad_maximum_fusion), channel_id=1, source_target_pairs={{0,64},{64,0},{1,65},{65,1},{2,66},{66,2},{3,67},{67,3},{4,68},{68... | collective-permute-start | bytes 1548296 | tf_op jit(solution)/shard_map/ppermute | solution.py:449
  43.4 1.9 %collective-permute-start.5 = (bf16[208,1152]{1,0:T(8,128)(2,1)S(1)}, bf16[208,1152]{1,0:T(8,128)(2,1)}, u32[]{:S(2)}, u32[]{:S(2)}) collective-permute-start(bf16[208,1152]{1,0:T(8,128)(2,1)S(1)} %collective-permute-done.w_0.refs_6_), channel_id=1, source_target_pairs={{0,16},{16,0},{1,17},{17,1},{2,18},{18,2},{3,19},{19,3},{4,20},{20... | collective-permute-start | bytes 1437704 | tf_op jit(solution)/shard_map/ppermute | solution.py:449
  45.3 10.6 %collective-permute-done.4.w_0.refs_7_ = bf16[224,1152]{1,0:T(8,128)(2,1)S(1)} collective-permute-done((bf16[224,1152]{1,0:T(8,128)(2,1)S(1)}, bf16[224,1152]{1,0:T(8,128)(2,1)S(1)}, u32[]{:S(2)}, u32[]{:S(2)}) %collective-permute-start.4) | collective-permute-done | bytes 516128 | tf_op jit(solution)/shard_map/ppermute | solution.py:449
  55.9 1.9 %collective-permute-start.6 = (bf16[224,1152]{1,0:T(8,128)(2,1)S(1)}, bf16[224,1152]{1,0:T(8,128)(2,1)S(1)}, u32[]{:S(2)}, u32[]{:S(2)}) collective-permute-start(bf16[224,1152]{1,0:T(8,128)(2,1)S(1)} %collective-permute-done.4.w_0.refs_7_), channel_id=1, source_target_pairs={{0,16},{16,0},{1,17},{17,1},{2,18},{18,2},{3,19},{19,3},{4,20},{20... | collective-permute-start | bytes 1548296 | tf_op jit(solution)/shard_map/ppermute | solution.py:449
  57.8 2.2 %all-to-all-done.1.got_ref.qg_ref = bf16[16,184,128]{2,1,0:T(8,128)(2,1)S(1)} async-done(((bf16[16,184,128]{2,1,0:T(8,128)(2,1)}), bf16[16,184,128]{2,1,0:T(8,128)(2,1)S(1)}, u32[]{:S(2)}, u32[]{:S(2)}) %all-to-all-start.1) | async-done | bytes 753696 | tf_op jit(solution)/shard_map/all_to_all | solution.py:416
  60.0 0.0 copy-done.7
  60.0 0.7 copy-done.8
  60.7 1.1 shard_map.207
  61.8 9.2 %all-to-all-start.2 = ((bf16[8,16,2432]{2,1,0:T(8,128)(2,1)}), bf16[8,16,2432]{2,1,0:T(8,128)(2,1)S(1)}, u32[]{:S(2)}, u32[]{:S(2)}) async-start(bf16[8,16,2432]{2,1,0:T(8,128)(2,1)} %get-tuple-element.46), calls=%async_computation.2 | async-start | bytes 1245184 | tf_op jit(solution)/shard_map/all_to_all | solution.py:416
  71.0 12.6 %shard_map.208 = (bf16[16,104,128]{2,1,0:T(8,128)(2,1)}, f32[144,2048]{1,0:T(8,128)}) custom-call(bf16[16,160,128]{2,1,0:T(8,128)(2,1)S(1)} %all-to-all-done.got_ref.kv_in_ref, bf16[16,184,128]{2,1,0:T(8,128)(2,1)S(1)} %all-to-all-done.1.got_ref.qg_ref, f32[16,128]{1,0:T(8,128)} %get-tuple-element.47.refs_0_.inv_ref), custom_call_target="tpu_custom_call" | custom-call | flops 120000004096 | bytes 2000000 | tf_op jit(solution)/shard_map/pallas_call | solution.py:503
  83.6 0.0 collective-permute-done.5.refs_8_
  83.6 0.0 collective-permute-done.6.refs_9_
  83.6 1.4 all-to-all-done.2.rows_ref
  85.0 6.1 %shard_map.209 = (bf16[8,16,1280]{2,1,0:T(8,128)(2,1)}, bf16[4,128,144]{2,1,0:T(8,128)(2,1)}, bf16[4,128,144]{2,1,0:T(8,128)(2,1)}, bf16[4,128,144]{2,1,0:T(8,128)(2,1)}) custom-call(bf16[8,16,2432]{2,1,0:T(8,128)(2,1)S(1)} %all-to-all-done.2.rows_ref, bf16[1,144,1152]{2,1,0:T(8,128)(2,1)} %refs_0_.1, bf16[1,144,1152]{2,1,0:T(8,128)(2,1)} %refs_1_.1, ...), custom_call_target="tpu_custom_call" | custom-call | flops 1000000 | bytes 2000000 | tf_op jit(solution)/shard_map/pallas_call | solution.py:524
  91.1 8.3 %all-to-all-start.3 = ((bf16[8,16,1280]{2,1,0:T(8,128)(2,1)}), bf16[8,16,1280]{2,1,0:T(8,128)(2,1)S(1)}, u32[]{:S(2)}, u32[]{:S(2)}) async-start(bf16[8,16,1280]{2,1,0:T(8,128)(2,1)} %get-tuple-element.49.refs_1_), calls=%async_computation.3 | async-start | bytes 655360 | tf_op jit(solution)/shard_map/all_to_all | solution.py:416
  99.4 6.1 %shard_map.210 = (bf16[16,104,128]{2,1,0:T(8,128)(2,1)}, f32[144,2048]{1,0:T(8,128)}) custom-call(bf16[16,160,128]{2,1,0:T(8,128)(2,1)S(1)} %all-to-all-done.got_ref.kv_in_ref, bf16[16,184,128]{2,1,0:T(8,128)(2,1)S(1)} %all-to-all-done.1.got_ref.qg_ref, bf16[16,104,128]{2,1,0:T(8,128)(2,1)} %get-tuple-element.51.refs_0_, ...), custom_call_target="tpu_custom_call", output_to_operand_aliasing={{0}: (2, {})} | custom-call | flops 40000000000 | bytes 2000000 | tf_op jit(solution)/shard_map/pallas_call | solution.py:503
  105.5 4.1 %shard_map.211 = (bf16[2,3,144,1152]{3,2,1,0:T(8,128)(2,1)}, bf16[3,144,1152]{2,1,0:T(8,128)(2,1)}, bf16[144,1152]{1,0:T(8,128)(2,1)}, bf16[144,1152]{1,0:T(8,128)(2,1)}, bf16[144,1152]{1,0:T(8,128)(2,1)}) custom-call(bf16[8,16,2432]{2,1,0:T(8,128)(2,1)S(1)} %all-to-all-done.2.rows_ref, bf16[4,128,144]{2,1,0:T(8,128)(2,1)} %get-tuple-element.53.hidden_ref, ...), custom_call_target="tpu_custom_call" | custom-call | flops 1000000 | bytes 2000000 | tf_op jit(solution)/shard_map/pallas_call | solution.py:546
  109.6 0.2 all-to-all-done.3.got_ref
  109.9 2.4 %shard_map.212 = (bf16[16,104,128]{2,1,0:T(8,128)(2,1)}, f32[1,1,16]{2,1,0:T(1,128)}, bf16[3,144,1152]{2,1,0:T(8,128)(2,1)}, bf16[144,1152]{1,0:T(8,128)(2,1)}, ...) custom-call(bf16[8,16,1280]{2,1,0:T(8,128)(2,1)S(1)} %all-to-all-don, ...), custom_call_target="tpu_custom_call", output_to_operand_aliasing={{0}: (4, {}), {2}: (5, {}), {3}: (6, {}), {4}: (7, {}), {5}... | custom-call | flops 1000000 | bytes 2000000 | tf_op jit(solution)/shard_map/pallas_call | solution.py:553
  112.2 6.1 %all-to-all-start.4 = ((bf16[16,104,128]{2,1,0:T(8,128)(2,1)}), bf16[16,104,128]{2,1,0:T(8,128)(2,1)S(1)}, u32[]{:S(2)}, u32[]{:S(2)}) async-start(bf16[16,104,128]{2,1,0:T(8,128)(2,1)} %get-tuple-element.61), calls=%async_computation.4 | async-start | bytes 851968 | tf_op jit(solution)/shard_map/all_to_all | solution.py:416
  118.3 1.9 %collective-permute-start.7 = (bf16[144,1152]{1,0:T(8,128)(2,1)}, bf16[144,1152]{1,0:T(8,128)(2,1)S(1)}, u32[]{:S(2)}, u32[]{:S(2)}) collective-permute-start(bf16[144,1152]{1,0:T(8,128)(2,1)} %get-tuple-element.65), channel_id=1, source_target_pairs={{0,16},{16,0},{1,17},{17,1},{2,18},{18,2},{3,19},{19,3},{4,20},{20... | collective-permute-start | bytes 995336 | tf_op jit(solution)/shard_map/ppermute | solution.py:449
  120.3 2.4 %collective-permute-start.8 = (bf16[144,1152]{1,0:T(8,128)(2,1)}, bf16[144,1152]{1,0:T(8,128)(2,1)S(1)}, u32[]{:S(2)}, u32[]{:S(2)}) collective-permute-start(bf16[144,1152]{1,0:T(8,128)(2,1)} %get-tuple-element.66), channel_id=1, source_target_pairs={{0,16},{16,0},{1,17},{17,1},{2,18},{18,2},{3,19},{19,3},{4,20},{20... | collective-permute-start | bytes 995336 | tf_op jit(solution)/shard_map/ppermute | solution.py:449
  122.7 1.9 %collective-permute-start.9 = (bf16[144,1152]{1,0:T(8,128)(2,1)}, bf16[144,1152]{1,0:T(8,128)(2,1)S(1)}, u32[]{:S(2)}, u32[]{:S(2)}) collective-permute-start(bf16[144,1152]{1,0:T(8,128)(2,1)} %get-tuple-element.67), channel_id=1, source_target_pairs={{0,16},{16,0},{1,17},{17,1},{2,18},{18,2},{3,19},{19,3},{4,20},{20... | collective-permute-start | bytes 995336 | tf_op jit(solution)/shard_map/ppermute | solution.py:449
  124.6 2.4 %collective-permute-start.10 = (bf16[3,144,1152]{2,1,0:T(8,128)(2,1)}, bf16[3,144,1152]{2,1,0:T(8,128)(2,1)}, u32[]{:S(2)}, u32[]{:S(2)}) collective-permute-start(bf16[3,144,1152]{2,1,0:T(8,128)(2,1)} %get-tuple-element.76), channel_id=1, source_target_pairs={{0,16},{16,0},{1,17},{17,1},{2,18},{18,2},{3,19},{19,3},{4,20},{20... | collective-permute-start | bytes 2985992 | tf_op jit(solution)/shard_map/ppermute | solution.py:449
  127.0 0.0 collective-permute-done.7.got_0
  127.0 0.0 collective-permute-done.8.got_1
  127.0 0.0 collective-permute-done.9.got_2
  127.0 2.4 %shard_map.213.near = bf16[3,144,1152]{2,1,0:T(8,128)(2,1)} custom-call(bf16[2,3,144,1152]{3,2,1,0:T(8,128)(2,1)} %get-tuple-element.64.own_ref, bf16[144,1152]{1,0:T(8,128)(2,1)S(1)} %collective-permute-done.7.got_0, bf16[144,1152]{1,0:T(8,128)(2,1)S(1)} %collective-permute-done.8.got_1, bf16[144,1152]{1,0:T(8,128)(2,1)S(1)} %collective-permute-done.9.got_2), custom_call_target="tpu_custom_call" | custom-call | flops 1000000 | bytes 2000000 | tf_op jit(solution)/shard_map/pallas_call | solution.py:578
  129.5 5.6 %collective-permute-start.11 = (bf16[3,144,1152]{2,1,0:T(8,128)(2,1)}, bf16[3,144,1152]{2,1,0:T(8,128)(2,1)}, u32[]{:S(2)}, u32[]{:S(2)}) collective-permute-start(bf16[3,144,1152]{2,1,0:T(8,128)(2,1)} %shard_map.213.near), channel_id=1, source_target_pairs={{0,64},{64,0},{1,65},{65,1},{2,66},{66,2},{3,67},{67,3},{4,68},{68... | collective-permute-start | bytes 2985992 | tf_op jit(solution)/shard_map/ppermute | solution.py:449
  135.1 0.0 all-to-all-done.4.got_ref
  135.2 0.0 copy-start.4
  135.2 4.0 %shard_map.214 = bf16[16,160,128]{2,1,0:T(8,128)(2,1)} custom-call(bf16[16,104,128]{2,1,0:T(8,128)(2,1)S(1)} %all-to-all-done.4.got_ref, bf16[16,160,128]{2,1,0:T(8,128)(2,1)S(1)} %all-to-all-done.got_ref.kv_in_ref, bf16[256,128]{1,0:T(8,128)(2,1)} %get-tuple-element.62.query_ref, bf16[16,16,128]{2,1,0:T(8,128)(2,1)} %get-tuple-element.63.att_ref, ...), custom_call_target="tpu_custom_call" | custom-call | flops 1000000 | bytes 2000000 | tf_op jit(solution)/shard_map/pallas_call | solution.py:593
  139.2 8.2 %all-to-all-start.5 = ((bf16[16,160,128]{2,1,0:T(8,128)(2,1)}), bf16[16,160,128]{2,1,0:T(8,128)(2,1)S(1)}, u32[]{:S(2)}, u32[]{:S(2)}) async-start(bf16[16,160,128]{2,1,0:T(8,128)(2,1)} %shard_map.214), calls=%async_computation.5 | async-start | bytes 1310720 | tf_op jit(solution)/shard_map/all_to_all | solution.py:416
  147.5 1.7 %shard_map.215 = (bf16[1,128,1152]{2,1,0:T(8,128)(2,1)}, bf16[128,1152]{1,0:T(8,128)(2,1)}) custom-call(bf16[16,104,128]{2,1,0:T(8,128)(2,1)S(1)} %all-to-all-done.4.got_ref, bf16[1,128,1152]{2,1,0:T(8,128)(2,1)S(1)} %copy-done.4, bf16[16,128]{1,0:T(8,128)(2,1)} %get-tuple-element.68.sel_ref), custom_call_target="tpu_custom_call" | custom-call | flops 1000000 | bytes 2000000 | tf_op jit(solution)/shard_map/pallas_call | solution.py:605
  149.2 0.0 collective-permute-done.10
  149.2 8.4 %collective-permute-done.11 = bf16[3,144,1152]{2,1,0:T(8,128)(2,1)} collective-permute-done((bf16[3,144,1152]{2,1,0:T(8,128)(2,1)}, bf16[3,144,1152]{2,1,0:T(8,128)(2,1)}, u32[]{:S(2)}, u32[]{:S(2)}) %collective-permute-start.11) | collective-permute-done | bytes 995360 | tf_op jit(solution)/shard_map/ppermute | solution.py:449
  157.6 2.7 %fusion.1 = (bf16[1,144,1152]{2,1,0:T(8,128)(2,1)}, bf16[1,144,1152]{2,1,0:T(8,128)(2,1)}, bf16[1,144,1152]{2,1,0:T(8,128)(2,1)}) fusion(bf16[3,144,1152]{2,1,0:T(8,128)(2,1)} %collective-permute-done.11, bf16[3,144,1152]{2,1,0:T(8,128)(2,1)} %collective-permute-done.10, bf16[2,3,144,1152]{3,2,1,0:T(8,128)(2,1)S(1)} %copy-done.12), kind=kLoop, calls=%fused_computation.2 | loop fusion | flops 2985984 | bytes 3981312 | tf_op jit(solution)/shard_map/convert_element_type | solution.py:589
  160.3 5.2 %all-to-all-done.5.got_ref = bf16[16,160,128]{2,1,0:T(8,128)(2,1)S(1)} async-done(((bf16[16,160,128]{2,1,0:T(8,128)(2,1)}), bf16[16,160,128]{2,1,0:T(8,128)(2,1)S(1)}, u32[]{:S(2)}, u32[]{:S(2)}) %all-to-all-start.5) | async-done | bytes 655392 | tf_op jit(solution)/shard_map/all_to_all | solution.py:416
  165.6 2.2 %shard_map.216 = (bf16[1,128,1152]{2,1,0:T(8,128)(2,1)}, bf16[1,128,1152]{2,1,0:T(8,128)(2,1)}, bf16[1,128,1152]{2,1,0:T(8,128)(2,1)}, f32[1,1152]{1,0:T(1,128)}, f32[1,1152]{1,0:T(1,128)}) custom-call(bf16[16,160,128]{2,1,0:T(8,128)(2,1)S(1)} %all-to-all-done.5.got_ref, bf16[128,1152]{1,0:T(8,128)(2,1)} %get-tuple-element.69.early_ref, ...), custom_call_target="tpu_custom_call" | custom-call | flops 1000000 | bytes 2000000 | tf_op jit(solution)/shard_map/pallas_call | solution.py:608
  (18 shorter events, 0.1 us)
Async XLA Ops:
  0.6 13.5 %copy-start.13 = (bf16[1,144,1152]{2,1,0:T(8,128)(2,1)S(1)}, bf16[1,144,1152]{2,1,0:T(8,128)(2,1)}, u32[]{:S(2)}) copy-start(bf16[1,144,1152]{2,1,0:T(8,128)(2,1)} %refs_1_.1) | copy-start | bytes 995332
  0.7 23.2 %copy-start.3 = (bf16[1,128,1152]{2,1,0:T(8,128)(2,1)S(1)}, bf16[1,128,1152]{2,1,0:T(8,128)(2,1)}, u32[]{:S(2)}) copy-start(bf16[1,128,1152]{2,1,0:T(8,128)(2,1)} %g_ref.3) | copy-start | bytes 884740
  0.7 23.2 %copy-start.5 = (bf16[1,128,1152]{2,1,0:T(8,128)(2,1)S(1)}, bf16[1,128,1152]{2,1,0:T(8,128)(2,1)}, u32[]{:S(2)}) copy-start(bf16[1,128,1152]{2,1,0:T(8,128)(2,1)} %q_ref.3) | copy-start | bytes 884740
  0.7 23.2 %copy-start.6 = (bf16[1,128,1152]{2,1,0:T(8,128)(2,1)S(1)}, bf16[1,128,1152]{2,1,0:T(8,128)(2,1)}, u32[]{:S(2)}) copy-start(bf16[1,128,1152]{2,1,0:T(8,128)(2,1)} %x_ref.1) | copy-start | bytes 884740
  0.7 23.2 %copy-start.9 = (s32[1,1,16,1]{2,3,1,0:T(1,128)S(1)}, s32[1,1,16,1]{2,3,1,0:T(1,128)}, u32[]{:S(2)}) copy-start(s32[1,1,16,1]{2,3,1,0:T(1,128)} %param.20) | copy-start | bytes 196
  0.7 23.2 %copy-start.10 = (s32[1,1,16]{2,1,0:T(1,128)S(1)}, s32[1,1,16]{2,1,0:T(1,128)}, u32[]{:S(2)}) copy-start(s32[1,1,16]{2,1,0:T(1,128)} %cnt_ref.3) | copy-start | bytes 196
  0.7 23.2 %copy-start.11 = (bf16[1,1,16,1]{2,3,1,0:T(2,128)(2,1)S(1)}, bf16[1,1,16,1]{2,3,1,0:T(2,128)(2,1)}, u32[]{:S(2)}) copy-start(bf16[1,1,16,1]{2,3,1,0:T(2,128)(2,1)} %param.22) | copy-start | bytes 100
  3.1 29.3 %all-to-all-start = ((bf16[16,160,128]{2,1,0:T(8,128)(2,1)}), bf16[16,160,128]{2,1,0:T(8,128)(2,1)S(1)}, u32[]{:S(2)}, u32[]{:S(2)}) async-start(bf16[16,160,128]{2,1,0:T(8,128)(2,1)} %shard_map.204), calls=%async_computation | async-start | bytes 1310720 | tf_op jit(solution)/shard_map/all_to_all | solution.py:416
  15.2 14.3 %collective-permute-start = (bf16[208,1152]{1,0:T(8,128)(2,1)S(1)}, bf16[208,1152]{1,0:T(8,128)(2,1)S(1)}, u32[]{:S(2)}, u32[]{:S(2)}) collective-permute-start(bf16[208,1152]{1,0:T(8,128)(2,1)S(1)} %pad_maximum_fusion.1), channel_id=1, source_target_pairs={{0,64},{64,0},{1,65},{65,1},{2,66},{66,2},{3,67},{67,3},{4,68},{68... | collective-permute-start | bytes 1437704 | tf_op jit(solution)/shard_map/ppermute | solution.py:449
  17.6 7.5 %collective-permute-start.1 = (bf16[1,144,1152]{2,1,0:T(8,128)(2,1)}, bf16[1,144,1152]{2,1,0:T(8,128)(2,1)S(1)}, u32[]{:S(2)}, u32[]{:S(2)}) collective-permute-start(bf16[1,144,1152]{2,1,0:T(8,128)(2,1)} %refs_0_.1), channel_id=1, source_target_pairs={{0,16},{16,0},{1,17},{17,1},{2,18},{18,2},{3,19},{19,3},{4,20},{20... | collective-permute-start | bytes 995336 | tf_op jit(solution)/shard_map/ppermute | solution.py:449
  19.5 5.6 %collective-permute-start.3 = (bf16[1,144,1152]{2,1,0:T(8,128)(2,1)}, bf16[1,144,1152]{2,1,0:T(8,128)(2,1)S(1)}, u32[]{:S(2)}, u32[]{:S(2)}) collective-permute-start(bf16[1,144,1152]{2,1,0:T(8,128)(2,1)} %refs_2_.1), channel_id=1, source_target_pairs={{0,16},{16,0},{1,17},{17,1},{2,18},{18,2},{3,19},{19,3},{4,20},{20... | collective-permute-start | bytes 995336 | tf_op jit(solution)/shard_map/ppermute | solution.py:449
  21.9 3.5 %collective-permute-start.2 = (bf16[1,144,1152]{2,1,0:T(8,128)(2,1)S(1)}, bf16[1,144,1152]{2,1,0:T(8,128)(2,1)S(1)}, u32[]{:S(2)}, u32[]{:S(2)}) collective-permute-start(bf16[1,144,1152]{2,1,0:T(8,128)(2,1)S(1)} %copy-done.13), channel_id=1, source_target_pairs={{0,16},{16,0},{1,17},{17,1},{2,18},{18,2},{3,19},{19,3},{4,20},{20... | collective-permute-start | bytes 995336 | tf_op jit(solution)/shard_map/ppermute | solution.py:449
  25.1 9.8 %copy-start = (bf16[1,144,1152]{2,1,0:T(8,128)(2,1)}, bf16[1,144,1152]{2,1,0:T(8,128)(2,1)S(1)}, u32[]{:S(2)}) copy-start(bf16[1,144,1152]{2,1,0:T(8,128)(2,1)S(1)} %collective-permute-done.1.w_1.refs_3_) | copy-start | bytes 995332
  25.1 9.8 %copy-start.1 = (bf16[1,144,1152]{2,1,0:T(8,128)(2,1)}, bf16[1,144,1152]{2,1,0:T(8,128)(2,1)S(1)}, u32[]{:S(2)}) copy-start(bf16[1,144,1152]{2,1,0:T(8,128)(2,1)S(1)} %collective-permute-done.3.w_3.refs_5_) | copy-start | bytes 995332
  25.5 9.5 %copy-start.2 = (bf16[1,144,1152]{2,1,0:T(8,128)(2,1)}, bf16[1,144,1152]{2,1,0:T(8,128)(2,1)S(1)}, u32[]{:S(2)}) copy-start(bf16[1,144,1152]{2,1,0:T(8,128)(2,1)S(1)} %collective-permute-done.2.w_2.refs_4_) | copy-start | bytes 995332
  34.9 25.1 %copy-start.7 = (f32[1,1152]{1,0:T(1,128)S(1)}, f32[1,1152]{1,0:T(1,128)}, u32[]{:S(2)}) copy-start(f32[1,1152]{1,0:T(1,128)} %scale_ref.3) | copy-start | bytes 13828
  35.0 25.0 %all-to-all-start.1 = ((bf16[16,184,128]{2,1,0:T(8,128)(2,1)}), bf16[16,184,128]{2,1,0:T(8,128)(2,1)S(1)}, u32[]{:S(2)}, u32[]{:S(2)}) async-start(bf16[16,184,128]{2,1,0:T(8,128)(2,1)} %get-tuple-element.45), calls=%async_computation.1 | async-start | bytes 1507328 | tf_op jit(solution)/shard_map/all_to_all | solution.py:416
  41.0 14.9 %collective-permute-start.4 = (bf16[224,1152]{1,0:T(8,128)(2,1)S(1)}, bf16[224,1152]{1,0:T(8,128)(2,1)S(1)}, u32[]{:S(2)}, u32[]{:S(2)}) collective-permute-start(bf16[224,1152]{1,0:T(8,128)(2,1)S(1)} %pad_maximum_fusion), channel_id=1, source_target_pairs={{0,64},{64,0},{1,65},{65,1},{2,66},{66,2},{3,67},{67,3},{4,68},{68... | collective-permute-start | bytes 1548296 | tf_op jit(solution)/shard_map/ppermute | solution.py:449
  43.4 40.2 %collective-permute-start.5 = (bf16[208,1152]{1,0:T(8,128)(2,1)S(1)}, bf16[208,1152]{1,0:T(8,128)(2,1)}, u32[]{:S(2)}, u32[]{:S(2)}) collective-permute-start(bf16[208,1152]{1,0:T(8,128)(2,1)S(1)} %collective-permute-done.w_0.refs_6_), channel_id=1, source_target_pairs={{0,16},{16,0},{1,17},{17,1},{2,18},{18,2},{3,19},{19,3},{4,20},{20... | collective-permute-start | bytes 1437704 | tf_op jit(solution)/shard_map/ppermute | solution.py:449
  55.9 27.7 %collective-permute-start.6 = (bf16[224,1152]{1,0:T(8,128)(2,1)S(1)}, bf16[224,1152]{1,0:T(8,128)(2,1)S(1)}, u32[]{:S(2)}, u32[]{:S(2)}) collective-permute-start(bf16[224,1152]{1,0:T(8,128)(2,1)S(1)} %collective-permute-done.4.w_0.refs_7_), channel_id=1, source_target_pairs={{0,16},{16,0},{1,17},{17,1},{2,18},{18,2},{3,19},{19,3},{4,20},{20... | collective-permute-start | bytes 1548296 | tf_op jit(solution)/shard_map/ppermute | solution.py:449
  60.0 0.7 copy-start.8
  61.8 23.2 %all-to-all-start.2 = ((bf16[8,16,2432]{2,1,0:T(8,128)(2,1)}), bf16[8,16,2432]{2,1,0:T(8,128)(2,1)S(1)}, u32[]{:S(2)}, u32[]{:S(2)}) async-start(bf16[8,16,2432]{2,1,0:T(8,128)(2,1)} %get-tuple-element.46), calls=%async_computation.2 | async-start | bytes 1245184 | tf_op jit(solution)/shard_map/all_to_all | solution.py:416
  91.1 18.7 %all-to-all-start.3 = ((bf16[8,16,1280]{2,1,0:T(8,128)(2,1)}), bf16[8,16,1280]{2,1,0:T(8,128)(2,1)S(1)}, u32[]{:S(2)}, u32[]{:S(2)}) async-start(bf16[8,16,1280]{2,1,0:T(8,128)(2,1)} %get-tuple-element.49.refs_1_), calls=%async_computation.3 | async-start | bytes 655360 | tf_op jit(solution)/shard_map/all_to_all | solution.py:416
  112.2 22.9 %all-to-all-start.4 = ((bf16[16,104,128]{2,1,0:T(8,128)(2,1)}), bf16[16,104,128]{2,1,0:T(8,128)(2,1)S(1)}, u32[]{:S(2)}, u32[]{:S(2)}) async-start(bf16[16,104,128]{2,1,0:T(8,128)(2,1)} %get-tuple-element.61), calls=%async_computation.4 | async-start | bytes 851968 | tf_op jit(solution)/shard_map/all_to_all | solution.py:416
  118.3 8.7 %collective-permute-start.7 = (bf16[144,1152]{1,0:T(8,128)(2,1)}, bf16[144,1152]{1,0:T(8,128)(2,1)S(1)}, u32[]{:S(2)}, u32[]{:S(2)}) collective-permute-start(bf16[144,1152]{1,0:T(8,128)(2,1)} %get-tuple-element.65), channel_id=1, source_target_pairs={{0,16},{16,0},{1,17},{17,1},{2,18},{18,2},{3,19},{19,3},{4,20},{20... | collective-permute-start | bytes 995336 | tf_op jit(solution)/shard_map/ppermute | solution.py:449
  120.3 6.8 %collective-permute-start.8 = (bf16[144,1152]{1,0:T(8,128)(2,1)}, bf16[144,1152]{1,0:T(8,128)(2,1)S(1)}, u32[]{:S(2)}, u32[]{:S(2)}) collective-permute-start(bf16[144,1152]{1,0:T(8,128)(2,1)} %get-tuple-element.66), channel_id=1, source_target_pairs={{0,16},{16,0},{1,17},{17,1},{2,18},{18,2},{3,19},{19,3},{4,20},{20... | collective-permute-start | bytes 995336 | tf_op jit(solution)/shard_map/ppermute | solution.py:449
  122.7 4.4 %collective-permute-start.9 = (bf16[144,1152]{1,0:T(8,128)(2,1)}, bf16[144,1152]{1,0:T(8,128)(2,1)S(1)}, u32[]{:S(2)}, u32[]{:S(2)}) collective-permute-start(bf16[144,1152]{1,0:T(8,128)(2,1)} %get-tuple-element.67), channel_id=1, source_target_pairs={{0,16},{16,0},{1,17},{17,1},{2,18},{18,2},{3,19},{19,3},{4,20},{20... | collective-permute-start | bytes 995336 | tf_op jit(solution)/shard_map/ppermute | solution.py:449
  124.6 24.6 %collective-permute-start.10 = (bf16[3,144,1152]{2,1,0:T(8,128)(2,1)}, bf16[3,144,1152]{2,1,0:T(8,128)(2,1)}, u32[]{:S(2)}, u32[]{:S(2)}) collective-permute-start(bf16[3,144,1152]{2,1,0:T(8,128)(2,1)} %get-tuple-element.76), channel_id=1, source_target_pairs={{0,16},{16,0},{1,17},{17,1},{2,18},{18,2},{3,19},{19,3},{4,20},{20... | collective-permute-start | bytes 2985992 | tf_op jit(solution)/shard_map/ppermute | solution.py:449
  129.5 28.1 %collective-permute-start.11 = (bf16[3,144,1152]{2,1,0:T(8,128)(2,1)}, bf16[3,144,1152]{2,1,0:T(8,128)(2,1)}, u32[]{:S(2)}, u32[]{:S(2)}) collective-permute-start(bf16[3,144,1152]{2,1,0:T(8,128)(2,1)} %shard_map.213.near), channel_id=1, source_target_pairs={{0,64},{64,0},{1,65},{65,1},{2,66},{66,2},{3,67},{67,3},{4,68},{68... | collective-permute-start | bytes 2985992 | tf_op jit(solution)/shard_map/ppermute | solution.py:449
  135.2 12.3 %copy-start.4 = (bf16[1,128,1152]{2,1,0:T(8,128)(2,1)S(1)}, bf16[1,128,1152]{2,1,0:T(8,128)(2,1)}, u32[]{:S(2)}) copy-start(bf16[1,128,1152]{2,1,0:T(8,128)(2,1)} %g_ref.3) | copy-start | bytes 884740
  139.2 18.4 %copy-start.12 = (bf16[2,3,144,1152]{3,2,1,0:T(8,128)(2,1)S(1)}, bf16[2,3,144,1152]{3,2,1,0:T(8,128)(2,1)}, u32[]{:S(2)}) copy-start(bf16[2,3,144,1152]{3,2,1,0:T(8,128)(2,1)} %get-tuple-element.64.own_ref) | copy-start | bytes 5971972
  139.2 26.4 %all-to-all-start.5 = ((bf16[16,160,128]{2,1,0:T(8,128)(2,1)}), bf16[16,160,128]{2,1,0:T(8,128)(2,1)S(1)}, u32[]{:S(2)}, u32[]{:S(2)}) async-start(bf16[16,160,128]{2,1,0:T(8,128)(2,1)} %shard_map.214), calls=%async_computation.5 | async-start | bytes 1310720 | tf_op jit(solution)/shard_map/all_to_all | solution.py:416

commit v4 on v3

--- a/solution.py
+++ b/solution.py
@@ -340,7 +340,7 @@
     sums_ref[HEAD:, :] += mm(scaled[HEAD:].astype(BF), expo_b, NN)
 
 
-def late_kernel(got_ref, kv_in_ref, query_ref, att_ref, sums_ref, near, sent_ref):
+def late_kernel(got_ref, kv_in_ref, query_ref, att_ref, sums_ref, near, _, sent_ref, others):
     experts = got_ref.shape[0]
     frames = sent_ref.shape[0]
     total = experts * frames
@@ -584,22 +584,24 @@
         out_specs=[whole((3,) + grad_shape)],
     )(*hbm(own), *far_got)
     got_near = across(own_near, "yl")
-    got_core = across(others[0], "core")
+
+    late_sent, kept = call(
+        late_kernel,
+        [pltpu.HBM((frames, body + experts, tokens), BF), pltpu.HBM((3,) + grad_shape, BF)],
+        grid=(1,),
+        in_specs=[whole((experts, 2 * frames, LANES))]
+        + [whole(a.shape) for a in (keys_got, slot_query, att)]
+        + [whole((body, length)), ANY, ANY],
+        input_output_aliases={6: 1},
+        out_specs=[whole((frames, body + experts, tokens)), ANY],
+    )(delta_got, keys_got, *hbm(slot_query, att, sums, own_near, others[0]))
+    late_got = swap(late_sent, SEQ)
+    got_core = across(kept, "core")
     w_grads = [
         (own[0, i].astype(F32) + got_core[i].astype(F32) + got_near[i].astype(F32)).astype(BF)[None]
         for i in range(3)
     ]
 
-    (late_sent,) = call(
-        late_kernel,
-        [pltpu.HBM((frames, body + experts, tokens), BF)],
-        grid=(1,),
-        in_specs=[whole((experts, 2 * frames, LANES))]
-        + [whole(a.shape) for a in (keys_got, slot_query, att)]
-        + [whole((body, length)), ANY],
-        out_specs=[whole((frames, body + experts, tokens))],
-    )(delta_got, keys_got, *hbm(slot_query, att, sums, own_near))
-    late_got = swap(late_sent, SEQ)
 
     block_shape = jax.ShapeDtypeStruct((1, tokens, width), BF)
     input_grad, query_early = call(inputs_kernel, [block_shape, pltpu.HBM((tokens, width), BF)])(

time: 169 us -> 172 us (1.018)
  waiting for transfers between devices: 35.3 us -> 38.5 us
    all_to_all x6, waiting for transfers between devices: 11.9 us -> 15 us  [swap(): return lax.all_to_all(block, axes, split_axis=0, concat_axis=0, tiled=True)]
  transfers between devices with their start and end apart: 18 -> 18, of which waited for: 9 -> 10; matrix products, arithmetic and copies ran while one was open for 3% -> 3% of each run, Pallas kernels for 20% -> 20%
where the time goes in v4:
time: 172 us; the launch traced here: 170 us
  starting transfers between devices  76.5 us (44%)
  Pallas kernels  48.9 us (28%)
  waiting for transfers between devices  38.5 us (22%)
  other arithmetic  4.7 us (3%)
    all_to_all x6, starting transfers between devices, swap(): return lax.all_to_all(block, axes, split_axis=0, concat_axis=0, tiled=True)  47.7 us
    ppermute x12, starting transfers between devices, across(): return lax.ppermute(block, axis, other)  28.8 us
    ppermute x12, waiting for transfers between devices, across(): return lax.ppermute(block, axis, other)  23.5 us
    pallas_call x2, Pallas kernels, early(): call(functools.partial(attention_kernel, started), early_outs, flops=4000...  18.8 us
    all_to_all x6, waiting for transfers between devices, swap(): return lax.all_to_all(block, axes, split_axis=0, concat_axis=0, tiled=True)  15 us
    pallas_call x1, Pallas kernels, shards(): call(expert_kernel, [pltpu.HBM((groups, frames, width + LANES), BF)] + [p...  6.12 us
    pallas_call x1, Pallas kernels, shards(): call(weight_grads_kernel, [pltpu.HBM((2, 3) + grad_shape, BF), pltpu.HBM(...  4.09 us
    pallas_call x1, Pallas kernels, shards(): call(late_kernel, [pltpu.HBM((frames, body + experts, tokens), BF), pltpu...  3.97 us
  transfers between devices with their start and end apart: 18, of which 10 were waited for; matrix products, arithmetic and copies ran while one was open for 3% of the time, Pallas kernels for 20%

profile of v4, /device:TPU:12, one launch (start us, length us, event | category | flops | bytes accessed | tf_op | source)
XLA Modules:
  0.0 170.4 jit_solution(6159098021510580798)
XLA Ops:
  0.6 0.0 copy-start.13
  0.7 0.0 copy-start.3
  0.7 0.0 copy-start.5
  0.7 0.0 copy-start.6
  0.7 0.0 copy-start.9
  0.7 0.0 copy-start.10
  0.7 2.4 %shard_map.204 = bf16[16,160,128]{2,1,0:T(8,128)(2,1)} custom-call(bf16[1,128,1152]{2,1,0:T(8,128)(2,1)} %q_ref.3, bf16[1,128,1152]{2,1,0:T(8,128)(2,1)} %k_ref.1, bf16[1,128,1152]{2,1,0:T(8,128)(2,1)} %v_ref.1, s32[1,1,16]{2,1,0:T(1,128)} %bitcast.18, s32[1,1,16]{2,1,0:T(1,128)} %cnt_ref.3), custom_call_target="tpu_custom_call" | custom-call | flops 1000000 | bytes 2000000 | tf_op jit(solution)/shard_map/pallas_call | solution.py:458
  3.1 11.1 %all-to-all-start = ((bf16[16,160,128]{2,1,0:T(8,128)(2,1)}), bf16[16,160,128]{2,1,0:T(8,128)(2,1)S(1)}, u32[]{:S(2)}, u32[]{:S(2)}) async-start(bf16[16,160,128]{2,1,0:T(8,128)(2,1)} %shard_map.204), calls=%async_computation | async-start | bytes 1310720 | tf_op jit(solution)/shard_map/all_to_all | solution.py:416
  14.2 1.0 pad_maximum_fusion.1
  15.2 2.4 %collective-permute-start = (bf16[208,1152]{1,0:T(8,128)(2,1)S(1)}, bf16[208,1152]{1,0:T(8,128)(2,1)S(1)}, u32[]{:S(2)}, u32[]{:S(2)}) collective-permute-start(bf16[208,1152]{1,0:T(8,128)(2,1)S(1)} %pad_maximum_fusion.1), channel_id=1, source_target_pairs={{0,64},{64,0},{1,65},{65,1},{2,66},{66,2},{3,67},{67,3},{4,68},{68... | collective-permute-start | bytes 1437704 | tf_op jit(solution)/shard_map/ppermute | solution.py:449
  17.6 1.9 %collective-permute-start.1 = (bf16[1,144,1152]{2,1,0:T(8,128)(2,1)}, bf16[1,144,1152]{2,1,0:T(8,128)(2,1)S(1)}, u32[]{:S(2)}, u32[]{:S(2)}) collective-permute-start(bf16[1,144,1152]{2,1,0:T(8,128)(2,1)} %refs_0_.1), channel_id=1, source_target_pairs={{0,16},{16,0},{1,17},{17,1},{2,18},{18,2},{3,19},{19,3},{4,20},{20... | collective-permute-start | bytes 995336 | tf_op jit(solution)/shard_map/ppermute | solution.py:449
  19.5 2.4 %collective-permute-start.3 = (bf16[1,144,1152]{2,1,0:T(8,128)(2,1)}, bf16[1,144,1152]{2,1,0:T(8,128)(2,1)S(1)}, u32[]{:S(2)}, u32[]{:S(2)}) collective-permute-start(bf16[1,144,1152]{2,1,0:T(8,128)(2,1)} %refs_2_.1), channel_id=1, source_target_pairs={{0,16},{16,0},{1,17},{17,1},{2,18},{18,2},{3,19},{19,3},{4,20},{20... | collective-permute-start | bytes 995336 | tf_op jit(solution)/shard_map/ppermute | solution.py:449
  21.9 1.9 %collective-permute-start.2 = (bf16[1,144,1152]{2,1,0:T(8,128)(2,1)S(1)}, bf16[1,144,1152]{2,1,0:T(8,128)(2,1)S(1)}, u32[]{:S(2)}, u32[]{:S(2)}) collective-permute-start(bf16[1,144,1152]{2,1,0:T(8,128)(2,1)S(1)} %copy-done.13), channel_id=1, source_target_pairs={{0,16},{16,0},{1,17},{17,1},{2,18},{18,2},{3,19},{19,3},{4,20},{20... | collective-permute-start | bytes 995336 | tf_op jit(solution)/shard_map/ppermute | solution.py:449
  23.9 1.2 shard_map.205
  25.1 0.0 collective-permute-done.1.w_1.refs_3_
  25.1 0.0 collective-permute-done.3.w_3.refs_5_
  25.1 0.0 copy-start.1
  25.2 0.3 collective-permute-done.2.w_2.refs_4_
  25.5 4.1 %collective-permute-done.w_0.refs_6_ = bf16[208,1152]{1,0:T(8,128)(2,1)S(1)} collective-permute-done((bf16[208,1152]{1,0:T(8,128)(2,1)S(1)}, bf16[208,1152]{1,0:T(8,128)(2,1)S(1)}, u32[]{:S(2)}, u32[]{:S(2)}) %collective-permute-start) | collective-permute-done | bytes 479264 | tf_op jit(solution)/shard_map/ppermute | solution.py:449
  29.5 2.8 %all-to-all-done.got_ref.kv_in_ref = bf16[16,160,128]{2,1,0:T(8,128)(2,1)S(1)} async-done(((bf16[16,160,128]{2,1,0:T(8,128)(2,1)}), bf16[16,160,128]{2,1,0:T(8,128)(2,1)S(1)}, u32[]{:S(2)}, u32[]{:S(2)}) %all-to-all-start) | async-done | bytes 655392 | tf_op jit(solution)/shard_map/all_to_all | solution.py:416
  32.4 2.5 %shard_map.206 = (bf16[16,184,128]{2,1,0:T(8,128)(2,1)}, bf16[16,16,128]{2,1,0:T(8,128)(2,1)}, bf16[256,128]{1,0:T(8,128)(2,1)}) custom-call(bf16[16,160,128]{2,1,0:T(8,128)(2,1)S(1)} %all-to-all-done.got_ref.kv_in_ref, bf16[16,184,128]{2,1,0:T(8,128)(2,1)} %get-tuple-element.46._, ...), custom_call_target="tpu_custom_call", output_to_operand_aliasing={{0}: (1, {})} | custom-call | flops 1000000 | bytes 2000000 | tf_op jit(solution)/shard_map/pallas_call | solution.py:467
  34.9 0.0 copy-start.7
  35.0 5.0 %all-to-all-start.1 = ((bf16[16,184,128]{2,1,0:T(8,128)(2,1)}), bf16[16,184,128]{2,1,0:T(8,128)(2,1)S(1)}, u32[]{:S(2)}, u32[]{:S(2)}) async-start(bf16[16,184,128]{2,1,0:T(8,128)(2,1)} %get-tuple-element.47), calls=%async_computation.1 | async-start | bytes 1507328 | tf_op jit(solution)/shard_map/all_to_all | solution.py:416
  40.0 1.0 pad_maximum_fusion
  41.0 2.4 %collective-permute-start.4 = (bf16[224,1152]{1,0:T(8,128)(2,1)S(1)}, bf16[224,1152]{1,0:T(8,128)(2,1)S(1)}, u32[]{:S(2)}, u32[]{:S(2)}) collective-permute-start(bf16[224,1152]{1,0:T(8,128)(2,1)S(1)} %pad_maximum_fusion), channel_id=1, source_target_pairs={{0,64},{64,0},{1,65},{65,1},{2,66},{66,2},{3,67},{67,3},{4,68},{68... | collective-permute-start | bytes 1548296 | tf_op jit(solution)/shard_map/ppermute | solution.py:449
  43.4 1.9 %collective-permute-start.5 = (bf16[208,1152]{1,0:T(8,128)(2,1)S(1)}, bf16[208,1152]{1,0:T(8,128)(2,1)}, u32[]{:S(2)}, u32[]{:S(2)}) collective-permute-start(bf16[208,1152]{1,0:T(8,128)(2,1)S(1)} %collective-permute-done.w_0.refs_6_), channel_id=1, source_target_pairs={{0,16},{16,0},{1,17},{17,1},{2,18},{18,2},{3,19},{19,3},{4,20},{20... | collective-permute-start | bytes 1437704 | tf_op jit(solution)/shard_map/ppermute | solution.py:449
  45.3 10.6 %collective-permute-done.4.w_0.refs_7_ = bf16[224,1152]{1,0:T(8,128)(2,1)S(1)} collective-permute-done((bf16[224,1152]{1,0:T(8,128)(2,1)S(1)}, bf16[224,1152]{1,0:T(8,128)(2,1)S(1)}, u32[]{:S(2)}, u32[]{:S(2)}) %collective-permute-start.4) | collective-permute-done | bytes 516128 | tf_op jit(solution)/shard_map/ppermute | solution.py:449
  55.9 1.9 %collective-permute-start.6 = (bf16[224,1152]{1,0:T(8,128)(2,1)S(1)}, bf16[224,1152]{1,0:T(8,128)(2,1)S(1)}, u32[]{:S(2)}, u32[]{:S(2)}) collective-permute-start(bf16[224,1152]{1,0:T(8,128)(2,1)S(1)} %collective-permute-done.4.w_0.refs_7_), channel_id=1, source_target_pairs={{0,16},{16,0},{1,17},{17,1},{2,18},{18,2},{3,19},{19,3},{4,20},{20... | collective-permute-start | bytes 1548296 | tf_op jit(solution)/shard_map/ppermute | solution.py:449
  57.8 2.2 %all-to-all-done.1.got_ref.qg_ref = bf16[16,184,128]{2,1,0:T(8,128)(2,1)S(1)} async-done(((bf16[16,184,128]{2,1,0:T(8,128)(2,1)}), bf16[16,184,128]{2,1,0:T(8,128)(2,1)S(1)}, u32[]{:S(2)}, u32[]{:S(2)}) %all-to-all-start.1) | async-done | bytes 753696 | tf_op jit(solution)/shard_map/all_to_all | solution.py:416
  60.0 0.0 copy-done.7
  60.0 0.7 copy-done.8
  60.7 1.1 shard_map.207
  61.8 9.2 %all-to-all-start.2 = ((bf16[8,16,2432]{2,1,0:T(8,128)(2,1)}), bf16[8,16,2432]{2,1,0:T(8,128)(2,1)S(1)}, u32[]{:S(2)}, u32[]{:S(2)}) async-start(bf16[8,16,2432]{2,1,0:T(8,128)(2,1)} %get-tuple-element.48), calls=%async_computation.2 | async-start | bytes 1245184 | tf_op jit(solution)/shard_map/all_to_all | solution.py:416
  71.0 12.6 %shard_map.208 = (bf16[16,104,128]{2,1,0:T(8,128)(2,1)}, f32[144,2048]{1,0:T(8,128)}) custom-call(bf16[16,160,128]{2,1,0:T(8,128)(2,1)S(1)} %all-to-all-done.got_ref.kv_in_ref, bf16[16,184,128]{2,1,0:T(8,128)(2,1)S(1)} %all-to-all-done.1.got_ref.qg_ref, f32[16,128]{1,0:T(8,128)} %get-tuple-element.49.refs_0_.inv_ref), custom_call_target="tpu_custom_call" | custom-call | flops 120000004096 | bytes 2000000 | tf_op jit(solution)/shard_map/pallas_call | solution.py:503
  83.6 0.0 collective-permute-done.5.refs_8_
  83.6 0.0 collective-permute-done.6.refs_9_
  83.6 1.4 all-to-all-done.2.rows_ref
  85.0 6.1 %shard_map.209 = (bf16[8,16,1280]{2,1,0:T(8,128)(2,1)}, bf16[4,128,144]{2,1,0:T(8,128)(2,1)}, bf16[4,128,144]{2,1,0:T(8,128)(2,1)}, bf16[4,128,144]{2,1,0:T(8,128)(2,1)}) custom-call(bf16[8,16,2432]{2,1,0:T(8,128)(2,1)S(1)} %all-to-all-done.2.rows_ref, bf16[1,144,1152]{2,1,0:T(8,128)(2,1)} %refs_0_.1, bf16[1,144,1152]{2,1,0:T(8,128)(2,1)} %refs_1_.1, ...), custom_call_target="tpu_custom_call" | custom-call | flops 1000000 | bytes 2000000 | tf_op jit(solution)/shard_map/pallas_call | solution.py:524
  91.1 8.3 %all-to-all-start.3 = ((bf16[8,16,1280]{2,1,0:T(8,128)(2,1)}), bf16[8,16,1280]{2,1,0:T(8,128)(2,1)S(1)}, u32[]{:S(2)}, u32[]{:S(2)}) async-start(bf16[8,16,1280]{2,1,0:T(8,128)(2,1)} %get-tuple-element.51.refs_1_), calls=%async_computation.3 | async-start | bytes 655360 | tf_op jit(solution)/shard_map/all_to_all | solution.py:416
  99.4 6.1 %shard_map.210 = (bf16[16,104,128]{2,1,0:T(8,128)(2,1)}, f32[144,2048]{1,0:T(8,128)}) custom-call(bf16[16,160,128]{2,1,0:T(8,128)(2,1)S(1)} %all-to-all-done.got_ref.kv_in_ref, bf16[16,184,128]{2,1,0:T(8,128)(2,1)S(1)} %all-to-all-done.1.got_ref.qg_ref, bf16[16,104,128]{2,1,0:T(8,128)(2,1)} %get-tuple-element.53.refs_0_, ...), custom_call_target="tpu_custom_call", output_to_operand_aliasing={{0}: (2, {})} | custom-call | flops 40000000000 | bytes 2000000 | tf_op jit(solution)/shard_map/pallas_call | solution.py:503
  105.6 4.1 %shard_map.211 = (bf16[2,3,144,1152]{3,2,1,0:T(8,128)(2,1)}, bf16[3,144,1152]{2,1,0:T(8,128)(2,1)}, bf16[144,1152]{1,0:T(8,128)(2,1)}, bf16[144,1152]{1,0:T(8,128)(2,1)}, bf16[144,1152]{1,0:T(8,128)(2,1)}) custom-call(bf16[8,16,2432]{2,1,0:T(8,128)(2,1)S(1)} %all-to-all-done.2.rows_ref, bf16[4,128,144]{2,1,0:T(8,128)(2,1)} %get-tuple-element.55.hidden_ref, ...), custom_call_target="tpu_custom_call" | custom-call | flops 1000000 | bytes 2000000 | tf_op jit(solution)/shard_map/pallas_call | solution.py:546
  109.6 0.2 all-to-all-done.3.got_ref
  109.9 2.3 %shard_map.212 = (bf16[16,104,128]{2,1,0:T(8,128)(2,1)}, f32[1,1,16]{2,1,0:T(1,128)}, bf16[3,144,1152]{2,1,0:T(8,128)(2,1)}, bf16[144,1152]{1,0:T(8,128)(2,1)}, ...) custom-call(bf16[8,16,1280]{2,1,0:T(8,128)(2,1)S(1)} %all-to-all-don, ...), custom_call_target="tpu_custom_call", output_to_operand_aliasing={{0}: (4, {}), {2}: (5, {}), {3}: (6, {}), {4}: (7, {}), {5}... | custom-call | flops 1000000 | bytes 2000000 | tf_op jit(solution)/shard_map/pallas_call | solution.py:553
  112.2 6.1 %all-to-all-start.4 = ((bf16[16,104,128]{2,1,0:T(8,128)(2,1)}), bf16[16,104,128]{2,1,0:T(8,128)(2,1)S(1)}, u32[]{:S(2)}, u32[]{:S(2)}) async-start(bf16[16,104,128]{2,1,0:T(8,128)(2,1)} %get-tuple-element.63), calls=%async_computation.4 | async-start | bytes 851968 | tf_op jit(solution)/shard_map/all_to_all | solution.py:416
  118.3 1.9 %collective-permute-start.7 = (bf16[144,1152]{1,0:T(8,128)(2,1)}, bf16[144,1152]{1,0:T(8,128)(2,1)S(1)}, u32[]{:S(2)}, u32[]{:S(2)}) collective-permute-start(bf16[144,1152]{1,0:T(8,128)(2,1)} %get-tuple-element.67), channel_id=1, source_target_pairs={{0,16},{16,0},{1,17},{17,1},{2,18},{18,2},{3,19},{19,3},{4,20},{20... | collective-permute-start | bytes 995336 | tf_op jit(solution)/shard_map/ppermute | solution.py:449
  120.2 2.4 %collective-permute-start.8 = (bf16[144,1152]{1,0:T(8,128)(2,1)}, bf16[144,1152]{1,0:T(8,128)(2,1)S(1)}, u32[]{:S(2)}, u32[]{:S(2)}) collective-permute-start(bf16[144,1152]{1,0:T(8,128)(2,1)} %get-tuple-element.68), channel_id=1, source_target_pairs={{0,16},{16,0},{1,17},{17,1},{2,18},{18,2},{3,19},{19,3},{4,20},{20... | collective-permute-start | bytes 995336 | tf_op jit(solution)/shard_map/ppermute | solution.py:449
  122.7 1.9 %collective-permute-start.9 = (bf16[144,1152]{1,0:T(8,128)(2,1)}, bf16[144,1152]{1,0:T(8,128)(2,1)S(1)}, u32[]{:S(2)}, u32[]{:S(2)}) collective-permute-start(bf16[144,1152]{1,0:T(8,128)(2,1)} %get-tuple-element.69), channel_id=1, source_target_pairs={{0,16},{16,0},{1,17},{17,1},{2,18},{18,2},{3,19},{19,3},{4,20},{20... | collective-permute-start | bytes 995336 | tf_op jit(solution)/shard_map/ppermute | solution.py:449
  124.6 0.0 collective-permute-done.7.got_0
  124.6 0.0 collective-permute-done.8.got_1
  124.6 1.8 %collective-permute-done.9.got_2 = bf16[144,1152]{1,0:T(8,128)(2,1)S(1)} collective-permute-done((bf16[144,1152]{1,0:T(8,128)(2,1)}, bf16[144,1152]{1,0:T(8,128)(2,1)S(1)}, u32[]{:S(2)}, u32[]{:S(2)}) %collective-permute-start.9) | collective-permute-done | bytes 331808 | tf_op jit(solution)/shard_map/ppermute | solution.py:449
  126.4 2.4 %shard_map.213.near = bf16[3,144,1152]{2,1,0:T(8,128)(2,1)} custom-call(bf16[2,3,144,1152]{3,2,1,0:T(8,128)(2,1)} %get-tuple-element.66.own_ref, bf16[144,1152]{1,0:T(8,128)(2,1)S(1)} %collective-permute-done.7.got_0, bf16[144,1152]{1,0:T(8,128)(2,1)S(1)} %collective-permute-done.8.got_1, bf16[144,1152]{1,0:T(8,128)(2,1)S(1)} %collective-permute-done.9.got_2), custom_call_target="tpu_custom_call" | custom-call | flops 1000000 | bytes 2000000 | tf_op jit(solution)/shard_map/pallas_call | solution.py:578
  128.8 5.7 %collective-permute-start.11 = (bf16[3,144,1152]{2,1,0:T(8,128)(2,1)}, bf16[3,144,1152]{2,1,0:T(8,128)(2,1)}, u32[]{:S(2)}, u32[]{:S(2)}) collective-permute-start(bf16[3,144,1152]{2,1,0:T(8,128)(2,1)} %shard_map.213.near), channel_id=1, source_target_pairs={{0,64},{64,0},{1,65},{65,1},{2,66},{66,2},{3,67},{67,3},{4,68},{68... | collective-permute-start | bytes 2985992 | tf_op jit(solution)/shard_map/ppermute | solution.py:449
  134.5 0.0 all-to-all-done.4.got_ref
  134.5 0.0 copy-start.4
  134.5 4.0 %shard_map.214 = (bf16[16,160,128]{2,1,0:T(8,128)(2,1)}, bf16[3,144,1152]{2,1,0:T(8,128)(2,1)}) custom-call(bf16[16,104,128]{2,1,0:T(8,128)(2,1)S(1)} %all-to-all-done.4.got_ref, bf16[16,160,128]{2,1,0:T(8,128)(2,1)S(1)} %all-to-all-done.got_ref.kv_in_ref, bf16[256,128]{1,0:T(8,128)(2,1)} %get-tuple-element.64.query_ref, ...), custom_call_target="tpu_custom_call", output_to_operand_aliasing={{1}: (6, {})} | custom-call | flops 1000000 | bytes 2000000 | tf_op jit(solution)/shard_map/pallas_call | solution.py:588
  138.5 2.0 %collective-permute-start.10 = (bf16[3,144,1152]{2,1,0:T(8,128)(2,1)}, bf16[3,144,1152]{2,1,0:T(8,128)(2,1)}, u32[]{:S(2)}, u32[]{:S(2)}) collective-permute-start(bf16[3,144,1152]{2,1,0:T(8,128)(2,1)} %get-tuple-element.80), channel_id=1, source_target_pairs={{0,16},{16,0},{1,17},{17,1},{2,18},{18,2},{3,19},{19,3},{4,20},{20... | collective-permute-start | bytes 2985992 | tf_op jit(solution)/shard_map/ppermute | solution.py:449
  140.6 8.1 %all-to-all-start.5 = ((bf16[16,160,128]{2,1,0:T(8,128)(2,1)}), bf16[16,160,128]{2,1,0:T(8,128)(2,1)S(1)}, u32[]{:S(2)}, u32[]{:S(2)}) async-start(bf16[16,160,128]{2,1,0:T(8,128)(2,1)} %get-tuple-element.71), calls=%async_computation.5 | async-start | bytes 1310720 | tf_op jit(solution)/shard_map/all_to_all | solution.py:416
  148.7 1.7 %shard_map.215 = (bf16[1,128,1152]{2,1,0:T(8,128)(2,1)}, bf16[128,1152]{1,0:T(8,128)(2,1)}) custom-call(bf16[16,104,128]{2,1,0:T(8,128)(2,1)S(1)} %all-to-all-done.4.got_ref, bf16[1,128,1152]{2,1,0:T(8,128)(2,1)S(1)} %copy-done.4, bf16[16,128]{1,0:T(8,128)(2,1)} %get-tuple-element.72.sel_ref), custom_call_target="tpu_custom_call" | custom-call | flops 1000000 | bytes 2000000 | tf_op jit(solution)/shard_map/pallas_call | solution.py:607
  150.4 6.7 %collective-permute-done.11 = bf16[3,144,1152]{2,1,0:T(8,128)(2,1)} collective-permute-done((bf16[3,144,1152]{2,1,0:T(8,128)(2,1)}, bf16[3,144,1152]{2,1,0:T(8,128)(2,1)}, u32[]{:S(2)}, u32[]{:S(2)}) %collective-permute-start.11) | collective-permute-done | bytes 995360 | tf_op jit(solution)/shard_map/ppermute | solution.py:449
  157.1 0.0 collective-permute-done.10
  157.1 0.0 copy-done.12
  157.1 2.7 %fusion.1 = (bf16[1,144,1152]{2,1,0:T(8,128)(2,1)}, bf16[1,144,1152]{2,1,0:T(8,128)(2,1)}, bf16[1,144,1152]{2,1,0:T(8,128)(2,1)}) fusion(bf16[3,144,1152]{2,1,0:T(8,128)(2,1)} %collective-permute-done.11, bf16[3,144,1152]{2,1,0:T(8,128)(2,1)} %collective-permute-done.10, bf16[2,3,144,1152]{3,2,1,0:T(8,128)(2,1)S(1)} %copy-done.12), kind=kLoop, calls=%fused_computation.2 | loop fusion | flops 2985984 | bytes 3981312 | tf_op jit(solution)/shard_map/convert_element_type | solution.py:601
  159.8 8.4 %all-to-all-done.5.got_ref = bf16[16,160,128]{2,1,0:T(8,128)(2,1)S(1)} async-done(((bf16[16,160,128]{2,1,0:T(8,128)(2,1)}), bf16[16,160,128]{2,1,0:T(8,128)(2,1)S(1)}, u32[]{:S(2)}, u32[]{:S(2)}) %all-to-all-start.5) | async-done | bytes 655392 | tf_op jit(solution)/shard_map/all_to_all | solution.py:416
  168.2 2.2 %shard_map.216 = (bf16[1,128,1152]{2,1,0:T(8,128)(2,1)}, bf16[1,128,1152]{2,1,0:T(8,128)(2,1)}, bf16[1,128,1152]{2,1,0:T(8,128)(2,1)}, f32[1,1152]{1,0:T(1,128)}, f32[1,1152]{1,0:T(1,128)}) custom-call(bf16[16,160,128]{2,1,0:T(8,128)(2,1)S(1)} %all-to-all-done.5.got_ref, bf16[128,1152]{1,0:T(8,128)(2,1)} %get-tuple-element.73.early_ref, ...), custom_call_target="tpu_custom_call" | custom-call | flops 1000000 | bytes 2000000 | tf_op jit(solution)/shard_map/pallas_call | solution.py:610
  (18 shorter events, 0.1 us)
Async XLA Ops:
  0.6 13.5 %copy-start.13 = (bf16[1,144,1152]{2,1,0:T(8,128)(2,1)S(1)}, bf16[1,144,1152]{2,1,0:T(8,128)(2,1)}, u32[]{:S(2)}) copy-start(bf16[1,144,1152]{2,1,0:T(8,128)(2,1)} %refs_1_.1) | copy-start | bytes 995332
  0.7 23.2 %copy-start.3 = (bf16[1,128,1152]{2,1,0:T(8,128)(2,1)S(1)}, bf16[1,128,1152]{2,1,0:T(8,128)(2,1)}, u32[]{:S(2)}) copy-start(bf16[1,128,1152]{2,1,0:T(8,128)(2,1)} %g_ref.3) | copy-start | bytes 884740
  0.7 23.2 %copy-start.5 = (bf16[1,128,1152]{2,1,0:T(8,128)(2,1)S(1)}, bf16[1,128,1152]{2,1,0:T(8,128)(2,1)}, u32[]{:S(2)}) copy-start(bf16[1,128,1152]{2,1,0:T(8,128)(2,1)} %q_ref.3) | copy-start | bytes 884740
  0.7 23.2 %copy-start.6 = (bf16[1,128,1152]{2,1,0:T(8,128)(2,1)S(1)}, bf16[1,128,1152]{2,1,0:T(8,128)(2,1)}, u32[]{:S(2)}) copy-start(bf16[1,128,1152]{2,1,0:T(8,128)(2,1)} %x_ref.1) | copy-start | bytes 884740
  0.7 23.2 %copy-start.9 = (s32[1,1,16,1]{2,3,1,0:T(1,128)S(1)}, s32[1,1,16,1]{2,3,1,0:T(1,128)}, u32[]{:S(2)}) copy-start(s32[1,1,16,1]{2,3,1,0:T(1,128)} %param.20) | copy-start | bytes 196
  0.7 23.2 %copy-start.10 = (s32[1,1,16]{2,1,0:T(1,128)S(1)}, s32[1,1,16]{2,1,0:T(1,128)}, u32[]{:S(2)}) copy-start(s32[1,1,16]{2,1,0:T(1,128)} %cnt_ref.3) | copy-start | bytes 196
  0.7 23.2 %copy-start.11 = (bf16[1,1,16,1]{2,3,1,0:T(2,128)(2,1)S(1)}, bf16[1,1,16,1]{2,3,1,0:T(2,128)(2,1)}, u32[]{:S(2)}) copy-start(bf16[1,1,16,1]{2,3,1,0:T(2,128)(2,1)} %param.22) | copy-start | bytes 100
  3.1 29.3 %all-to-all-start = ((bf16[16,160,128]{2,1,0:T(8,128)(2,1)}), bf16[16,160,128]{2,1,0:T(8,128)(2,1)S(1)}, u32[]{:S(2)}, u32[]{:S(2)}) async-start(bf16[16,160,128]{2,1,0:T(8,128)(2,1)} %shard_map.204), calls=%async_computation | async-start | bytes 1310720 | tf_op jit(solution)/shard_map/all_to_all | solution.py:416
  15.2 14.3 %collective-permute-start = (bf16[208,1152]{1,0:T(8,128)(2,1)S(1)}, bf16[208,1152]{1,0:T(8,128)(2,1)S(1)}, u32[]{:S(2)}, u32[]{:S(2)}) collective-permute-start(bf16[208,1152]{1,0:T(8,128)(2,1)S(1)} %pad_maximum_fusion.1), channel_id=1, source_target_pairs={{0,64},{64,0},{1,65},{65,1},{2,66},{66,2},{3,67},{67,3},{4,68},{68... | collective-permute-start | bytes 1437704 | tf_op jit(solution)/shard_map/ppermute | solution.py:449
  17.6 7.6 %collective-permute-start.1 = (bf16[1,144,1152]{2,1,0:T(8,128)(2,1)}, bf16[1,144,1152]{2,1,0:T(8,128)(2,1)S(1)}, u32[]{:S(2)}, u32[]{:S(2)}) collective-permute-start(bf16[1,144,1152]{2,1,0:T(8,128)(2,1)} %refs_0_.1), channel_id=1, source_target_pairs={{0,16},{16,0},{1,17},{17,1},{2,18},{18,2},{3,19},{19,3},{4,20},{20... | collective-permute-start | bytes 995336 | tf_op jit(solution)/shard_map/ppermute | solution.py:449
  19.5 5.6 %collective-permute-start.3 = (bf16[1,144,1152]{2,1,0:T(8,128)(2,1)}, bf16[1,144,1152]{2,1,0:T(8,128)(2,1)S(1)}, u32[]{:S(2)}, u32[]{:S(2)}) collective-permute-start(bf16[1,144,1152]{2,1,0:T(8,128)(2,1)} %refs_2_.1), channel_id=1, source_target_pairs={{0,16},{16,0},{1,17},{17,1},{2,18},{18,2},{3,19},{19,3},{4,20},{20... | collective-permute-start | bytes 995336 | tf_op jit(solution)/shard_map/ppermute | solution.py:449
  21.9 3.5 %collective-permute-start.2 = (bf16[1,144,1152]{2,1,0:T(8,128)(2,1)S(1)}, bf16[1,144,1152]{2,1,0:T(8,128)(2,1)S(1)}, u32[]{:S(2)}, u32[]{:S(2)}) collective-permute-start(bf16[1,144,1152]{2,1,0:T(8,128)(2,1)S(1)} %copy-done.13), channel_id=1, source_target_pairs={{0,16},{16,0},{1,17},{17,1},{2,18},{18,2},{3,19},{19,3},{4,20},{20... | collective-permute-start | bytes 995336 | tf_op jit(solution)/shard_map/ppermute | solution.py:449
  25.1 9.8 %copy-start = (bf16[1,144,1152]{2,1,0:T(8,128)(2,1)}, bf16[1,144,1152]{2,1,0:T(8,128)(2,1)S(1)}, u32[]{:S(2)}) copy-start(bf16[1,144,1152]{2,1,0:T(8,128)(2,1)S(1)} %collective-permute-done.1.w_1.refs_3_) | copy-start | bytes 995332
  25.1 9.8 %copy-start.1 = (bf16[1,144,1152]{2,1,0:T(8,128)(2,1)}, bf16[1,144,1152]{2,1,0:T(8,128)(2,1)S(1)}, u32[]{:S(2)}) copy-start(bf16[1,144,1152]{2,1,0:T(8,128)(2,1)S(1)} %collective-permute-done.3.w_3.refs_5_) | copy-start | bytes 995332
  25.5 9.5 %copy-start.2 = (bf16[1,144,1152]{2,1,0:T(8,128)(2,1)}, bf16[1,144,1152]{2,1,0:T(8,128)(2,1)S(1)}, u32[]{:S(2)}) copy-start(bf16[1,144,1152]{2,1,0:T(8,128)(2,1)S(1)} %collective-permute-done.2.w_2.refs_4_) | copy-start | bytes 995332
  34.9 25.1 %copy-start.7 = (f32[1,1152]{1,0:T(1,128)S(1)}, f32[1,1152]{1,0:T(1,128)}, u32[]{:S(2)}) copy-start(f32[1,1152]{1,0:T(1,128)} %scale_ref.3) | copy-start | bytes 13828
  35.0 25.1 %all-to-all-start.1 = ((bf16[16,184,128]{2,1,0:T(8,128)(2,1)}), bf16[16,184,128]{2,1,0:T(8,128)(2,1)S(1)}, u32[]{:S(2)}, u32[]{:S(2)}) async-start(bf16[16,184,128]{2,1,0:T(8,128)(2,1)} %get-tuple-element.47), calls=%async_computation.1 | async-start | bytes 1507328 | tf_op jit(solution)/shard_map/all_to_all | solution.py:416
  41.0 14.9 %collective-permute-start.4 = (bf16[224,1152]{1,0:T(8,128)(2,1)S(1)}, bf16[224,1152]{1,0:T(8,128)(2,1)S(1)}, u32[]{:S(2)}, u32[]{:S(2)}) collective-permute-start(bf16[224,1152]{1,0:T(8,128)(2,1)S(1)} %pad_maximum_fusion), channel_id=1, source_target_pairs={{0,64},{64,0},{1,65},{65,1},{2,66},{66,2},{3,67},{67,3},{4,68},{68... | collective-permute-start | bytes 1548296 | tf_op jit(solution)/shard_map/ppermute | solution.py:449
  43.4 40.3 %collective-permute-start.5 = (bf16[208,1152]{1,0:T(8,128)(2,1)S(1)}, bf16[208,1152]{1,0:T(8,128)(2,1)}, u32[]{:S(2)}, u32[]{:S(2)}) collective-permute-start(bf16[208,1152]{1,0:T(8,128)(2,1)S(1)} %collective-permute-done.w_0.refs_6_), channel_id=1, source_target_pairs={{0,16},{16,0},{1,17},{17,1},{2,18},{18,2},{3,19},{19,3},{4,20},{20... | collective-permute-start | bytes 1437704 | tf_op jit(solution)/shard_map/ppermute | solution.py:449
  55.9 27.7 %collective-permute-start.6 = (bf16[224,1152]{1,0:T(8,128)(2,1)S(1)}, bf16[224,1152]{1,0:T(8,128)(2,1)S(1)}, u32[]{:S(2)}, u32[]{:S(2)}) collective-permute-start(bf16[224,1152]{1,0:T(8,128)(2,1)S(1)} %collective-permute-done.4.w_0.refs_7_), channel_id=1, source_target_pairs={{0,16},{16,0},{1,17},{17,1},{2,18},{18,2},{3,19},{19,3},{4,20},{20... | collective-permute-start | bytes 1548296 | tf_op jit(solution)/shard_map/ppermute | solution.py:449
  60.0 0.7 copy-start.8
  61.8 23.2 %all-to-all-start.2 = ((bf16[8,16,2432]{2,1,0:T(8,128)(2,1)}), bf16[8,16,2432]{2,1,0:T(8,128)(2,1)S(1)}, u32[]{:S(2)}, u32[]{:S(2)}) async-start(bf16[8,16,2432]{2,1,0:T(8,128)(2,1)} %get-tuple-element.48), calls=%async_computation.2 | async-start | bytes 1245184 | tf_op jit(solution)/shard_map/all_to_all | solution.py:416
  91.1 18.7 %all-to-all-start.3 = ((bf16[8,16,1280]{2,1,0:T(8,128)(2,1)}), bf16[8,16,1280]{2,1,0:T(8,128)(2,1)S(1)}, u32[]{:S(2)}, u32[]{:S(2)}) async-start(bf16[8,16,1280]{2,1,0:T(8,128)(2,1)} %get-tuple-element.51.refs_1_), calls=%async_computation.3 | async-start | bytes 655360 | tf_op jit(solution)/shard_map/all_to_all | solution.py:416
  112.2 22.3 %all-to-all-start.4 = ((bf16[16,104,128]{2,1,0:T(8,128)(2,1)}), bf16[16,104,128]{2,1,0:T(8,128)(2,1)S(1)}, u32[]{:S(2)}, u32[]{:S(2)}) async-start(bf16[16,104,128]{2,1,0:T(8,128)(2,1)} %get-tuple-element.63), calls=%async_computation.4 | async-start | bytes 851968 | tf_op jit(solution)/shard_map/all_to_all | solution.py:416
  118.3 6.3 %collective-permute-start.7 = (bf16[144,1152]{1,0:T(8,128)(2,1)}, bf16[144,1152]{1,0:T(8,128)(2,1)S(1)}, u32[]{:S(2)}, u32[]{:S(2)}) collective-permute-start(bf16[144,1152]{1,0:T(8,128)(2,1)} %get-tuple-element.67), channel_id=1, source_target_pairs={{0,16},{16,0},{1,17},{17,1},{2,18},{18,2},{3,19},{19,3},{4,20},{20... | collective-permute-start | bytes 995336 | tf_op jit(solution)/shard_map/ppermute | solution.py:449
  120.2 4.4 %collective-permute-start.8 = (bf16[144,1152]{1,0:T(8,128)(2,1)}, bf16[144,1152]{1,0:T(8,128)(2,1)S(1)}, u32[]{:S(2)}, u32[]{:S(2)}) collective-permute-start(bf16[144,1152]{1,0:T(8,128)(2,1)} %get-tuple-element.68), channel_id=1, source_target_pairs={{0,16},{16,0},{1,17},{17,1},{2,18},{18,2},{3,19},{19,3},{4,20},{20... | collective-permute-start | bytes 995336 | tf_op jit(solution)/shard_map/ppermute | solution.py:449
  122.7 3.7 %collective-permute-start.9 = (bf16[144,1152]{1,0:T(8,128)(2,1)}, bf16[144,1152]{1,0:T(8,128)(2,1)S(1)}, u32[]{:S(2)}, u32[]{:S(2)}) collective-permute-start(bf16[144,1152]{1,0:T(8,128)(2,1)} %get-tuple-element.69), channel_id=1, source_target_pairs={{0,16},{16,0},{1,17},{17,1},{2,18},{18,2},{3,19},{19,3},{4,20},{20... | collective-permute-start | bytes 995336 | tf_op jit(solution)/shard_map/ppermute | solution.py:449
  128.8 28.3 %collective-permute-start.11 = (bf16[3,144,1152]{2,1,0:T(8,128)(2,1)}, bf16[3,144,1152]{2,1,0:T(8,128)(2,1)}, u32[]{:S(2)}, u32[]{:S(2)}) collective-permute-start(bf16[3,144,1152]{2,1,0:T(8,128)(2,1)} %shard_map.213.near), channel_id=1, source_target_pairs={{0,64},{64,0},{1,65},{65,1},{2,66},{66,2},{3,67},{67,3},{4,68},{68... | collective-permute-start | bytes 2985992 | tf_op jit(solution)/shard_map/ppermute | solution.py:449
  134.5 14.2 %copy-start.4 = (bf16[1,128,1152]{2,1,0:T(8,128)(2,1)S(1)}, bf16[1,128,1152]{2,1,0:T(8,128)(2,1)}, u32[]{:S(2)}) copy-start(bf16[1,128,1152]{2,1,0:T(8,128)(2,1)} %g_ref.3) | copy-start | bytes 884740
  138.5 18.6 %copy-start.12 = (bf16[2,3,144,1152]{3,2,1,0:T(8,128)(2,1)S(1)}, bf16[2,3,144,1152]{3,2,1,0:T(8,128)(2,1)}, u32[]{:S(2)}) copy-start(bf16[2,3,144,1152]{3,2,1,0:T(8,128)(2,1)} %get-tuple-element.66.own_ref) | copy-start | bytes 5971972
  138.5 18.6 %collective-permute-start.10 = (bf16[3,144,1152]{2,1,0:T(8,128)(2,1)}, bf16[3,144,1152]{2,1,0:T(8,128)(2,1)}, u32[]{:S(2)}, u32[]{:S(2)}) collective-permute-start(bf16[3,144,1152]{2,1,0:T(8,128)(2,1)} %get-tuple-element.80), channel_id=1, source_target_pairs={{0,16},{16,0},{1,17},{17,1},{2,18},{18,2},{3,19},{19,3},{4,20},{20... | collective-permute-start | bytes 2985992 | tf_op jit(solution)/shard_map/ppermute | solution.py:449
  140.6 27.7 %all-to-all-start.5 = ((bf16[16,160,128]{2,1,0:T(8,128)(2,1)}), bf16[16,160,128]{2,1,0:T(8,128)(2,1)S(1)}, u32[]{:S(2)}, u32[]{:S(2)}) async-start(bf16[16,160,128]{2,1,0:T(8,128)(2,1)} %get-tuple-element.71), calls=%async_computation.5 | async-start | bytes 1310720 | tf_op jit(solution)/shard_map/all_to_all | solution.py:416
